TPU v7x, 32 devices: a whole 2x2x4 slice. The times are simulated.
32 devices in a mesh: group: 2 (over x), node: 2 (over core), local: 8 (over z, y).
Axes of the slice: x: 2, y: 2, z: 4, core: 2. Of those that a mesh axis runs over, the one named last changes fastest.
Arguments:
- query_rows: bfloat16 [6144, 2048], P(('group', 'node', 'local')), parts along dimension 0, may hold values from -6 to 6
- key_rows: bfloat16 [6144, 2048], P(('group', 'node', 'local')), parts along dimension 0, may hold values from -6 to 6
- value_rows: bfloat16 [6144, 2048], P(('group', 'node', 'local')), parts along dimension 0, may hold values from -6 to 6
- out_grad: bfloat16 [6144, 2048], P(('group', 'node', 'local')), parts along dimension 0, may hold values from -6 to 6
Outputs:
- attended: bfloat16 [6144, 2048], P(('group', 'node', 'local')), parts along dimension 0
- query_grad: bfloat16 [6144, 2048], P(('group', 'node', 'local')), parts along dimension 0
- key_grad: bfloat16 [6144, 2048], P(('group', 'node', 'local')), parts along dimension 0
- value_grad: bfloat16 [6144, 2048], P(('group', 'node', 'local')), parts along dimension 0
There are 2 independent parts, one for each index of `group`. A program takes and returns all parts, laid end to end along the dimension named above; each array names one. Nothing has to cross between parts.
All inputs are finite; a program needn't handle non-finite values.
Results may differ from a plain program's by a relative error of at most 0.0051.
Values sent between devices are 32-bit elements; how exact they have to be, the bound alone decides.
No kernel may reach another device: no remote copies, remote signals or barrier semaphores. Data moves between devices by JAX's collectives and lax.ppermute only.
A program may use at most 320 MiB of HBM per device.

v0:
```python
import math

import jax
import jax.numpy as jnp
from jax import lax
from jax.sharding import PartitionSpec as P

HEADS = 16
HEAD_DIM = 128


def prefix_2(shard, axis, combine, identity, reverse):
    count, mine = (lax.axis_size(axis), lax.axis_index(axis))
    everything = lax.all_gather(shard, axis)
    start = jnp.broadcast_to(jnp.asarray(identity, shard.dtype), shard.shape)

    def turn(k, before):
        at = count - 1 - k if reverse else k
        reached = at > mine if reverse else at < mine
        new = combine(before, everything[at])
        return jnp.where(reached, new, before)

    return lax.fori_loop(0, count, turn, start)


def add_tree(earlier, later):
    return jax.tree.map(jnp.add, earlier, later)


def chain_sum(pieces, reverse):
    blanks = jax.tree.map(jnp.zeros_like, pieces)
    return prefix_2(pieces, ("node", "local"), add_tree, blanks, reverse)


def head_major(array, rows):
    return jnp.transpose(array.reshape(rows, HEADS, HEAD_DIM), (1, 0, 2))


def local(query_rows, key_rows, value_rows, out_grad):
    rows = query_rows.shape[0]
    queries = head_major(query_rows, rows)
    keyset = head_major(key_rows, rows)
    valueset = head_major(value_rows, rows)
    gradset = head_major(out_grad, rows)
    key_state = jnp.einsum("htd,hte->hde", keyset, valueset, preferred_element_type=jnp.float32)
    grad_state = jnp.einsum("htd,hte->hde", queries, gradset, preferred_element_type=jnp.float32)
    prefix = chain_sum(key_state, False)
    suffix = chain_sum(grad_state, True)
    factor = 1.0 / math.sqrt(HEAD_DIM * rows * lax.axis_size("node") * lax.axis_size("local"))
    causal = jnp.tril(jnp.ones((rows, rows), dtype=bool))
    prefix_low = prefix.astype(jnp.bfloat16)
    suffix_low = suffix.astype(jnp.bfloat16)
    scores = jnp.einsum("htd,hsd->hts", queries, keyset, preferred_element_type=jnp.float32)
    weights = jnp.where(causal[None], scores, 0.0).astype(jnp.bfloat16)
    grad_scores = jnp.einsum("hte,hse->hts", gradset, valueset, preferred_element_type=jnp.float32)
    grad_weights = jnp.where(causal[None], grad_scores, 0.0).astype(jnp.bfloat16)
    attended = jnp.einsum("hts,hse->hte", weights, valueset, preferred_element_type=jnp.float32)
    attended = attended + jnp.einsum(
        "htd,hde->hte", queries, prefix_low, preferred_element_type=jnp.float32
    )
    query_grad = jnp.einsum(
        "hts,hsd->htd", grad_weights, keyset, preferred_element_type=jnp.float32
    )
    query_grad = query_grad + jnp.einsum(
        "hte,hde->htd", gradset, prefix_low, preferred_element_type=jnp.float32
    )
    key_grad = jnp.einsum("hts,htd->hsd", grad_weights, queries, preferred_element_type=jnp.float32)
    key_grad = key_grad + jnp.einsum(
        "hse,hde->hsd", valueset, suffix_low, preferred_element_type=jnp.float32
    )
    value_grad = jnp.einsum("hts,hte->hse", weights, gradset, preferred_element_type=jnp.float32)
    value_grad = value_grad + jnp.einsum(
        "hsd,hde->hse", keyset, suffix_low, preferred_element_type=jnp.float32
    )
    return tuple(
        (
            jnp.transpose((factor * item).astype(jnp.bfloat16), (1, 0, 2)).reshape(
                rows, HEADS * HEAD_DIM
            )
            for item in (attended, query_grad, key_grad, value_grad)
        )
    )


def solution(mesh):
    return jax.shard_map(
        local,
        mesh=mesh,
        in_specs=(
            P(("group", "node", "local"), None),
            P(("group", "node", "local"), None),
            P(("group", "node", "local"), None),
            P(("group", "node", "local"), None),
        ),
        out_specs=(
            P(("group", "node", "local"), None),
            P(("group", "node", "local"), None),
            P(("group", "node", "local"), None),
            P(("group", "node", "local"), None),
        ),
        check_vma=False,
    )
```

profile of v0, /device:TPU:0, one launch (start us, length us, event | category | flops | bytes accessed | tf_op | source)
XLA Modules:
  0.0 306.3 jit_solution(387233581689154259)
XLA Ops:
  7.2 0.0 copy-start
  7.2 0.0 copy-start.1
  7.2 0.0 all-gather.7.cloned.1.call-start
  7.2 3.0 fusion.13
  10.3 0.0 all-gather.7.cloned.1.call-update
  10.3 0.0 all-gather.5.cloned.1.call-start
  10.3 1.5 fusion.14
  11.8 0.0 all-gather.5.cloned.1.call-update
  11.9 0.0 copy-start.2
  11.9 1.8 select_convert_fusion
  13.8 0.0 copy-start.6
  13.8 0.6 select_convert_fusion.1
  14.4 0.5 copy-done.6
  14.9 2.0 fusion.12
  16.9 1.7 fusion.15
  18.6 1.9 fusion.17
  20.5 1.7 fusion.16
  22.2 117.8 %all-gather.7.cloned.1.call-done = f32[256,128,128]{2,1,0:T(8,128)} async-done(((f32[16,128,128]{2,1,0:T(8,128)}), f32[256,128,128]{2,1,0:T(8,128)}) %all-gather.7.cloned.1.call-update) | async-done | bytes 16777232 | tf_op jit(solution)/shard_map/all_gather | solution.py:14
  140.0 26.3 %while.31 = (s32[]{:T(128)}, f32[16,128,128]{2,1,0:T(8,128)S(1)}, s32[]{:T(128)}, f32[16,16,128,128]{3,2,1,0:T(8,128)}, s32[]{:T(128)}, /*index=5*/s32[]{:T(128)}, s32[]{:T(128)}, s32[]{:T(128)}) while((s32[]{:T(128)}, f32[16,128,128]{2,1,0:T(8,128)S(1)}, s32[]{:T(128)}, f32[16,16,128,128]{3,2,1,0:T(8,128)}, s32[]{:T(128)}, ...), condition=%wide.region_3.4_spmd.clone, body=%wide.region_2.3_spmd.clone.sunk | while | flops 786440 | bytes 3145883 | solution.py:23
  140.0 1.6 add_select_fusion.5
  141.6 1.6 add_select_fusion.5
  143.3 1.6 add_select_fusion.5
  144.9 1.6 add_select_fusion.5
  146.5 1.7 add_select_fusion.5
  148.2 1.7 add_select_fusion.5
  150.0 1.7 add_select_fusion.5
  151.7 1.6 add_select_fusion.5
  153.4 1.6 add_select_fusion.5
  155.0 1.6 add_select_fusion.5
  156.6 1.6 add_select_fusion.5
  158.2 1.6 add_select_fusion.5
  159.9 1.6 add_select_fusion.5
  161.5 1.6 add_select_fusion.5
  163.1 1.6 add_select_fusion.5
  164.7 1.6 add_select_fusion.5
  166.3 0.0 copy-start.3
  166.4 2.9 fusion.10
  169.3 1.3 fusion.11
  170.6 96.7 %all-gather.5.cloned.1.call-done = f32[256,128,128]{2,1,0:T(8,128)} async-done(((f32[16,128,128]{2,1,0:T(8,128)}), f32[256,128,128]{2,1,0:T(8,128)}) %all-gather.5.cloned.1.call-update) | async-done | bytes 16777232 | tf_op jit(solution)/shard_map/all_gather | solution.py:14
  267.3 25.9 %while.30 = (s32[]{:T(128)}, f32[16,128,128]{2,1,0:T(8,128)S(1)}, s32[]{:T(128)}, f32[16,16,128,128]{3,2,1,0:T(8,128)}, s32[]{:T(128)}, /*index=5*/s32[]{:T(128)}) while((s32[]{:T(128)}, f32[16,128,128]{2,1,0:T(8,128)S(1)}, s32[]{:T(128)}, f32[16,16,128,128]{3,2,1,0:T(8,128)}, s32[]{:T(128)}, /*index=5*/s32[]{:T(128)}) %tuple.83), condition=%wide.region_1.2_spmd.clone, body=%wide.region_0.1_spmd.clone.sunk | while | flops 786436 | bytes 3145821 | solution.py:23
  267.3 1.7 add_select_fusion.4
  269.0 1.6 add_select_fusion.4
  270.6 1.6 add_select_fusion.4
  272.2 1.6 add_select_fusion.4
  273.9 1.6 add_select_fusion.4
  275.5 1.6 add_select_fusion.4
  277.1 1.6 add_select_fusion.4
  278.7 1.6 add_select_fusion.4
  280.3 1.6 add_select_fusion.4
  281.9 1.6 add_select_fusion.4
  283.5 1.6 add_select_fusion.4
  285.1 1.6 add_select_fusion.4
  286.8 1.6 add_select_fusion.4
  288.4 1.6 add_select_fusion.4
  290.0 1.6 add_select_fusion.4
  291.6 1.6 add_select_fusion.4
  293.2 0.0 copy-start.7
  293.2 1.9 fusion.8
  295.2 0.2 copy-done.8
  295.3 0.5 fusion.9
  295.8 0.6 copy-done.10
  296.5 0.2 copy-done.11
  296.7 1.4 copy_bitcast_fusion
  298.1 1.4 copy_bitcast_fusion.2
  (17 shorter events, 0.1 us)
Async XLA Ops:
  7.2 3.2 %copy-start = (bf16[192,2048]{1,0:T(8,128)(2,1)S(1)}, bf16[192,2048]{1,0:T(8,128)(2,1)}, u32[]{:S(2)}) copy-start(bf16[192,2048]{1,0:T(8,128)(2,1)} %param.10) | copy-start | bytes 2359300
  7.2 3.2 %copy-start.1 = (bf16[192,2048]{1,0:T(8,128)(2,1)S(1)}, bf16[192,2048]{1,0:T(8,128)(2,1)}, u32[]{:S(2)}) copy-start(bf16[192,2048]{1,0:T(8,128)(2,1)} %param.9) | copy-start | bytes 2359300
  7.2 132.8 %all-gather.7.cloned.1.call-start = ((), (), s32[]{:S(2)}) async-start(), calls=%async_computation.1 | async-start | bytes 17825792 | tf_op jit(solution)/shard_map/all_gather | solution.py:14
  10.3 257.0 %all-gather.5.cloned.1.call-start = ((), (), s32[]{:S(2)}) async-start(), calls=%async_computation | async-start | bytes 17825792 | tf_op jit(solution)/shard_map/all_gather | solution.py:14
  11.9 1.9 copy-start.2
  11.9 1.9 copy-start.4
  13.8 1.1 copy-start.6
  166.3 2.9 copy-start.3
  166.4 2.9 copy-start.9
  267.3 25.9 %copy-start.5 = (bf16[192,2048]{1,0:T(8,128)(2,1)S(1)}, bf16[192,2048]{1,0:T(8,128)(2,1)}, u32[]{:S(2)}) copy-start(bf16[192,2048]{1,0:T(8,128)(2,1)} %param.8) | copy-start | bytes 2359300
  293.2 2.0 copy-start.7
  293.2 2.1 copy-start.8
  295.3 1.1 copy-start.10
  295.3 1.4 copy-start.11
Sparse Core Ops, SparseCore 0:
  10.4 129.5 all-gather.6
  142.2 125.0 all-gather.4
where the time goes:
time: 308 us; the launch traced here: 306 us
  waiting for transfers between devices  215 us (70%)
  other arithmetic  51.4 us (17%)
  matrix products  20.9 us (7%)
  between operations  14.2 us (5%)
  local copies, waits for them, and re-layouts  4.36 us (1%)
    all_gather x2, waiting for transfers between devices, prefix_2(): everything = lax.all_gather(shard, axis)  215 us
    select_n x32, other arithmetic, turn(): return jnp.where(reached, new, before)  51.3 us
  transfers between devices with their start and end apart: 2, of which 2 were waited for; matrix products, arithmetic and copies ran while one was open for 13% of the time, Pallas kernels for 0%

commit v1 on v0

v1 whole, which is shorter than its diff:
```python
import functools
import math

import jax
import jax.numpy as jnp
from jax import lax
from jax.experimental import pallas as pl
from jax.experimental.pallas import tpu as pltpu
from jax.sharding import PartitionSpec as P

HEAD_DIM = 128
PARTS = 4
QUARTER = HEAD_DIM // PARTS
CHUNKS = (8, 8)
STEP = 4

F32 = jnp.float32
BF16 = jnp.bfloat16
VMEM_LIMIT = 40 * 1024 * 1024


def dot(a, b, ca, cb):
    return lax.dot_general(a, b, (((ca,), (cb,)), ((), ())), preferred_element_type=F32)


def place(info, r):
    return pl.multiple_of((info[0] ^ r) * QUARTER, QUARTER)


def state_kernel(step, info, q, k, v, g, *refs):
    outs, hold = refs[:PARTS], refs[PARTS]
    for h in range(step):
        cols = slice(h * HEAD_DIM, (h + 1) * HEAD_DIM)
        hold[0] = dot(k[:, cols], v[:, cols], 0, 0)
        hold[1] = dot(q[:, cols], g[:, cols], 0, 0)
        for r in range(PARTS):
            rows = pl.ds(place(info, r), QUARTER)
            outs[r][0, h] = hold[0, rows, :]
            outs[r][1, h] = hold[1, rows, :]


def states(info, arrays, first, heads, step):
    rows = arrays[0].shape[0]
    piece = jax.ShapeDtypeStruct((2, heads, QUARTER, HEAD_DIM), F32)
    return pl.pallas_call(
        functools.partial(state_kernel, step),
        out_shape=[piece] * PARTS,
        grid_spec=pltpu.PrefetchScalarGridSpec(
            num_scalar_prefetch=1,
            grid=(heads // step,),
            in_specs=[
                pl.BlockSpec((rows, step * HEAD_DIM), lambda i, info: (0, first // step + i))
            ]
            * 4,
            out_specs=[
                pl.BlockSpec((2, step, QUARTER, HEAD_DIM), lambda i, info: (0, i, 0, 0))
            ]
            * PARTS,
            scratch_shapes=[pltpu.VMEM((2, HEAD_DIM, HEAD_DIM), F32)],
        ),
        compiler_params=pltpu.CompilerParams(vmem_limit_bytes=VMEM_LIMIT),
        cost_estimate=pl.CostEstimate(
            flops=4 * heads * rows * HEAD_DIM * HEAD_DIM,
            bytes_accessed=heads * (8 * rows * HEAD_DIM + 8 * HEAD_DIM * HEAD_DIM),
            transcendentals=0,
        ),
    )(info, *arrays)


def spread_kernel(levels, info, *refs):
    pieces = refs[:PARTS]
    totals = refs[PARTS : PARTS + levels]
    across = refs[PARTS + levels]
    outs = refs[PARTS + levels + 1 :]
    mine, node, block = info[0], info[1], info[2]
    prefix = jnp.where(node > 0, across[...], 0.0)
    suffix = jnp.where(node > 0, 0.0, across[...])
    for level in range(levels):
        upper = ((block >> level) & 1) > 0
        prefix = prefix + jnp.where(upper, totals[level][0], 0.0)
        suffix = suffix + jnp.where(upper, 0.0, totals[level][1])
    for r in range(PARTS):
        before, after = prefix, suffix
        for other in range(PARTS):
            if other != r:
                earlier = (mine ^ other) < (mine ^ r)
                before = before + jnp.where(earlier, pieces[other][0], 0.0)
                after = after + jnp.where(earlier, 0.0, pieces[other][1])
        outs[r][0] = before
        outs[r][1] = after


def spread(info, pieces, totals, across):
    levels = len(totals)
    whole = pl.BlockSpec(memory_space=pltpu.VMEM)
    size = pieces[0].size * 4
    return pl.pallas_call(
        functools.partial(spread_kernel, levels),
        out_shape=[jax.ShapeDtypeStruct(pieces[0].shape, F32)] * PARTS,
        in_specs=[pl.BlockSpec(memory_space=pltpu.SMEM)] + [whole] * (PARTS + levels + 1),
        out_specs=[whole] * PARTS,
        compiler_params=pltpu.CompilerParams(vmem_limit_bytes=VMEM_LIMIT),
        cost_estimate=pl.CostEstimate(
            flops=pieces[0].size * 30,
            bytes_accessed=size * (2 * PARTS + levels + 1),
            transcendentals=0,
        ),
    )(info, *pieces, *totals, across)


def finish_kernel(step, factor, info, q, k, v, g, *refs):
    pieces, (att, qg, kg, vg), hold = refs[:PARTS], refs[-5:-1], refs[-1]
    rows = q.shape[0]
    causal = lax.broadcasted_iota(jnp.int32, (rows, rows), 0) >= lax.broadcasted_iota(
        jnp.int32, (rows, rows), 1
    )
    for h in range(step):
        cols = slice(h * HEAD_DIM, (h + 1) * HEAD_DIM)
        for r in range(PARTS):
            at = pl.ds(place(info, r), QUARTER)
            hold[0, at, :] = pieces[r][0, h].astype(BF16)
            hold[1, at, :] = pieces[r][1, h].astype(BF16)
        qh, kh, vh, gh = q[:, cols], k[:, cols], v[:, cols], g[:, cols]
        prefix, suffix = hold[0], hold[1]
        weights = jnp.where(causal, dot(qh, kh, 1, 1), 0.0).astype(BF16)
        grad_weights = jnp.where(causal, dot(gh, vh, 1, 1), 0.0).astype(BF16)
        att[:, cols] = (factor * (dot(weights, vh, 1, 0) + dot(qh, prefix, 1, 0))).astype(BF16)
        qg[:, cols] = (factor * (dot(grad_weights, kh, 1, 0) + dot(gh, prefix, 1, 1))).astype(BF16)
        kg[:, cols] = (factor * (dot(grad_weights, qh, 0, 0) + dot(vh, suffix, 1, 1))).astype(BF16)
        vg[:, cols] = (factor * (dot(weights, gh, 0, 0) + dot(kh, suffix, 1, 0))).astype(BF16)


def finish(info, arrays, pieces, outs, first, step, factor):
    rows, width = arrays[0].shape
    heads = pieces[0].shape[1]
    columns = pl.BlockSpec((rows, step * HEAD_DIM), lambda i, info: (0, first // step + i))
    quarter = pl.BlockSpec((2, step, QUARTER, HEAD_DIM), lambda i, info: (0, i, 0, 0))
    given = [info, *arrays, *pieces, *outs]
    fixed = 5 + PARTS
    return pl.pallas_call(
        functools.partial(finish_kernel, step, factor),
        out_shape=[jax.ShapeDtypeStruct((rows, width), BF16)] * 4,
        grid_spec=pltpu.PrefetchScalarGridSpec(
            num_scalar_prefetch=1,
            grid=(heads // step,),
            in_specs=[columns] * 4
            + [quarter] * PARTS
            + [pl.BlockSpec(memory_space=pl.ANY)] * len(outs),
            out_specs=[columns] * 4,
            scratch_shapes=[pltpu.VMEM((2, HEAD_DIM, HEAD_DIM), BF16)],
        ),
        input_output_aliases={fixed + i: i for i in range(len(outs))},
        compiler_params=pltpu.CompilerParams(vmem_limit_bytes=VMEM_LIMIT),
        cost_estimate=pl.CostEstimate(
            flops=heads * rows * HEAD_DIM * (12 * rows + 8 * HEAD_DIM),
            bytes_accessed=heads * HEAD_DIM * (16 * rows + 8 * HEAD_DIM),
            transcendentals=0,
        ),
    )(*given)


def swap(array, size, mask):
    return lax.ppermute(array, "local", [(i, i ^ mask) for i in range(size)])


def local(query_rows, key_rows, value_rows, out_grad):
    arrays = (query_rows, key_rows, value_rows, out_grad)
    rows, width = query_rows.shape
    heads = width // HEAD_DIM
    size, nodes = lax.axis_size("local"), lax.axis_size("node")
    blocks = size // PARTS
    levels = blocks.bit_length() - 1
    assert nodes == 2 and PARTS << levels == size and sum(CHUNKS) == heads
    factor = 1.0 / math.sqrt(HEAD_DIM * rows * nodes * size)
    node, place_in = lax.axis_index("node"), lax.axis_index("local")
    info = jnp.stack([place_in % PARTS, node, place_in // PARTS]).astype(jnp.int32)

    firsts = [sum(CHUNKS[:i]) for i in range(len(CHUNKS))]
    outs = ()
    gathered = []
    for first, count in zip(firsts, CHUNKS):
        own = states(info, arrays, first, count, STEP)
        gathered.append([own[0]] + [swap(own[r], size, r) for r in (1, 3, 2)])
    returned = []
    for got in gathered:
        pieces = [got[0], got[1], got[3], got[2]]
        total = (pieces[0] + pieces[1]) + (pieces[2] + pieces[3])
        totals = []
        for level in range(levels):
            totals.append(swap(total, size, PARTS << level))
            total = total + totals[-1]
        across = lax.ppermute(
            jnp.where(node > 0, total[1], total[0]), "node", [(0, 1), (1, 0)]
        )
        ready = spread(info, pieces, totals, across)
        back = [swap(ready[r], size, r) for r in (1, 3, 2)]
        returned.append([ready[0], back[0], back[2], back[1]])
    for first, pieces in zip(firsts, returned):
        outs = finish(info, arrays, pieces, outs, first, STEP, factor)
    return tuple(outs)


def solution(mesh):
    rows = P(("group", "node", "local"), None)
    return jax.shard_map(
        local, mesh=mesh, in_specs=(rows,) * 4, out_specs=(rows,) * 4, check_vma=False
    )
```

time: 308 us -> 86.6 us (0.28)
  waiting for transfers between devices: 215 us -> 44.3 us
  other arithmetic: 51.4 us -> 0.36 us
  starting transfers between devices: 0.08 us -> 22.8 us
  matrix products: 20.9 us -> 0 us
  Pallas kernels: 0 us -> 13.5 us
  between operations: 14.2 us -> 0.78 us
    all_gather x2 -> x0, waiting for transfers between devices: 215 us -> none  [prefix_2(): everything = lax.all_gather(shard, axis)]
    select_n x32 -> x2, other arithmetic: 51.3 us -> 0.04 us  [local(): jnp.where(node > 0, total[1], total[0])]
    ppermute x0 -> x16, waiting for transfers between devices: none -> 44.3 us  [the longest x14 44.3 us: swap(): return lax.ppermute(array, 'local', [(i, i ^ mask) for i in range(size)])]
    ppermute x0 -> x16, starting transfers between devices: none -> 22.8 us  [the longest x14 22.7 us: swap(): return lax.ppermute(array, 'local', [(i, i ^ mask) for i in range(size)])]
    dot_general x12 -> x0, matrix products: 20.9 us -> none  [the longest x1 3.01 us: local(): jnp.einsum('htd,hte->hde', queries, gradset, preferred_element_type=jnp.f...]
    pallas_call x0 -> x6, Pallas kernels: none -> 13.5 us  [the longest x2 8.74 us: finish(): pl.pallas_call(functools.partial(finish_kernel, step, factor), out_shape=...]
  transfers between devices with their start and end apart: 2 -> 16, of which waited for: 2 -> 10; matrix products, arithmetic and copies ran while one was open for 13% -> 0% of each run, Pallas kernels for 0% -> 8%
where the time goes in v1:
time: 86.6 us; the launch traced here: 86.3 us
  waiting for transfers between devices  44.3 us (51%)
  starting transfers between devices  22.8 us (26%)
  Pallas kernels  13.5 us (16%)
  local copies, waits for them, and re-layouts  4.56 us (5%)
    ppermute x14, waiting for transfers between devices, swap(): return lax.ppermute(array, 'local', [(i, i ^ mask) for i in range(size)])  44.3 us
    ppermute x14, starting transfers between devices, swap(): return lax.ppermute(array, 'local', [(i, i ^ mask) for i in range(size)])  22.7 us
    pallas_call x2, Pallas kernels, finish(): pl.pallas_call(functools.partial(finish_kernel, step, factor), out_shape=...  8.74 us
    unnamed x16, local copies, waits for them, and re-layouts  4.56 us
    pallas_call x2, Pallas kernels, states(): pl.pallas_call(functools.partial(state_kernel, step), out_shape=[piece] *...  2.98 us
    pallas_call x2, Pallas kernels, spread(): pl.pallas_call(functools.partial(spread_kernel, levels), out_shape=[jax.S...  1.75 us
  transfers between devices with their start and end apart: 16, of which 10 were waited for; matrix products, arithmetic and copies ran while one was open for 0% of the time, Pallas kernels for 8%

profile of v1, /device:TPU:0, one launch (start us, length us, event | category | flops | bytes accessed | tf_op | source)
XLA Modules:
  0.0 86.3 jit_solution(10592025036165063493)
XLA Ops:
  0.7 0.1 pad_add_fusion.info
  0.7 0.0 copy-start
  0.7 1.1 %copy-done = bf16[192,2048]{1,0:T(8,128)(2,1)S(1)} copy-done((bf16[192,2048]{1,0:T(8,128)(2,1)S(1)}, bf16[192,2048]{1,0:T(8,128)(2,1)}, u32[]{:S(2)}) %copy-start) | copy-done | bytes 786456
  1.9 0.0 copy-start.2
  1.9 1.1 %copy-done.2 = bf16[192,2048]{1,0:T(8,128)(2,1)S(1)} copy-done((bf16[192,2048]{1,0:T(8,128)(2,1)S(1)}, bf16[192,2048]{1,0:T(8,128)(2,1)}, u32[]{:S(2)}) %copy-start.2) | copy-done | bytes 786456
  3.0 0.0 copy-start.4
  3.0 1.1 %copy-done.4 = bf16[192,2048]{1,0:T(8,128)(2,1)S(1)} copy-done((bf16[192,2048]{1,0:T(8,128)(2,1)S(1)}, bf16[192,2048]{1,0:T(8,128)(2,1)}, u32[]{:S(2)}) %copy-start.4) | copy-done | bytes 786456
  4.1 0.0 copy-start.6
  4.1 1.1 %copy-done.6 = bf16[192,2048]{1,0:T(8,128)(2,1)S(1)} copy-done((bf16[192,2048]{1,0:T(8,128)(2,1)S(1)}, bf16[192,2048]{1,0:T(8,128)(2,1)}, u32[]{:S(2)}) %copy-start.6) | copy-done | bytes 786456
  5.3 1.5 %shard_map.77 = (f32[2,8,32,128]{3,2,1,0:T(8,128)S(1)}, f32[2,8,32,128]{3,2,1,0:T(8,128)S(1)}, f32[2,8,32,128]{3,2,1,0:T(8,128)S(1)}, f32[2,8,32,128]{3,2,1,0:T(8,128)S(1)}) custom-call(s32[3]{0:T(128)S(1)} %pad_add_fusion.info, bf16[192,2048]{1,0:T(8,128)(2,1)S(1)} %copy-done, bf16[192,2048]{1,0:T(8,128)(2,1)S(1)} %copy-done.2, ...), custom_call_target="tpu_custom_call" | custom-call | flops 100663296 | bytes 2621440 | tf_op jit(solution)/shard_map/pallas_call | solution.py:45
  6.8 3.0 %collective-permute-start.8 = (f32[2,8,32,128]{3,2,1,0:T(8,128)S(1)}, f32[2,8,32,128]{3,2,1,0:T(8,128)S(1)}, u32[]{:S(2)}, u32[]{:S(2)}) collective-permute-start(f32[2,8,32,128]{3,2,1,0:T(8,128)S(1)} %get-tuple-element.33), channel_id=1, source_target_pairs={{0,1},{1,0},{2,3},{3,2},{4,5},{5,4},{6,7},{7,6},{8,9},{9,8},{10,11... | collective-permute-start | bytes 786440 | tf_op jit(solution)/shard_map/ppermute | solution.py:163
  9.8 1.6 %collective-permute-start.9 = (f32[2,8,32,128]{3,2,1,0:T(8,128)S(1)}, f32[2,8,32,128]{3,2,1,0:T(8,128)S(1)}, u32[]{:S(2)}, u32[]{:S(2)}) collective-permute-start(f32[2,8,32,128]{3,2,1,0:T(8,128)S(1)} %get-tuple-element.34), channel_id=1, source_target_pairs={{0,2},{1,3},{2,0},{3,1},{4,6},{5,7},{6,4},{7,5},{8,10},{9,11},{10,... | collective-permute-start | bytes 786440 | tf_op jit(solution)/shard_map/ppermute | solution.py:163
  11.4 0.0 collective-permute-start.10
  11.4 1.5 %shard_map.75 = (f32[2,8,32,128]{3,2,1,0:T(8,128)S(1)}, f32[2,8,32,128]{3,2,1,0:T(8,128)S(1)}, f32[2,8,32,128]{3,2,1,0:T(8,128)S(1)}, f32[2,8,32,128]{3,2,1,0:T(8,128)S(1)}) custom-call(s32[3]{0:T(128)S(1)} %pad_add_fusion.info, bf16[192,2048]{1,0:T(8,128)(2,1)S(1)} %copy-done, bf16[192,2048]{1,0:T(8,128)(2,1)S(1)} %copy-done.2, ...), custom_call_target="tpu_custom_call" | custom-call | flops 100663296 | bytes 2621440 | tf_op jit(solution)/shard_map/pallas_call | solution.py:45
  12.9 2.0 %collective-permute-start = (f32[2,8,32,128]{3,2,1,0:T(8,128)S(1)}, f32[2,8,32,128]{3,2,1,0:T(8,128)S(1)}, u32[]{:S(2)}, u32[]{:S(2)}) collective-permute-start(f32[2,8,32,128]{3,2,1,0:T(8,128)S(1)} %get-tuple-element.25), channel_id=1, source_target_pairs={{0,1},{1,0},{2,3},{3,2},{4,5},{5,4},{6,7},{7,6},{8,9},{9,8},{10,11... | collective-permute-start | bytes 786440 | tf_op jit(solution)/shard_map/ppermute | solution.py:163
  14.9 1.6 %collective-permute-start.1 = (f32[2,8,32,128]{3,2,1,0:T(8,128)S(1)}, f32[2,8,32,128]{3,2,1,0:T(8,128)S(1)}, u32[]{:S(2)}, u32[]{:S(2)}) collective-permute-start(f32[2,8,32,128]{3,2,1,0:T(8,128)S(1)} %get-tuple-element.26), channel_id=1, source_target_pairs={{0,2},{1,3},{2,0},{3,1},{4,6},{5,7},{6,4},{7,5},{8,10},{9,11},{10,... | collective-permute-start | bytes 786440 | tf_op jit(solution)/shard_map/ppermute | solution.py:163
  16.4 1.2 %collective-permute-done.8.refs_1_ = f32[2,8,32,128]{3,2,1,0:T(8,128)S(1)} collective-permute-done((f32[2,8,32,128]{3,2,1,0:T(8,128)S(1)}, f32[2,8,32,128]{3,2,1,0:T(8,128)S(1)}, u32[]{:S(2)}, u32[]{:S(2)}) %collective-permute-start.8) | collective-permute-done | bytes 262176 | tf_op jit(solution)/shard_map/ppermute | solution.py:163
  17.6 3.8 %collective-permute-start.2 = (f32[2,8,32,128]{3,2,1,0:T(8,128)S(1)}, f32[2,8,32,128]{3,2,1,0:T(8,128)S(1)}, u32[]{:S(2)}, u32[]{:S(2)}) collective-permute-start(f32[2,8,32,128]{3,2,1,0:T(8,128)S(1)} %get-tuple-element.27), channel_id=1, source_target_pairs={{0,3},{1,2},{2,1},{3,0},{4,7},{5,6},{6,5},{7,4},{8,11},{9,10},{10,... | collective-permute-start | bytes 786440 | tf_op jit(solution)/shard_map/ppermute | solution.py:163
  21.4 0.0 collective-permute-done.9.refs_2_
  21.4 2.7 %collective-permute-done.10.refs_3_ = f32[2,8,32,128]{3,2,1,0:T(8,128)S(1)} collective-permute-done((f32[2,8,32,128]{3,2,1,0:T(8,128)S(1)}, f32[2,8,32,128]{3,2,1,0:T(8,128)S(1)}, u32[]{:S(2)}, u32[]{:S(2)}) %collective-permute-start.10) | collective-permute-done | bytes 262176 | tf_op jit(solution)/shard_map/ppermute | solution.py:163
  24.2 0.1 add_add_fusion
  24.3 3.1 %collective-permute-start.11 = (f32[2,8,32,128]{3,2,1,0:T(8,128)S(1)}, f32[2,8,32,128]{3,2,1,0:T(8,128)S(1)}, u32[]{:S(2)}, u32[]{:S(2)}) collective-permute-start(f32[2,8,32,128]{3,2,1,0:T(8,128)S(1)} %add_add_fusion), channel_id=1, source_target_pairs={{0,4},{1,5},{2,6},{3,7},{4,0},{5,1},{6,2},{7,3},{8,12},{9,13},{10,... | collective-permute-start | bytes 786440 | tf_op jit(solution)/shard_map/ppermute | solution.py:163
  27.4 0.0 collective-permute-done.refs_1_
  27.4 8.5 %collective-permute-done.1.refs_2_ = f32[2,8,32,128]{3,2,1,0:T(8,128)S(1)} collective-permute-done((f32[2,8,32,128]{3,2,1,0:T(8,128)S(1)}, f32[2,8,32,128]{3,2,1,0:T(8,128)S(1)}, u32[]{:S(2)}, u32[]{:S(2)}) %collective-permute-start.1) | collective-permute-done | bytes 262176 | tf_op jit(solution)/shard_map/ppermute | solution.py:163
  35.9 3.9 %collective-permute-done.2.refs_3_ = f32[2,8,32,128]{3,2,1,0:T(8,128)S(1)} collective-permute-done((f32[2,8,32,128]{3,2,1,0:T(8,128)S(1)}, f32[2,8,32,128]{3,2,1,0:T(8,128)S(1)}, u32[]{:S(2)}, u32[]{:S(2)}) %collective-permute-start.2) | collective-permute-done | bytes 262176 | tf_op jit(solution)/shard_map/ppermute | solution.py:163
  39.9 0.1 add_add_fusion.1
  40.0 2.0 %collective-permute-start.3 = (f32[2,8,32,128]{3,2,1,0:T(8,128)S(1)}, f32[2,8,32,128]{3,2,1,0:T(8,128)S(1)}, u32[]{:S(2)}, u32[]{:S(2)}) collective-permute-start(f32[2,8,32,128]{3,2,1,0:T(8,128)S(1)} %add_add_fusion.1), channel_id=1, source_target_pairs={{0,4},{1,5},{2,6},{3,7},{4,0},{5,1},{6,2},{7,3},{8,12},{9,13},{10,... | collective-permute-start | bytes 786440 | tf_op jit(solution)/shard_map/ppermute | solution.py:163
  41.9 0.0 collective-permute-done.11.refs_4_
  42.0 0.1 collective-permute-start.12
  42.1 11.6 %collective-permute-done.3.refs_4_ = f32[2,8,32,128]{3,2,1,0:T(8,128)S(1)} collective-permute-done((f32[2,8,32,128]{3,2,1,0:T(8,128)S(1)}, f32[2,8,32,128]{3,2,1,0:T(8,128)S(1)}, u32[]{:S(2)}, u32[]{:S(2)}) %collective-permute-start.3) | collective-permute-done | bytes 262176 | tf_op jit(solution)/shard_map/ppermute | solution.py:163
  53.8 0.0 collective-permute-done.12.refs_5_
  53.8 0.0 copy-start.5
  53.8 0.0 copy-start.7
  53.8 0.9 %shard_map.78 = (f32[2,8,32,128]{3,2,1,0:T(8,128)S(1)}, f32[2,8,32,128]{3,2,1,0:T(8,128)S(1)}, f32[2,8,32,128]{3,2,1,0:T(8,128)S(1)}, f32[2,8,32,128]{3,2,1,0:T(8,128)S(1)}) custom-call(s32[3]{0:T(128)S(1)} %pad_add_fusion.info, f32[2,8,32,128]{3,2,1,0:T(8,128)S(1)} %get-tuple-element.32.refs_0_, f32[2,8,32,128]{3,2,1,0:T(8,128)S(1)} %collective-permute-done.8.refs_1_, ...), custom_call_target="tpu_custom_call" | custom-call | flops 1966080 | bytes 2621440 | tf_op jit(solution)/shard_map/pallas_call | solution.py:97
  54.7 1.4 %collective-permute-start.13 = (f32[2,8,32,128]{3,2,1,0:T(8,128)S(1)}, f32[2,8,32,128]{3,2,1,0:T(8,128)S(1)}, u32[]{:S(2)}, u32[]{:S(2)}) collective-permute-start(f32[2,8,32,128]{3,2,1,0:T(8,128)S(1)} %get-tuple-element.37), channel_id=1, source_target_pairs={{0,1},{1,0},{2,3},{3,2},{4,5},{5,4},{6,7},{7,6},{8,9},{9,8},{10,11... | collective-permute-start | bytes 786440 | tf_op jit(solution)/shard_map/ppermute | solution.py:163
  56.1 0.0 copy-start.3
  56.1 0.0 copy-start.1
  56.1 0.1 collective-permute-start.4
  56.2 0.1 collective-permute-start.14
  56.3 2.1 %collective-permute-start.15 = (f32[2,8,32,128]{3,2,1,0:T(8,128)S(1)}, f32[2,8,32,128]{3,2,1,0:T(8,128)S(1)}, u32[]{:S(2)}, u32[]{:S(2)}) collective-permute-start(f32[2,8,32,128]{3,2,1,0:T(8,128)S(1)} %get-tuple-element.39), channel_id=1, source_target_pairs={{0,3},{1,2},{2,1},{3,0},{4,7},{5,6},{6,5},{7,4},{8,11},{9,10},{10,... | collective-permute-start | bytes 786440 | tf_op jit(solution)/shard_map/ppermute | solution.py:163
  58.4 0.0 collective-permute-done.4.refs_5_
  58.4 0.9 %shard_map.76 = (f32[2,8,32,128]{3,2,1,0:T(8,128)S(1)}, f32[2,8,32,128]{3,2,1,0:T(8,128)S(1)}, f32[2,8,32,128]{3,2,1,0:T(8,128)S(1)}, f32[2,8,32,128]{3,2,1,0:T(8,128)S(1)}) custom-call(s32[3]{0:T(128)S(1)} %pad_add_fusion.info, f32[2,8,32,128]{3,2,1,0:T(8,128)S(1)} %get-tuple-element.24.refs_0_, f32[2,8,32,128]{3,2,1,0:T(8,128)S(1)} %collective-permute-done.refs_1_, ...), custom_call_target="tpu_custom_call" | custom-call | flops 1966080 | bytes 2621440 | tf_op jit(solution)/shard_map/pallas_call | solution.py:97
  59.3 1.4 %collective-permute-start.5 = (f32[2,8,32,128]{3,2,1,0:T(8,128)S(1)}, f32[2,8,32,128]{3,2,1,0:T(8,128)S(1)}, u32[]{:S(2)}, u32[]{:S(2)}) collective-permute-start(f32[2,8,32,128]{3,2,1,0:T(8,128)S(1)} %get-tuple-element.29), channel_id=1, source_target_pairs={{0,1},{1,0},{2,3},{3,2},{4,5},{5,4},{6,7},{7,6},{8,9},{9,8},{10,11... | collective-permute-start | bytes 786440 | tf_op jit(solution)/shard_map/ppermute | solution.py:163
  60.7 0.1 collective-permute-start.6
  60.8 1.5 %collective-permute-done.13.refs_1_ = f32[2,8,32,128]{3,2,1,0:T(8,128)S(1)} collective-permute-done((f32[2,8,32,128]{3,2,1,0:T(8,128)S(1)}, f32[2,8,32,128]{3,2,1,0:T(8,128)S(1)}, u32[]{:S(2)}, u32[]{:S(2)}) %collective-permute-start.13) | collective-permute-done | bytes 262176 | tf_op jit(solution)/shard_map/ppermute | solution.py:163
  62.3 0.5 collective-permute-start.7
  62.8 2.5 %collective-permute-done.14.refs_2_ = f32[2,8,32,128]{3,2,1,0:T(8,128)S(1)} collective-permute-done((f32[2,8,32,128]{3,2,1,0:T(8,128)S(1)}, f32[2,8,32,128]{3,2,1,0:T(8,128)S(1)}, u32[]{:S(2)}, u32[]{:S(2)}) %collective-permute-start.14) | collective-permute-done | bytes 262176 | tf_op jit(solution)/shard_map/ppermute | solution.py:163
  65.4 5.8 %collective-permute-done.15.refs_3_ = f32[2,8,32,128]{3,2,1,0:T(8,128)S(1)} collective-permute-done((f32[2,8,32,128]{3,2,1,0:T(8,128)S(1)}, f32[2,8,32,128]{3,2,1,0:T(8,128)S(1)}, u32[]{:S(2)}, u32[]{:S(2)}) %collective-permute-start.15) | collective-permute-done | bytes 262176 | tf_op jit(solution)/shard_map/ppermute | solution.py:163
  71.1 0.0 copy-done.5
  71.1 0.0 copy-done.7
  71.2 0.0 copy-done.3
  71.2 0.0 copy-done.1
  71.2 4.4 %shard_map.79 = (bf16[192,2048]{1,0:T(8,128)(2,1)}, bf16[192,2048]{1,0:T(8,128)(2,1)}, bf16[192,2048]{1,0:T(8,128)(2,1)}, bf16[192,2048]{1,0:T(8,128)(2,1)}) custom-call(s32[3]{0:T(128)S(1)} %pad_add_fusion.info, bf16[192,2048]{1,0:T(8,128)(2,1)S(1)} %copy-done.1, bf16[192,2048]{1,0:T(8,128)(2,1)S(1)} %copy-done.3, bf16[192,2048]{1,0:T(8,128)(2,1)S(1)} %copy-done.5, ...), custom_call_target="tpu_custom_call" | custom-call | flops 654311424 | bytes 4194304 | tf_op jit(solution)/shard_map/pallas_call | solution.py:140
  75.5 0.0 collective-permute-done.5.refs_1_
  75.5 1.1 %collective-permute-done.6.refs_2_ = f32[2,8,32,128]{3,2,1,0:T(8,128)S(1)} collective-permute-done((f32[2,8,32,128]{3,2,1,0:T(8,128)S(1)}, f32[2,8,32,128]{3,2,1,0:T(8,128)S(1)}, u32[]{:S(2)}, u32[]{:S(2)}) %collective-permute-start.6) | collective-permute-done | bytes 262176 | tf_op jit(solution)/shard_map/ppermute | solution.py:163
  76.7 5.3 %collective-permute-done.7.refs_3_ = f32[2,8,32,128]{3,2,1,0:T(8,128)S(1)} collective-permute-done((f32[2,8,32,128]{3,2,1,0:T(8,128)S(1)}, f32[2,8,32,128]{3,2,1,0:T(8,128)S(1)}, u32[]{:S(2)}, u32[]{:S(2)}) %collective-permute-start.7) | collective-permute-done | bytes 262176 | tf_op jit(solution)/shard_map/ppermute | solution.py:163
  81.9 4.4 %shard_map.80 = (bf16[192,2048]{1,0:T(8,128)(2,1)}, bf16[192,2048]{1,0:T(8,128)(2,1)}, bf16[192,2048]{1,0:T(8,128)(2,1)}, bf16[192,2048]{1,0:T(8,128)(2,1)}) custom-call(s32[3]{0:T(128)S(1)} %pad_add_fusion.info, bf16[192,2048]{1,0:T(8,128)(2,1)S(1)} %copy-done.1, ...), custom_call_target="tpu_custom_call", output_to_operand_aliasing={{0}: (9, {}), {1}: (10, {}), {2}: (11, {}), {3}: (12, {})} | custom-call | flops 654311424 | bytes 4194304 | tf_op jit(solution)/shard_map/pallas_call | solution.py:140
  (4 shorter events, 0.1 us)
Async XLA Ops:
  0.7 1.1 %copy-start = (bf16[192,2048]{1,0:T(8,128)(2,1)S(1)}, bf16[192,2048]{1,0:T(8,128)(2,1)}, u32[]{:S(2)}) copy-start(bf16[192,2048]{1,0:T(8,128)(2,1)} %q.7) | copy-start | bytes 2359300
  1.9 1.1 %copy-start.2 = (bf16[192,2048]{1,0:T(8,128)(2,1)S(1)}, bf16[192,2048]{1,0:T(8,128)(2,1)}, u32[]{:S(2)}) copy-start(bf16[192,2048]{1,0:T(8,128)(2,1)} %k.7) | copy-start | bytes 2359300
  3.0 1.1 %copy-start.4 = (bf16[192,2048]{1,0:T(8,128)(2,1)S(1)}, bf16[192,2048]{1,0:T(8,128)(2,1)}, u32[]{:S(2)}) copy-start(bf16[192,2048]{1,0:T(8,128)(2,1)} %v.7) | copy-start | bytes 2359300
  4.1 1.1 %copy-start.6 = (bf16[192,2048]{1,0:T(8,128)(2,1)S(1)}, bf16[192,2048]{1,0:T(8,128)(2,1)}, u32[]{:S(2)}) copy-start(bf16[192,2048]{1,0:T(8,128)(2,1)} %g.7) | copy-start | bytes 2359300
  6.8 10.9 %collective-permute-start.8 = (f32[2,8,32,128]{3,2,1,0:T(8,128)S(1)}, f32[2,8,32,128]{3,2,1,0:T(8,128)S(1)}, u32[]{:S(2)}, u32[]{:S(2)}) collective-permute-start(f32[2,8,32,128]{3,2,1,0:T(8,128)S(1)} %get-tuple-element.33), channel_id=1, source_target_pairs={{0,1},{1,0},{2,3},{3,2},{4,5},{5,4},{6,7},{7,6},{8,9},{9,8},{10,11... | collective-permute-start | bytes 786440 | tf_op jit(solution)/shard_map/ppermute | solution.py:163
  9.8 11.6 %collective-permute-start.9 = (f32[2,8,32,128]{3,2,1,0:T(8,128)S(1)}, f32[2,8,32,128]{3,2,1,0:T(8,128)S(1)}, u32[]{:S(2)}, u32[]{:S(2)}) collective-permute-start(f32[2,8,32,128]{3,2,1,0:T(8,128)S(1)} %get-tuple-element.34), channel_id=1, source_target_pairs={{0,2},{1,3},{2,0},{3,1},{4,6},{5,7},{6,4},{7,5},{8,10},{9,11},{10,... | collective-permute-start | bytes 786440 | tf_op jit(solution)/shard_map/ppermute | solution.py:163
  11.4 12.8 %collective-permute-start.10 = (f32[2,8,32,128]{3,2,1,0:T(8,128)S(1)}, f32[2,8,32,128]{3,2,1,0:T(8,128)S(1)}, u32[]{:S(2)}, u32[]{:S(2)}) collective-permute-start(f32[2,8,32,128]{3,2,1,0:T(8,128)S(1)} %get-tuple-element.35), channel_id=1, source_target_pairs={{0,3},{1,2},{2,1},{3,0},{4,7},{5,6},{6,5},{7,4},{8,11},{9,10},{10,... | collective-permute-start | bytes 786440 | tf_op jit(solution)/shard_map/ppermute | solution.py:163
  12.9 14.5 %collective-permute-start = (f32[2,8,32,128]{3,2,1,0:T(8,128)S(1)}, f32[2,8,32,128]{3,2,1,0:T(8,128)S(1)}, u32[]{:S(2)}, u32[]{:S(2)}) collective-permute-start(f32[2,8,32,128]{3,2,1,0:T(8,128)S(1)} %get-tuple-element.25), channel_id=1, source_target_pairs={{0,1},{1,0},{2,3},{3,2},{4,5},{5,4},{6,7},{7,6},{8,9},{9,8},{10,11... | collective-permute-start | bytes 786440 | tf_op jit(solution)/shard_map/ppermute | solution.py:163
  14.9 21.1 %collective-permute-start.1 = (f32[2,8,32,128]{3,2,1,0:T(8,128)S(1)}, f32[2,8,32,128]{3,2,1,0:T(8,128)S(1)}, u32[]{:S(2)}, u32[]{:S(2)}) collective-permute-start(f32[2,8,32,128]{3,2,1,0:T(8,128)S(1)} %get-tuple-element.26), channel_id=1, source_target_pairs={{0,2},{1,3},{2,0},{3,1},{4,6},{5,7},{6,4},{7,5},{8,10},{9,11},{10,... | collective-permute-start | bytes 786440 | tf_op jit(solution)/shard_map/ppermute | solution.py:163
  17.6 22.2 %collective-permute-start.2 = (f32[2,8,32,128]{3,2,1,0:T(8,128)S(1)}, f32[2,8,32,128]{3,2,1,0:T(8,128)S(1)}, u32[]{:S(2)}, u32[]{:S(2)}) collective-permute-start(f32[2,8,32,128]{3,2,1,0:T(8,128)S(1)} %get-tuple-element.27), channel_id=1, source_target_pairs={{0,3},{1,2},{2,1},{3,0},{4,7},{5,6},{6,5},{7,4},{8,11},{9,10},{10,... | collective-permute-start | bytes 786440 | tf_op jit(solution)/shard_map/ppermute | solution.py:163
  24.3 17.7 %collective-permute-start.11 = (f32[2,8,32,128]{3,2,1,0:T(8,128)S(1)}, f32[2,8,32,128]{3,2,1,0:T(8,128)S(1)}, u32[]{:S(2)}, u32[]{:S(2)}) collective-permute-start(f32[2,8,32,128]{3,2,1,0:T(8,128)S(1)} %add_add_fusion), channel_id=1, source_target_pairs={{0,4},{1,5},{2,6},{3,7},{4,0},{5,1},{6,2},{7,3},{8,12},{9,13},{10,... | collective-permute-start | bytes 786440 | tf_op jit(solution)/shard_map/ppermute | solution.py:163
  40.0 13.8 %collective-permute-start.3 = (f32[2,8,32,128]{3,2,1,0:T(8,128)S(1)}, f32[2,8,32,128]{3,2,1,0:T(8,128)S(1)}, u32[]{:S(2)}, u32[]{:S(2)}) collective-permute-start(f32[2,8,32,128]{3,2,1,0:T(8,128)S(1)} %add_add_fusion.1), channel_id=1, source_target_pairs={{0,4},{1,5},{2,6},{3,7},{4,0},{5,1},{6,2},{7,3},{8,12},{9,13},{10,... | collective-permute-start | bytes 786440 | tf_op jit(solution)/shard_map/ppermute | solution.py:163
  42.0 11.8 %collective-permute-start.12 = (f32[8,32,128]{2,1,0:T(8,128)S(1)}, f32[8,32,128]{2,1,0:T(8,128)S(1)}, u32[]{:S(2)}, u32[]{:S(2)}) collective-permute-start(f32[8,32,128]{2,1,0:T(8,128)S(1)} %fusion), channel_id=1, source_target_pairs={{0,8},{8,0},{1,9},{9,1},{2,10},{10,2},{3,11},{11,3},{4,12},{12,4},... | collective-permute-start | bytes 393224 | tf_op jit(solution)/shard_map/ppermute | solution.py:192
  53.8 17.4 %copy-start.5 = (bf16[192,2048]{1,0:T(8,128)(2,1)S(1)}, bf16[192,2048]{1,0:T(8,128)(2,1)}, u32[]{:S(2)}) copy-start(bf16[192,2048]{1,0:T(8,128)(2,1)} %v.7) | copy-start | bytes 2359300
  53.8 17.4 %copy-start.7 = (bf16[192,2048]{1,0:T(8,128)(2,1)S(1)}, bf16[192,2048]{1,0:T(8,128)(2,1)}, u32[]{:S(2)}) copy-start(bf16[192,2048]{1,0:T(8,128)(2,1)} %g.7) | copy-start | bytes 2359300
  54.7 7.7 %collective-permute-start.13 = (f32[2,8,32,128]{3,2,1,0:T(8,128)S(1)}, f32[2,8,32,128]{3,2,1,0:T(8,128)S(1)}, u32[]{:S(2)}, u32[]{:S(2)}) collective-permute-start(f32[2,8,32,128]{3,2,1,0:T(8,128)S(1)} %get-tuple-element.37), channel_id=1, source_target_pairs={{0,1},{1,0},{2,3},{3,2},{4,5},{5,4},{6,7},{7,6},{8,9},{9,8},{10,11... | collective-permute-start | bytes 786440 | tf_op jit(solution)/shard_map/ppermute | solution.py:163
  56.1 15.1 %copy-start.3 = (bf16[192,2048]{1,0:T(8,128)(2,1)S(1)}, bf16[192,2048]{1,0:T(8,128)(2,1)}, u32[]{:S(2)}) copy-start(bf16[192,2048]{1,0:T(8,128)(2,1)} %k.7) | copy-start | bytes 2359300
  56.1 15.1 %copy-start.1 = (bf16[192,2048]{1,0:T(8,128)(2,1)S(1)}, bf16[192,2048]{1,0:T(8,128)(2,1)}, u32[]{:S(2)}) copy-start(bf16[192,2048]{1,0:T(8,128)(2,1)} %q.7) | copy-start | bytes 2359300
  56.1 2.3 %collective-permute-start.4 = (f32[8,32,128]{2,1,0:T(8,128)S(1)}, f32[8,32,128]{2,1,0:T(8,128)S(1)}, u32[]{:S(2)}, u32[]{:S(2)}) collective-permute-start(f32[8,32,128]{2,1,0:T(8,128)S(1)} %fusion.1), channel_id=1, source_target_pairs={{0,8},{8,0},{1,9},{9,1},{2,10},{10,2},{3,11},{11,3},{4,12},{12,4},... | collective-permute-start | bytes 393224 | tf_op jit(solution)/shard_map/ppermute | solution.py:192
  56.2 9.2 %collective-permute-start.14 = (f32[2,8,32,128]{3,2,1,0:T(8,128)S(1)}, f32[2,8,32,128]{3,2,1,0:T(8,128)S(1)}, u32[]{:S(2)}, u32[]{:S(2)}) collective-permute-start(f32[2,8,32,128]{3,2,1,0:T(8,128)S(1)} %get-tuple-element.38), channel_id=1, source_target_pairs={{0,2},{1,3},{2,0},{3,1},{4,6},{5,7},{6,4},{7,5},{8,10},{9,11},{10,... | collective-permute-start | bytes 786440 | tf_op jit(solution)/shard_map/ppermute | solution.py:163
  56.3 14.9 %collective-permute-start.15 = (f32[2,8,32,128]{3,2,1,0:T(8,128)S(1)}, f32[2,8,32,128]{3,2,1,0:T(8,128)S(1)}, u32[]{:S(2)}, u32[]{:S(2)}) collective-permute-start(f32[2,8,32,128]{3,2,1,0:T(8,128)S(1)} %get-tuple-element.39), channel_id=1, source_target_pairs={{0,3},{1,2},{2,1},{3,0},{4,7},{5,6},{6,5},{7,4},{8,11},{9,10},{10,... | collective-permute-start | bytes 786440 | tf_op jit(solution)/shard_map/ppermute | solution.py:163
  59.3 16.2 %collective-permute-start.5 = (f32[2,8,32,128]{3,2,1,0:T(8,128)S(1)}, f32[2,8,32,128]{3,2,1,0:T(8,128)S(1)}, u32[]{:S(2)}, u32[]{:S(2)}) collective-permute-start(f32[2,8,32,128]{3,2,1,0:T(8,128)S(1)} %get-tuple-element.29), channel_id=1, source_target_pairs={{0,1},{1,0},{2,3},{3,2},{4,5},{5,4},{6,7},{7,6},{8,9},{9,8},{10,11... | collective-permute-start | bytes 786440 | tf_op jit(solution)/shard_map/ppermute | solution.py:163
  60.7 16.0 %collective-permute-start.6 = (f32[2,8,32,128]{3,2,1,0:T(8,128)S(1)}, f32[2,8,32,128]{3,2,1,0:T(8,128)S(1)}, u32[]{:S(2)}, u32[]{:S(2)}) collective-permute-start(f32[2,8,32,128]{3,2,1,0:T(8,128)S(1)} %get-tuple-element.30), channel_id=1, source_target_pairs={{0,2},{1,3},{2,0},{3,1},{4,6},{5,7},{6,4},{7,5},{8,10},{9,11},{10,... | collective-permute-start | bytes 786440 | tf_op jit(solution)/shard_map/ppermute | solution.py:163
  62.3 19.6 %collective-permute-start.7 = (f32[2,8,32,128]{3,2,1,0:T(8,128)S(1)}, f32[2,8,32,128]{3,2,1,0:T(8,128)S(1)}, u32[]{:S(2)}, u32[]{:S(2)}) collective-permute-start(f32[2,8,32,128]{3,2,1,0:T(8,128)S(1)} %get-tuple-element.31), channel_id=1, source_target_pairs={{0,3},{1,2},{2,1},{3,0},{4,7},{5,6},{6,5},{7,4},{8,11},{9,10},{10,... | collective-permute-start | bytes 786440 | tf_op jit(solution)/shard_map/ppermute | solution.py:163

commit v2 on v1

v2 whole, which is shorter than its diff:
```python
import functools
import math

import jax
import jax.numpy as jnp
from jax import lax
from jax.experimental import pallas as pl
from jax.experimental.pallas import tpu as pltpu
from jax.sharding import PartitionSpec as P

HEAD_DIM = 128
PARTS = 4
QUARTER = HEAD_DIM // PARTS
CHUNKS = (8, 8)
STEP = 4
FINISH_STEP = (4, 4)
ORDER = (
    ("state", 0),
    ("state", 1),
    ("sum", 0),
    ("sum", 1),
    ("half", 0),
    ("spread", 0),
    ("half", 1),
    ("spread", 1, (0, 1), (0, 2), (0, 3)),
    ("finish", 0),
    ("finish", 1),
)

F32 = jnp.float32
BF16 = jnp.bfloat16
VMEM_LIMIT = 40 * 1024 * 1024
STATE_LIMIT = 60 * 1024 * 1024

LIGHT = pl.CostEstimate(flops=1, bytes_accessed=1, transcendentals=0)
SCALARS = pl.BlockSpec(memory_space=pltpu.SMEM)
WHOLE = pl.BlockSpec(memory_space=pltpu.VMEM)
FAR = pl.BlockSpec(memory_space=pltpu.HBM)
LEFT = pl.BlockSpec(memory_space=pl.ANY)


def dot(a, b, ca, cb):
    return lax.dot_general(a, b, (((ca,), (cb,)), ((), ())), preferred_element_type=F32)


def place(info, r):
    return pl.multiple_of((info[0] ^ r) * QUARTER, QUARTER)


def state_kernel(first, heads, info, q, k, v, g, *refs):
    outs, (held, hold, sems) = refs[-PARTS - 3 : -3], refs[-3:]
    groups = [(at, min(STEP, heads - at)) for at in range(0, heads, STEP)]
    copies = []
    for n, (at, wide) in enumerate(groups):
        there = pl.ds((first + at) * HEAD_DIM, wide * HEAD_DIM)
        here = pl.ds(at * HEAD_DIM, wide * HEAD_DIM)
        copies.append(
            [
                pltpu.make_async_copy(ref.at[:, there], held.at[i, :, here], sems.at[n, i])
                for i, ref in enumerate((k, v, q, g))
            ]
        )
        for copy in copies[-1]:
            copy.start()
    for n, (at, wide) in enumerate(groups):
        for half in range(2):
            copies[n][2 * half].wait()
            copies[n][2 * half + 1].wait()
            for h in range(at, at + wide):
                cols = slice(h * HEAD_DIM, (h + 1) * HEAD_DIM)
                hold[half] = dot(held[2 * half, :, cols], held[2 * half + 1, :, cols], 0, 0)
                for r in range(PARTS):
                    outs[r][half, h] = hold[half, pl.ds(place(info, r), QUARTER), :]


def states(info, arrays, first, heads, behind):
    rows = arrays[0].shape[0]
    piece = jax.ShapeDtypeStruct((2, heads, QUARTER, HEAD_DIM), F32)
    return pl.pallas_call(
        functools.partial(state_kernel, first, heads),
        out_shape=[piece] * PARTS,
        in_specs=[SCALARS] + [FAR] * 4 + [LEFT] * len(behind),
        out_specs=[WHOLE] * PARTS,
        scratch_shapes=[
            pltpu.VMEM((4, rows, heads * HEAD_DIM), BF16),
            pltpu.VMEM((2, HEAD_DIM, HEAD_DIM), F32),
            pltpu.SemaphoreType.DMA((-(-heads // STEP), 4)),
        ],
        compiler_params=pltpu.CompilerParams(vmem_limit_bytes=STATE_LIMIT),
        cost_estimate=LIGHT,
    )(info, *arrays, *behind)


def sum_kernel(a, b, c, d, *refs):
    refs[-1][...] = (a[...] + b[...]) + (c[...] + d[...])


def block_sum(pieces, behind):
    shape = jax.ShapeDtypeStruct(pieces[0].shape, F32)
    return pl.pallas_call(
        sum_kernel,
        out_shape=shape,
        in_specs=[WHOLE] * PARTS + [LEFT] * len(behind),
        out_specs=WHOLE,
        compiler_params=pltpu.CompilerParams(vmem_limit_bytes=VMEM_LIMIT),
        cost_estimate=LIGHT,
    )(*pieces, *behind)


def across_kernel(info, a, b, *refs):
    take = jnp.where(info[1] > 0, 1, 0)
    refs[-1][...] = a[take] + b[take]


def half_total(info, total, other, behind):
    shape = jax.ShapeDtypeStruct(total.shape[1:], F32)
    return pl.pallas_call(
        across_kernel,
        out_shape=shape,
        in_specs=[SCALARS, WHOLE, WHOLE] + [LEFT] * len(behind),
        out_specs=WHOLE,
        compiler_params=pltpu.CompilerParams(vmem_limit_bytes=VMEM_LIMIT),
        cost_estimate=LIGHT,
    )(info, total, other, *behind)


def spread_kernel(levels, info, *refs):
    pieces = refs[:PARTS]
    totals = refs[PARTS : PARTS + levels]
    across = refs[PARTS + levels]
    outs = refs[-PARTS:]
    mine, node, block = info[0], info[1], info[2]
    prefix = jnp.where(node > 0, across[...], 0.0)
    suffix = jnp.where(node > 0, 0.0, across[...])
    for level in range(levels):
        upper = ((block >> level) & 1) > 0
        prefix = prefix + jnp.where(upper, totals[level][0], 0.0)
        suffix = suffix + jnp.where(upper, 0.0, totals[level][1])
    for r in range(PARTS):
        before, after = prefix, suffix
        for other in range(PARTS):
            if other != r:
                earlier = (mine ^ other) < (mine ^ r)
                before = before + jnp.where(earlier, pieces[other][0], 0.0)
                after = after + jnp.where(earlier, 0.0, pieces[other][1])
        outs[r][0] = before
        outs[r][1] = after


def spread(info, pieces, totals, across, behind):
    levels = len(totals)
    shapes = [jax.ShapeDtypeStruct(pieces[0].shape, F32)] * PARTS
    return pl.pallas_call(
        functools.partial(spread_kernel, levels),
        out_shape=shapes,
        in_specs=[SCALARS] + [WHOLE] * (PARTS + levels + 1) + [LEFT] * len(behind),
        out_specs=[WHOLE] * PARTS,
        compiler_params=pltpu.CompilerParams(vmem_limit_bytes=VMEM_LIMIT),
        cost_estimate=LIGHT,
    )(info, *pieces, *totals, across, *behind)


def finish_kernel(step, factor, info, q, k, v, g, *refs):
    pieces, (att, qg, kg, vg), hold = refs[:PARTS], refs[-5:-1], refs[-1]
    rows = q.shape[0]
    causal = lax.broadcasted_iota(jnp.int32, (rows, rows), 0) >= lax.broadcasted_iota(
        jnp.int32, (rows, rows), 1
    )
    for h in range(step):
        cols = slice(h * HEAD_DIM, (h + 1) * HEAD_DIM)
        for r in range(PARTS):
            at = pl.ds(place(info, r), QUARTER)
            hold[0, at, :] = pieces[r][0, h].astype(BF16)
            hold[1, at, :] = pieces[r][1, h].astype(BF16)
        qh, kh, vh, gh = q[:, cols], k[:, cols], v[:, cols], g[:, cols]
        prefix, suffix = hold[0], hold[1]
        weights = jnp.where(causal, dot(qh, kh, 1, 1), 0.0).astype(BF16)
        grad_weights = jnp.where(causal, dot(gh, vh, 1, 1), 0.0).astype(BF16)
        att[:, cols] = (factor * (dot(weights, vh, 1, 0) + dot(qh, prefix, 1, 0))).astype(BF16)
        qg[:, cols] = (factor * (dot(grad_weights, kh, 1, 0) + dot(gh, prefix, 1, 1))).astype(BF16)
        kg[:, cols] = (factor * (dot(grad_weights, qh, 0, 0) + dot(vh, suffix, 1, 1))).astype(BF16)
        vg[:, cols] = (factor * (dot(weights, gh, 0, 0) + dot(kh, suffix, 1, 0))).astype(BF16)


def finish(info, arrays, pieces, outs, first, step, factor, behind):
    rows, width = arrays[0].shape
    heads = pieces[0].shape[1]
    columns = pl.BlockSpec((rows, step * HEAD_DIM), lambda i, info: (0, first // step + i))
    quarter = pl.BlockSpec((2, step, QUARTER, HEAD_DIM), lambda i, info: (0, i, 0, 0))
    given = [info, *arrays, *pieces, *outs, *behind]
    fixed = 5 + PARTS
    return pl.pallas_call(
        functools.partial(finish_kernel, step, factor),
        out_shape=[jax.ShapeDtypeStruct((rows, width), BF16)] * 4,
        grid_spec=pltpu.PrefetchScalarGridSpec(
            num_scalar_prefetch=1,
            grid=(heads // step,),
            in_specs=[columns] * 4
            + [quarter] * PARTS
            + [LEFT] * (len(outs) + len(behind)),
            out_specs=[columns] * 4,
            scratch_shapes=[pltpu.VMEM((2, HEAD_DIM, HEAD_DIM), BF16)],
        ),
        input_output_aliases={fixed + i: i for i in range(len(outs))},
        compiler_params=pltpu.CompilerParams(vmem_limit_bytes=VMEM_LIMIT),
        cost_estimate=LIGHT,
    )(*given)


def swap(array, size, mask):
    return lax.ppermute(array, "local", [(i, i ^ mask) for i in range(size)])


def local(query_rows, key_rows, value_rows, out_grad):
    arrays = (query_rows, key_rows, value_rows, out_grad)
    rows, width = query_rows.shape
    heads = width // HEAD_DIM
    size, nodes = lax.axis_size("local"), lax.axis_size("node")
    blocks = size // PARTS
    levels = blocks.bit_length() - 1
    assert nodes == 2 and PARTS << levels == size and sum(CHUNKS) == heads
    factor = 1.0 / math.sqrt(HEAD_DIM * rows * nodes * size)
    node, place_in = lax.axis_index("node"), lax.axis_index("local")
    info = jnp.stack([place_in % PARTS, node, place_in // PARTS]).astype(jnp.int32)

    firsts = [sum(CHUNKS[:i]) for i in range(len(CHUNKS))]
    done = {}
    outs = ()
    last = info
    for stage, i, *after in ORDER:
        first, count = firsts[i], CHUNKS[i]
        behind = [last] + [done["ready", j][r] for j, r in after]
        if stage == "state":
            own = states(info, arrays, first, count, behind)
            last = own[0]
            got = {r: swap(own[r], size, r) for r in (1, 3, 2)}
            done["pieces", i] = [own[0], got[1], got[2], got[3]]
        elif stage == "sum":
            last = total = block_sum(done["pieces", i], behind)
            totals = []
            for level in range(levels):
                if level:
                    total = total + totals[-1]
                totals.append(swap(total, size, PARTS << level))
            done["totals", i] = total, totals
        elif stage == "half":
            total, totals = done["totals", i]
            last = half_total(info, total, totals[-1], behind)
            done["across", i] = lax.ppermute(last, "node", [(0, 1), (1, 0)])
        elif stage == "spread":
            ready = spread(info, done["pieces", i], done["totals", i][1], done["across", i], behind)
            last = ready[0]
            back = {r: swap(ready[r], size, r) for r in (1, 3, 2)}
            done["ready", i] = [ready[0], back[1], back[2], back[3]]
        else:
            outs = finish(info, arrays, done["ready", i], outs, first, FINISH_STEP[i], factor, behind)
    return tuple(outs)


def solution(mesh):
    rows = P(("group", "node", "local"), None)
    return jax.shard_map(
        local, mesh=mesh, in_specs=(rows,) * 4, out_specs=(rows,) * 4, check_vma=False
    )
```

time: 86.6 us -> 82.1 us (0.948)
  Pallas kernels: 13.5 us -> 19.6 us
  waiting for transfers between devices: 44.3 us -> 38.3 us
  local copies, waits for them, and re-layouts: 4.56 us -> 0.98 us
  starting transfers between devices: 22.8 us -> 21.6 us
    ppermute x14, waiting for transfers between devices: 44.3 us -> 37 us  [swap(): return lax.ppermute(array, 'local', [(i, i ^ mask) for i in range(size)])]
    pallas_call x4 -> x8, Pallas kernels: 4.73 us -> 10.8 us  [the longest x2 7.88 us: states(): pl.pallas_call(functools.partial(state_kernel, first, heads), out_shape=[...]
    unnamed x16, local copies, waits for them, and re-layouts: 4.56 us -> 0.98 us
    ppermute x2, waiting for transfers between devices: 0.01 us -> 1.34 us  [local(): done['across', i] = lax.ppermute(last, 'node', [(0, 1), (1, 0)])]
    ppermute x14, starting transfers between devices: 22.7 us -> 21.4 us  [swap(): return lax.ppermute(array, 'local', [(i, i ^ mask) for i in range(size)])]
  transfers between devices with their start and end apart: 16 -> 16, of which waited for: 10 -> 9; matrix products, arithmetic and copies ran while one was open for 0% -> 0% of each run, Pallas kernels for 8% -> 12%
where the time goes in v2:
time: 82.1 us; the launch traced here: 81.8 us
  waiting for transfers between devices  38.3 us (47%)
  starting transfers between devices  21.6 us (26%)
  Pallas kernels  19.6 us (24%)
  local copies, waits for them, and re-layouts  0.98 us (1%)
    ppermute x14, waiting for transfers between devices, swap(): return lax.ppermute(array, 'local', [(i, i ^ mask) for i in range(size)])  37 us
    ppermute x14, starting transfers between devices, swap(): return lax.ppermute(array, 'local', [(i, i ^ mask) for i in range(size)])  21.4 us
    pallas_call x2, Pallas kernels, finish(): pl.pallas_call(functools.partial(finish_kernel, step, factor), out_shape=...  8.74 us
    pallas_call x2, Pallas kernels, states(): pl.pallas_call(functools.partial(state_kernel, first, heads), out_shape=[...  7.88 us
    pallas_call x2, Pallas kernels, spread(): pl.pallas_call(functools.partial(spread_kernel, levels), out_shape=shapes...  1.74 us
  transfers between devices with their start and end apart: 16, of which 9 were waited for; matrix products, arithmetic and copies ran while one was open for 0% of the time, Pallas kernels for 12%

profile of v2, /device:TPU:0, one launch (start us, length us, event | category | flops | bytes accessed | tf_op | source)
XLA Modules:
  0.0 81.8 jit_solution(185938126867791377)
XLA Ops:
  0.7 0.6 pad_add_fusion.info.refs_0_
  1.3 3.8 %shard_map.75 = (f32[2,8,32,128]{3,2,1,0:T(8,128)}, f32[2,8,32,128]{3,2,1,0:T(8,128)}, f32[2,8,32,128]{3,2,1,0:T(8,128)}, f32[2,8,32,128]{3,2,1,0:T(8,128)}) custom-call(s32[3]{0:T(128)} %pad_add_fusion.info.refs_0_, bf16[192,2048]{1,0:T(8,128)(2,1)} %q.7, bf16[192,2048]{1,0:T(8,128)(2,1)} %k.7, bf16[192,2048]{1,0:T(8,128)(2,1)} %v.7, bf16[192,2048]{1,0:T(8,128)(2,1)} %g.7, ...), custom_call_target="tpu_custom_call" | custom-call | flops 1 | bytes 1 | tf_op jit(solution)/shard_map/pallas_call | solution.py:79
  5.1 3.0 %collective-permute-start.3 = (f32[2,8,32,128]{3,2,1,0:T(8,128)}, f32[2,8,32,128]{3,2,1,0:T(8,128)S(1)}, u32[]{:S(2)}, u32[]{:S(2)}) collective-permute-start(f32[2,8,32,128]{3,2,1,0:T(8,128)} %get-tuple-element.29), channel_id=1, source_target_pairs={{0,1},{1,0},{2,3},{3,2},{4,5},{5,4},{6,7},{7,6},{8,9},{9,8},{10,11... | collective-permute-start | bytes 786440 | tf_op jit(solution)/shard_map/ppermute | solution.py:211
  8.2 1.6 %collective-permute-start.4 = (f32[2,8,32,128]{3,2,1,0:T(8,128)}, f32[2,8,32,128]{3,2,1,0:T(8,128)S(1)}, u32[]{:S(2)}, u32[]{:S(2)}) collective-permute-start(f32[2,8,32,128]{3,2,1,0:T(8,128)} %get-tuple-element.30), channel_id=1, source_target_pairs={{0,2},{1,3},{2,0},{3,1},{4,6},{5,7},{6,4},{7,5},{8,10},{9,11},{10,... | collective-permute-start | bytes 786440 | tf_op jit(solution)/shard_map/ppermute | solution.py:211
  9.7 0.0 collective-permute-start.5
  9.7 0.0 copy-start.6
  9.7 4.0 %shard_map.76 = (f32[2,8,32,128]{3,2,1,0:T(8,128)}, f32[2,8,32,128]{3,2,1,0:T(8,128)}, f32[2,8,32,128]{3,2,1,0:T(8,128)}, f32[2,8,32,128]{3,2,1,0:T(8,128)}) custom-call(s32[3]{0:T(128)} %pad_add_fusion.info.refs_0_, bf16[192,2048]{1,0:T(8,128)(2,1)} %q.7, bf16[192,2048]{1,0:T(8,128)(2,1)} %k.7, bf16[192,2048]{1,0:T(8,128)(2,1)} %v.7, bf16[192,2048]{1,0:T(8,128)(2,1)} %g.7, ...), custom_call_target="tpu_custom_call" | custom-call | flops 1 | bytes 1 | tf_op jit(solution)/shard_map/pallas_call | solution.py:79
  13.8 2.0 %collective-permute-start = (f32[2,8,32,128]{3,2,1,0:T(8,128)}, f32[2,8,32,128]{3,2,1,0:T(8,128)S(1)}, u32[]{:S(2)}, u32[]{:S(2)}) collective-permute-start(f32[2,8,32,128]{3,2,1,0:T(8,128)} %get-tuple-element.26), channel_id=1, source_target_pairs={{0,1},{1,0},{2,3},{3,2},{4,5},{5,4},{6,7},{7,6},{8,9},{9,8},{10,11... | collective-permute-start | bytes 786440 | tf_op jit(solution)/shard_map/ppermute | solution.py:211
  15.8 1.6 %collective-permute-start.1 = (f32[2,8,32,128]{3,2,1,0:T(8,128)}, f32[2,8,32,128]{3,2,1,0:T(8,128)S(1)}, u32[]{:S(2)}, u32[]{:S(2)}) collective-permute-start(f32[2,8,32,128]{3,2,1,0:T(8,128)} %get-tuple-element.27), channel_id=1, source_target_pairs={{0,2},{1,3},{2,0},{3,1},{4,6},{5,7},{6,4},{7,5},{8,10},{9,11},{10,... | collective-permute-start | bytes 786440 | tf_op jit(solution)/shard_map/ppermute | solution.py:211
  17.4 0.0 collective-permute-done.3.b.refs_1_
  17.4 0.4 collective-permute-start.2
  17.7 0.0 collective-permute-done.4.c.refs_2_
  17.7 5.0 %collective-permute-done.5.d.refs_3_ = f32[2,8,32,128]{3,2,1,0:T(8,128)S(1)} collective-permute-done((f32[2,8,32,128]{3,2,1,0:T(8,128)}, f32[2,8,32,128]{3,2,1,0:T(8,128)S(1)}, u32[]{:S(2)}, u32[]{:S(2)}) %collective-permute-start.5) | collective-permute-done | bytes 262176 | tf_op jit(solution)/shard_map/ppermute | solution.py:211
  22.7 0.0 copy-done.6
  22.7 0.0 copy-start.4
  22.7 0.9 %copy-done.4 = f32[2,8,32,128]{3,2,1,0:T(8,128)S(1)} copy-done((f32[2,8,32,128]{3,2,1,0:T(8,128)S(1)}, f32[2,8,32,128]{3,2,1,0:T(8,128)}, u32[]{:S(2)}) %copy-start.4) | copy-done | bytes 262168
  23.7 0.0 copy-start.5
  23.7 0.1 shard_map.77.refs_0_.a
  23.8 0.0 copy-start.7
  23.8 3.1 %collective-permute-start.7 = (f32[2,8,32,128]{3,2,1,0:T(8,128)S(1)}, f32[2,8,32,128]{3,2,1,0:T(8,128)S(1)}, u32[]{:S(2)}, u32[]{:S(2)}) collective-permute-start(f32[2,8,32,128]{3,2,1,0:T(8,128)S(1)} %shard_map.77.refs_0_.a), channel_id=1, source_target_pairs={{0,4},{1,5},{2,6},{3,7},{4,0},{5,1},{6,2},{7,3},{8,12},{9,13},{10,... | collective-permute-start | bytes 786440 | tf_op jit(solution)/shard_map/ppermute | solution.py:211
  26.9 0.0 collective-permute-done.b.refs_1_
  26.9 7.6 %collective-permute-done.1.c.refs_2_ = f32[2,8,32,128]{3,2,1,0:T(8,128)S(1)} collective-permute-done((f32[2,8,32,128]{3,2,1,0:T(8,128)}, f32[2,8,32,128]{3,2,1,0:T(8,128)S(1)}, u32[]{:S(2)}, u32[]{:S(2)}) %collective-permute-start.1) | collective-permute-done | bytes 262176 | tf_op jit(solution)/shard_map/ppermute | solution.py:211
  34.5 3.9 %collective-permute-done.2.d.refs_3_ = f32[2,8,32,128]{3,2,1,0:T(8,128)S(1)} collective-permute-done((f32[2,8,32,128]{3,2,1,0:T(8,128)}, f32[2,8,32,128]{3,2,1,0:T(8,128)S(1)}, u32[]{:S(2)}, u32[]{:S(2)}) %collective-permute-start.2) | collective-permute-done | bytes 262176 | tf_op jit(solution)/shard_map/ppermute | solution.py:211
  38.4 0.0 copy-done.5
  38.4 0.1 shard_map.78.refs_0_.a
  38.5 0.0 collective-permute-done.7.b.refs_4_
  38.5 0.0 copy-done.7
  38.5 0.6 shard_map.79.refs_6_
  39.1 0.1 collective-permute-start.8
  39.2 2.7 %collective-permute-start.6 = (f32[2,8,32,128]{3,2,1,0:T(8,128)S(1)}, f32[2,8,32,128]{3,2,1,0:T(8,128)S(1)}, u32[]{:S(2)}, u32[]{:S(2)}) collective-permute-start(f32[2,8,32,128]{3,2,1,0:T(8,128)S(1)} %shard_map.78.refs_0_.a), channel_id=1, source_target_pairs={{0,4},{1,5},{2,6},{3,7},{4,0},{5,1},{6,2},{7,3},{8,12},{9,13},{10,... | collective-permute-start | bytes 786440 | tf_op jit(solution)/shard_map/ppermute | solution.py:211
  41.8 0.0 collective-permute-done.8.refs_5_
  41.9 0.9 %shard_map.80 = (f32[2,8,32,128]{3,2,1,0:T(8,128)S(1)}, f32[2,8,32,128]{3,2,1,0:T(8,128)S(1)}, f32[2,8,32,128]{3,2,1,0:T(8,128)S(1)}, f32[2,8,32,128]{3,2,1,0:T(8,128)S(1)}) custom-call(s32[3]{0:T(128)S(1)} %copy-done.7, f32[2,8,32,128]{3,2,1,0:T(8,128)S(1)} %copy-done.6, f32[2,8,32,128]{3,2,1,0:T(8,128)S(1)} %collective-permute-done.3.b.refs_1_, ...), custom_call_target="tpu_custom_call" | custom-call | flops 1 | bytes 1 | tf_op jit(solution)/shard_map/pallas_call | solution.py:153
  42.7 0.6 collective-permute-start.10
  43.3 2.7 %collective-permute-start.11 = (f32[2,8,32,128]{3,2,1,0:T(8,128)S(1)}, f32[2,8,32,128]{3,2,1,0:T(8,128)S(1)}, u32[]{:S(2)}, u32[]{:S(2)}) collective-permute-start(f32[2,8,32,128]{3,2,1,0:T(8,128)S(1)} %get-tuple-element.34), channel_id=1, source_target_pairs={{0,2},{1,3},{2,0},{3,1},{4,6},{5,7},{6,4},{7,5},{8,10},{9,11},{10,... | collective-permute-start | bytes 786440 | tf_op jit(solution)/shard_map/ppermute | solution.py:211
  46.0 0.3 collective-permute-start.12
  46.3 8.2 %collective-permute-done.6.b.refs_4_ = f32[2,8,32,128]{3,2,1,0:T(8,128)S(1)} collective-permute-done((f32[2,8,32,128]{3,2,1,0:T(8,128)S(1)}, f32[2,8,32,128]{3,2,1,0:T(8,128)S(1)}, u32[]{:S(2)}, u32[]{:S(2)}) %collective-permute-start.6) | collective-permute-done | bytes 262176 | tf_op jit(solution)/shard_map/ppermute | solution.py:211
  54.5 0.0 copy-start.3
  54.5 0.6 shard_map.81.refs_6_
  55.1 0.0 copy-start
  55.1 0.0 copy-start.1
  55.1 0.0 copy-start.2
  55.1 0.1 collective-permute-start.9
  55.2 1.3 %collective-permute-done.9.refs_5_ = f32[8,32,128]{2,1,0:T(8,128)S(1)} collective-permute-done((f32[8,32,128]{2,1,0:T(8,128)S(1)}, f32[8,32,128]{2,1,0:T(8,128)S(1)}, u32[]{:S(2)}, u32[]{:S(2)}) %collective-permute-start.9) | collective-permute-done | bytes 131104 | tf_op jit(solution)/shard_map/ppermute | solution.py:249
  56.5 0.0 collective-permute-done.10.refs_7_.refs_1_
  56.5 0.0 collective-permute-done.11.refs_8_.refs_2_
  56.5 5.9 %collective-permute-done.12.refs_9_.refs_3_ = f32[2,8,32,128]{3,2,1,0:T(8,128)S(1)} collective-permute-done((f32[2,8,32,128]{3,2,1,0:T(8,128)S(1)}, f32[2,8,32,128]{3,2,1,0:T(8,128)S(1)}, u32[]{:S(2)}, u32[]{:S(2)}) %collective-permute-start.12) | collective-permute-done | bytes 262176 | tf_op jit(solution)/shard_map/ppermute | solution.py:211
  62.5 0.9 %shard_map.82 = (f32[2,8,32,128]{3,2,1,0:T(8,128)S(1)}, f32[2,8,32,128]{3,2,1,0:T(8,128)S(1)}, f32[2,8,32,128]{3,2,1,0:T(8,128)S(1)}, f32[2,8,32,128]{3,2,1,0:T(8,128)S(1)}) custom-call(s32[3]{0:T(128)S(1)} %copy-done.7, f32[2,8,32,128]{3,2,1,0:T(8,128)S(1)} %copy-done.5, f32[2,8,32,128]{3,2,1,0:T(8,128)S(1)} %collective-permute-done.b.refs_1_, ...), custom_call_target="tpu_custom_call" | custom-call | flops 1 | bytes 1 | tf_op jit(solution)/shard_map/pallas_call | solution.py:153
  63.4 0.4 collective-permute-start.13
  63.8 0.4 collective-permute-start.14
  64.2 2.7 %collective-permute-start.15 = (f32[2,8,32,128]{3,2,1,0:T(8,128)S(1)}, f32[2,8,32,128]{3,2,1,0:T(8,128)S(1)}, u32[]{:S(2)}, u32[]{:S(2)}) collective-permute-start(f32[2,8,32,128]{3,2,1,0:T(8,128)S(1)} %get-tuple-element.39), channel_id=1, source_target_pairs={{0,3},{1,2},{2,1},{3,0},{4,7},{5,6},{6,5},{7,4},{8,11},{9,10},{10,... | collective-permute-start | bytes 786440 | tf_op jit(solution)/shard_map/ppermute | solution.py:211
  66.9 0.0 copy-done.3
  66.9 0.0 copy-done
  66.9 0.0 copy-done.1
  66.9 0.0 copy-done.2
  66.9 4.4 %shard_map.83 = (bf16[192,2048]{1,0:T(8,128)(2,1)}, bf16[192,2048]{1,0:T(8,128)(2,1)}, bf16[192,2048]{1,0:T(8,128)(2,1)}, bf16[192,2048]{1,0:T(8,128)(2,1)}) custom-call(s32[3]{0:T(128)S(1)} %copy-done.7, bf16[192,2048]{1,0:T(8,128)(2,1)S(1)} %copy-done, bf16[192,2048]{1,0:T(8,128)(2,1)S(1)} %copy-done.1, bf16[192,2048]{1,0:T(8,128)(2,1)S(1)} %copy-done.2, ...), custom_call_target="tpu_custom_call" | custom-call | flops 1 | bytes 1 | tf_op jit(solution)/shard_map/pallas_call | solution.py:192
  71.3 0.5 collective-permute-done.13.refs_1_
  71.8 1.2 %collective-permute-done.14.refs_2_ = f32[2,8,32,128]{3,2,1,0:T(8,128)S(1)} collective-permute-done((f32[2,8,32,128]{3,2,1,0:T(8,128)S(1)}, f32[2,8,32,128]{3,2,1,0:T(8,128)S(1)}, u32[]{:S(2)}, u32[]{:S(2)}) %collective-permute-start.14) | collective-permute-done | bytes 262176 | tf_op jit(solution)/shard_map/ppermute | solution.py:211
  73.0 4.5 %collective-permute-done.15.refs_3_ = f32[2,8,32,128]{3,2,1,0:T(8,128)S(1)} collective-permute-done((f32[2,8,32,128]{3,2,1,0:T(8,128)S(1)}, f32[2,8,32,128]{3,2,1,0:T(8,128)S(1)}, u32[]{:S(2)}, u32[]{:S(2)}) %collective-permute-start.15) | collective-permute-done | bytes 262176 | tf_op jit(solution)/shard_map/ppermute | solution.py:211
  77.5 4.4 %shard_map.84 = (bf16[192,2048]{1,0:T(8,128)(2,1)}, bf16[192,2048]{1,0:T(8,128)(2,1)}, bf16[192,2048]{1,0:T(8,128)(2,1)}, bf16[192,2048]{1,0:T(8,128)(2,1)}) custom-call(s32[3]{0:T(128)S(1)} %copy-done.7, bf16[192,2048]{1,0:T(8,128)(2,1)S(1)} %copy-done, ...), custom_call_target="tpu_custom_call", output_to_operand_aliasing={{0}: (9, {}), {1}: (10, {}), {2}: (11, {}), {3}: (12, {})} | custom-call | flops 1 | bytes 1 | tf_op jit(solution)/shard_map/pallas_call | solution.py:192
Async XLA Ops:
  5.1 12.2 %collective-permute-start.3 = (f32[2,8,32,128]{3,2,1,0:T(8,128)}, f32[2,8,32,128]{3,2,1,0:T(8,128)S(1)}, u32[]{:S(2)}, u32[]{:S(2)}) collective-permute-start(f32[2,8,32,128]{3,2,1,0:T(8,128)} %get-tuple-element.29), channel_id=1, source_target_pairs={{0,1},{1,0},{2,3},{3,2},{4,5},{5,4},{6,7},{7,6},{8,9},{9,8},{10,11... | collective-permute-start | bytes 786440 | tf_op jit(solution)/shard_map/ppermute | solution.py:211
  8.2 9.6 %collective-permute-start.4 = (f32[2,8,32,128]{3,2,1,0:T(8,128)}, f32[2,8,32,128]{3,2,1,0:T(8,128)S(1)}, u32[]{:S(2)}, u32[]{:S(2)}) collective-permute-start(f32[2,8,32,128]{3,2,1,0:T(8,128)} %get-tuple-element.30), channel_id=1, source_target_pairs={{0,2},{1,3},{2,0},{3,1},{4,6},{5,7},{6,4},{7,5},{8,10},{9,11},{10,... | collective-permute-start | bytes 786440 | tf_op jit(solution)/shard_map/ppermute | solution.py:211
  9.7 13.0 %collective-permute-start.5 = (f32[2,8,32,128]{3,2,1,0:T(8,128)}, f32[2,8,32,128]{3,2,1,0:T(8,128)S(1)}, u32[]{:S(2)}, u32[]{:S(2)}) collective-permute-start(f32[2,8,32,128]{3,2,1,0:T(8,128)} %get-tuple-element.31), channel_id=1, source_target_pairs={{0,3},{1,2},{2,1},{3,0},{4,7},{5,6},{6,5},{7,4},{8,11},{9,10},{10,... | collective-permute-start | bytes 786440 | tf_op jit(solution)/shard_map/ppermute | solution.py:211
  9.7 13.0 %copy-start.6 = (f32[2,8,32,128]{3,2,1,0:T(8,128)S(1)}, f32[2,8,32,128]{3,2,1,0:T(8,128)}, u32[]{:S(2)}) copy-start(f32[2,8,32,128]{3,2,1,0:T(8,128)} %get-tuple-element.24.refs_0_.a) | copy-start | bytes 786436
  13.8 13.1 %collective-permute-start = (f32[2,8,32,128]{3,2,1,0:T(8,128)}, f32[2,8,32,128]{3,2,1,0:T(8,128)S(1)}, u32[]{:S(2)}, u32[]{:S(2)}) collective-permute-start(f32[2,8,32,128]{3,2,1,0:T(8,128)} %get-tuple-element.26), channel_id=1, source_target_pairs={{0,1},{1,0},{2,3},{3,2},{4,5},{5,4},{6,7},{7,6},{8,9},{9,8},{10,11... | collective-permute-start | bytes 786440 | tf_op jit(solution)/shard_map/ppermute | solution.py:211
  15.8 18.7 %collective-permute-start.1 = (f32[2,8,32,128]{3,2,1,0:T(8,128)}, f32[2,8,32,128]{3,2,1,0:T(8,128)S(1)}, u32[]{:S(2)}, u32[]{:S(2)}) collective-permute-start(f32[2,8,32,128]{3,2,1,0:T(8,128)} %get-tuple-element.27), channel_id=1, source_target_pairs={{0,2},{1,3},{2,0},{3,1},{4,6},{5,7},{6,4},{7,5},{8,10},{9,11},{10,... | collective-permute-start | bytes 786440 | tf_op jit(solution)/shard_map/ppermute | solution.py:211
  17.4 21.1 %collective-permute-start.2 = (f32[2,8,32,128]{3,2,1,0:T(8,128)}, f32[2,8,32,128]{3,2,1,0:T(8,128)S(1)}, u32[]{:S(2)}, u32[]{:S(2)}) collective-permute-start(f32[2,8,32,128]{3,2,1,0:T(8,128)} %get-tuple-element.28), channel_id=1, source_target_pairs={{0,3},{1,2},{2,1},{3,0},{4,7},{5,6},{6,5},{7,4},{8,11},{9,10},{10,... | collective-permute-start | bytes 786440 | tf_op jit(solution)/shard_map/ppermute | solution.py:211
  22.7 1.0 %copy-start.4 = (f32[2,8,32,128]{3,2,1,0:T(8,128)S(1)}, f32[2,8,32,128]{3,2,1,0:T(8,128)}, u32[]{:S(2)}) copy-start(f32[2,8,32,128]{3,2,1,0:T(8,128)} %get-tuple-element.25.refs_0_.a) | copy-start | bytes 786436
  23.7 14.7 %copy-start.5 = (f32[2,8,32,128]{3,2,1,0:T(8,128)S(1)}, f32[2,8,32,128]{3,2,1,0:T(8,128)}, u32[]{:S(2)}) copy-start(f32[2,8,32,128]{3,2,1,0:T(8,128)} %get-tuple-element.25.refs_0_.a) | copy-start | bytes 786436
  23.8 14.8 %copy-start.7 = (s32[3]{0:T(128)S(1)}, s32[3]{0:T(128)}, u32[]{:S(2)}) copy-start(s32[3]{0:T(128)} %pad_add_fusion.info.refs_0_) | copy-start | bytes 40
  23.8 14.7 %collective-permute-start.7 = (f32[2,8,32,128]{3,2,1,0:T(8,128)S(1)}, f32[2,8,32,128]{3,2,1,0:T(8,128)S(1)}, u32[]{:S(2)}, u32[]{:S(2)}) collective-permute-start(f32[2,8,32,128]{3,2,1,0:T(8,128)S(1)} %shard_map.77.refs_0_.a), channel_id=1, source_target_pairs={{0,4},{1,5},{2,6},{3,7},{4,0},{5,1},{6,2},{7,3},{8,12},{9,13},{10,... | collective-permute-start | bytes 786440 | tf_op jit(solution)/shard_map/ppermute | solution.py:211
  39.1 2.8 %collective-permute-start.8 = (f32[8,32,128]{2,1,0:T(8,128)S(1)}, f32[8,32,128]{2,1,0:T(8,128)S(1)}, u32[]{:S(2)}, u32[]{:S(2)}) collective-permute-start(f32[8,32,128]{2,1,0:T(8,128)S(1)} %shard_map.79.refs_6_), channel_id=1, source_target_pairs={{0,8},{8,0},{1,9},{9,1},{2,10},{10,2},{3,11},{11,3},{4,12},{12,4},... | collective-permute-start | bytes 393224 | tf_op jit(solution)/shard_map/ppermute | solution.py:249
  39.2 15.3 %collective-permute-start.6 = (f32[2,8,32,128]{3,2,1,0:T(8,128)S(1)}, f32[2,8,32,128]{3,2,1,0:T(8,128)S(1)}, u32[]{:S(2)}, u32[]{:S(2)}) collective-permute-start(f32[2,8,32,128]{3,2,1,0:T(8,128)S(1)} %shard_map.78.refs_0_.a), channel_id=1, source_target_pairs={{0,4},{1,5},{2,6},{3,7},{4,0},{5,1},{6,2},{7,3},{8,12},{9,13},{10,... | collective-permute-start | bytes 786440 | tf_op jit(solution)/shard_map/ppermute | solution.py:211
  42.7 13.8 %collective-permute-start.10 = (f32[2,8,32,128]{3,2,1,0:T(8,128)S(1)}, f32[2,8,32,128]{3,2,1,0:T(8,128)S(1)}, u32[]{:S(2)}, u32[]{:S(2)}) collective-permute-start(f32[2,8,32,128]{3,2,1,0:T(8,128)S(1)} %get-tuple-element.33), channel_id=1, source_target_pairs={{0,1},{1,0},{2,3},{3,2},{4,5},{5,4},{6,7},{7,6},{8,9},{9,8},{10,11... | collective-permute-start | bytes 786440 | tf_op jit(solution)/shard_map/ppermute | solution.py:211
  43.3 13.3 %collective-permute-start.11 = (f32[2,8,32,128]{3,2,1,0:T(8,128)S(1)}, f32[2,8,32,128]{3,2,1,0:T(8,128)S(1)}, u32[]{:S(2)}, u32[]{:S(2)}) collective-permute-start(f32[2,8,32,128]{3,2,1,0:T(8,128)S(1)} %get-tuple-element.34), channel_id=1, source_target_pairs={{0,2},{1,3},{2,0},{3,1},{4,6},{5,7},{6,4},{7,5},{8,10},{9,11},{10,... | collective-permute-start | bytes 786440 | tf_op jit(solution)/shard_map/ppermute | solution.py:211
  46.0 16.5 %collective-permute-start.12 = (f32[2,8,32,128]{3,2,1,0:T(8,128)S(1)}, f32[2,8,32,128]{3,2,1,0:T(8,128)S(1)}, u32[]{:S(2)}, u32[]{:S(2)}) collective-permute-start(f32[2,8,32,128]{3,2,1,0:T(8,128)S(1)} %get-tuple-element.35), channel_id=1, source_target_pairs={{0,3},{1,2},{2,1},{3,0},{4,7},{5,6},{6,5},{7,4},{8,11},{9,10},{10,... | collective-permute-start | bytes 786440 | tf_op jit(solution)/shard_map/ppermute | solution.py:211
  54.5 12.4 %copy-start.3 = (bf16[192,2048]{1,0:T(8,128)(2,1)S(1)}, bf16[192,2048]{1,0:T(8,128)(2,1)}, u32[]{:S(2)}) copy-start(bf16[192,2048]{1,0:T(8,128)(2,1)} %g.7) | copy-start | bytes 2359300
  55.1 11.8 %copy-start = (bf16[192,2048]{1,0:T(8,128)(2,1)S(1)}, bf16[192,2048]{1,0:T(8,128)(2,1)}, u32[]{:S(2)}) copy-start(bf16[192,2048]{1,0:T(8,128)(2,1)} %q.7) | copy-start | bytes 2359300
  55.1 11.8 %copy-start.1 = (bf16[192,2048]{1,0:T(8,128)(2,1)S(1)}, bf16[192,2048]{1,0:T(8,128)(2,1)}, u32[]{:S(2)}) copy-start(bf16[192,2048]{1,0:T(8,128)(2,1)} %k.7) | copy-start | bytes 2359300
  55.1 11.8 %copy-start.2 = (bf16[192,2048]{1,0:T(8,128)(2,1)S(1)}, bf16[192,2048]{1,0:T(8,128)(2,1)}, u32[]{:S(2)}) copy-start(bf16[192,2048]{1,0:T(8,128)(2,1)} %v.7) | copy-start | bytes 2359300
  55.1 1.4 %collective-permute-start.9 = (f32[8,32,128]{2,1,0:T(8,128)S(1)}, f32[8,32,128]{2,1,0:T(8,128)S(1)}, u32[]{:S(2)}, u32[]{:S(2)}) collective-permute-start(f32[8,32,128]{2,1,0:T(8,128)S(1)} %shard_map.81.refs_6_), channel_id=1, source_target_pairs={{0,8},{8,0},{1,9},{9,1},{2,10},{10,2},{3,11},{11,3},{4,12},{12,4},... | collective-permute-start | bytes 393224 | tf_op jit(solution)/shard_map/ppermute | solution.py:249
  63.4 8.4 %collective-permute-start.13 = (f32[2,8,32,128]{3,2,1,0:T(8,128)S(1)}, f32[2,8,32,128]{3,2,1,0:T(8,128)S(1)}, u32[]{:S(2)}, u32[]{:S(2)}) collective-permute-start(f32[2,8,32,128]{3,2,1,0:T(8,128)S(1)} %get-tuple-element.37), channel_id=1, source_target_pairs={{0,1},{1,0},{2,3},{3,2},{4,5},{5,4},{6,7},{7,6},{8,9},{9,8},{10,11... | collective-permute-start | bytes 786440 | tf_op jit(solution)/shard_map/ppermute | solution.py:211
  63.8 9.2 %collective-permute-start.14 = (f32[2,8,32,128]{3,2,1,0:T(8,128)S(1)}, f32[2,8,32,128]{3,2,1,0:T(8,128)S(1)}, u32[]{:S(2)}, u32[]{:S(2)}) collective-permute-start(f32[2,8,32,128]{3,2,1,0:T(8,128)S(1)} %get-tuple-element.38), channel_id=1, source_target_pairs={{0,2},{1,3},{2,0},{3,1},{4,6},{5,7},{6,4},{7,5},{8,10},{9,11},{10,... | collective-permute-start | bytes 786440 | tf_op jit(solution)/shard_map/ppermute | solution.py:211
  64.2 13.3 %collective-permute-start.15 = (f32[2,8,32,128]{3,2,1,0:T(8,128)S(1)}, f32[2,8,32,128]{3,2,1,0:T(8,128)S(1)}, u32[]{:S(2)}, u32[]{:S(2)}) collective-permute-start(f32[2,8,32,128]{3,2,1,0:T(8,128)S(1)} %get-tuple-element.39), channel_id=1, source_target_pairs={{0,3},{1,2},{2,1},{3,0},{4,7},{5,6},{6,5},{7,4},{8,11},{9,10},{10,... | collective-permute-start | bytes 786440 | tf_op jit(solution)/shard_map/ppermute | solution.py:211

commit v3 on v2

--- a/solution.py
+++ b/solution.py
@@ -18,11 +18,11 @@
     ("state", 0),
     ("state", 1),
     ("sum", 0),
+    ("offer", 0),
     ("sum", 1),
-    ("half", 0),
+    ("offer", 1),
     ("spread", 0),
-    ("half", 1),
-    ("spread", 1, (0, 1), (0, 2), (0, 3)),
+    ("spread", 1),
     ("finish", 0),
     ("finish", 1),
 )
@@ -32,7 +32,6 @@
 VMEM_LIMIT = 40 * 1024 * 1024
 STATE_LIMIT = 60 * 1024 * 1024
 
-LIGHT = pl.CostEstimate(flops=1, bytes_accessed=1, transcendentals=0)
 SCALARS = pl.BlockSpec(memory_space=pltpu.SMEM)
 WHOLE = pl.BlockSpec(memory_space=pltpu.VMEM)
 FAR = pl.BlockSpec(memory_space=pltpu.HBM)
@@ -87,55 +86,56 @@
             pltpu.SemaphoreType.DMA((-(-heads // STEP), 4)),
         ],
         compiler_params=pltpu.CompilerParams(vmem_limit_bytes=STATE_LIMIT),
-        cost_estimate=LIGHT,
     )(info, *arrays, *behind)
 
 
-def sum_kernel(a, b, c, d, *refs):
-    refs[-1][...] = (a[...] + b[...]) + (c[...] + d[...])
-
-
-def block_sum(pieces, behind):
-    shape = jax.ShapeDtypeStruct(pieces[0].shape, F32)
-    return pl.pallas_call(
-        sum_kernel,
-        out_shape=shape,
-        in_specs=[WHOLE] * PARTS + [LEFT] * len(behind),
-        out_specs=WHOLE,
-        compiler_params=pltpu.CompilerParams(vmem_limit_bytes=VMEM_LIMIT),
-        cost_estimate=LIGHT,
-    )(*pieces, *behind)
-
-
-def across_kernel(info, a, b, *refs):
-    take = jnp.where(info[1] > 0, 1, 0)
-    refs[-1][...] = a[take] + b[take]
-
-
-def half_total(info, total, other, behind):
-    shape = jax.ShapeDtypeStruct(total.shape[1:], F32)
-    return pl.pallas_call(
-        across_kernel,
-        out_shape=shape,
+def add_kernel(info, a, b, c, d, *refs):
+    total, halves = refs[-2:]
+    total[...] = (a[...] + b[...]) + (c[...] + d[...])
+    halves[...] = total[info[1]]
+
+
+def block_sum(info, pieces, behind):
+    shape = pieces[0].shape
+    return pl.pallas_call(
+        add_kernel,
+        out_shape=[jax.ShapeDtypeStruct(shape, F32), jax.ShapeDtypeStruct(shape[1:], F32)],
+        in_specs=[SCALARS] + [WHOLE] * PARTS + [LEFT] * len(behind),
+        out_specs=[WHOLE] * 2,
+        compiler_params=pltpu.CompilerParams(vmem_limit_bytes=VMEM_LIMIT),
+    )(info, *pieces, *behind)
+
+
+def offer_kernel(info, total, across, *refs):
+    out = refs[-1]
+    upper = info[2] > 0
+    whole = 1 - info[1]
+    other = info[1]
+    send = jnp.logical_xor(upper, whole == 0)
+    out[other] = total[other]
+    out[whole] = across[...] + jnp.where(send, total[whole], 0.0)
+
+
+def offer(info, total, across, behind):
+    return pl.pallas_call(
+        offer_kernel,
+        out_shape=jax.ShapeDtypeStruct(total.shape, F32),
         in_specs=[SCALARS, WHOLE, WHOLE] + [LEFT] * len(behind),
         out_specs=WHOLE,
         compiler_params=pltpu.CompilerParams(vmem_limit_bytes=VMEM_LIMIT),
-        cost_estimate=LIGHT,
-    )(info, total, other, *behind)
-
-
-def spread_kernel(levels, info, *refs):
-    pieces = refs[:PARTS]
-    totals = refs[PARTS : PARTS + levels]
-    across = refs[PARTS + levels]
-    outs = refs[-PARTS:]
-    mine, node, block = info[0], info[1], info[2]
-    prefix = jnp.where(node > 0, across[...], 0.0)
-    suffix = jnp.where(node > 0, 0.0, across[...])
-    for level in range(levels):
-        upper = ((block >> level) & 1) > 0
-        prefix = prefix + jnp.where(upper, totals[level][0], 0.0)
-        suffix = suffix + jnp.where(upper, 0.0, totals[level][1])
+    )(info, total, across, *behind)
+
+
+def spread_kernel(pair, info, *refs):
+    pieces, given, outs = refs[:PARTS], refs[PARTS : PARTS + 1 + pair], refs[-PARTS:]
+    mine, node, upper = info[0], info[1], info[2] > 0
+    if pair:
+        across, other = given
+        late = node > 0
+        prefix = jnp.where(late, across[...], 0.0) + jnp.where(late | upper, other[0], 0.0)
+        suffix = jnp.where(late, 0.0, across[...]) + jnp.where(late & upper, 0.0, other[1])
+    else:
+        prefix, suffix = given[0][0], given[0][1]
     for r in range(PARTS):
         before, after = prefix, suffix
         for other in range(PARTS):
@@ -147,17 +147,27 @@
         outs[r][1] = after
 
 
-def spread(info, pieces, totals, across, behind):
-    levels = len(totals)
-    shapes = [jax.ShapeDtypeStruct(pieces[0].shape, F32)] * PARTS
-    return pl.pallas_call(
-        functools.partial(spread_kernel, levels),
-        out_shape=shapes,
-        in_specs=[SCALARS] + [WHOLE] * (PARTS + levels + 1) + [LEFT] * len(behind),
+def spread(info, pieces, given, behind):
+    return pl.pallas_call(
+        functools.partial(spread_kernel, len(given) > 1),
+        out_shape=[jax.ShapeDtypeStruct(pieces[0].shape, F32)] * PARTS,
+        in_specs=[SCALARS] + [WHOLE] * (PARTS + len(given)) + [LEFT] * len(behind),
         out_specs=[WHOLE] * PARTS,
         compiler_params=pltpu.CompilerParams(vmem_limit_bytes=VMEM_LIMIT),
-        cost_estimate=LIGHT,
-    )(info, *pieces, *totals, across, *behind)
+    )(info, *pieces, *given, *behind)
+
+
+def sums_outside(total, node, block, blocks):
+    everything = lax.all_gather(total, ("node", "local"))
+    everything = everything.reshape(-1, blocks, PARTS, *total.shape)
+    everything = lax.dynamic_index_in_dim(everything, lax.axis_index("local") % PARTS, 2, False)
+    everything = everything.reshape(-1, *total.shape)
+    at = node * blocks + block
+    earlier = (jnp.arange(everything.shape[0]) < at)[:, None, None, None]
+    later = (jnp.arange(everything.shape[0]) > at)[:, None, None, None]
+    prefix = jnp.sum(jnp.where(earlier, everything[:, 0], 0.0), axis=0)
+    suffix = jnp.sum(jnp.where(later, everything[:, 1], 0.0), axis=0)
+    return jnp.stack([prefix, suffix])
 
 
 def finish_kernel(step, factor, info, q, k, v, g, *refs):
@@ -203,7 +213,6 @@
         ),
         input_output_aliases={fixed + i: i for i in range(len(outs))},
         compiler_params=pltpu.CompilerParams(vmem_limit_bytes=VMEM_LIMIT),
-        cost_estimate=LIGHT,
     )(*given)
 
 
@@ -217,43 +226,41 @@
     heads = width // HEAD_DIM
     size, nodes = lax.axis_size("local"), lax.axis_size("node")
     blocks = size // PARTS
-    levels = blocks.bit_length() - 1
-    assert nodes == 2 and PARTS << levels == size and sum(CHUNKS) == heads
+    assert nodes == 2 and size % PARTS == 0 and sum(CHUNKS) == heads
     factor = 1.0 / math.sqrt(HEAD_DIM * rows * nodes * size)
     node, place_in = lax.axis_index("node"), lax.axis_index("local")
     info = jnp.stack([place_in % PARTS, node, place_in // PARTS]).astype(jnp.int32)
 
     firsts = [sum(CHUNKS[:i]) for i in range(len(CHUNKS))]
-    done = {}
+    pieces, given, ready, state = {}, {}, {}, {}
     outs = ()
     last = info
-    for stage, i, *after in ORDER:
+    for stage, i in ORDER:
         first, count = firsts[i], CHUNKS[i]
-        behind = [last] + [done["ready", j][r] for j, r in after]
+        behind = [last]
         if stage == "state":
             own = states(info, arrays, first, count, behind)
             last = own[0]
             got = {r: swap(own[r], size, r) for r in (1, 3, 2)}
-            done["pieces", i] = [own[0], got[1], got[2], got[3]]
+            pieces[i] = [own[0], got[1], got[2], got[3]]
         elif stage == "sum":
-            last = total = block_sum(done["pieces", i], behind)
-            totals = []
-            for level in range(levels):
-                if level:
-                    total = total + totals[-1]
-                totals.append(swap(total, size, PARTS << level))
-            done["totals", i] = total, totals
-        elif stage == "half":
-            total, totals = done["totals", i]
-            last = half_total(info, total, totals[-1], behind)
-            done["across", i] = lax.ppermute(last, "node", [(0, 1), (1, 0)])
+            last, halves = block_sum(info, pieces[i], behind)
+            across = lax.ppermute(halves, "node", [(0, 1), (1, 0)])
+            state[i] = last, across
+        elif stage == "offer":
+            total, across = state[i]
+            if blocks == 2:
+                last = offer(info, total, across, behind)
+                given[i] = [across, swap(last, size, PARTS)]
+            else:
+                given[i] = [sums_outside(total, node, place_in // PARTS, blocks)]
         elif stage == "spread":
-            ready = spread(info, done["pieces", i], done["totals", i][1], done["across", i], behind)
-            last = ready[0]
-            back = {r: swap(ready[r], size, r) for r in (1, 3, 2)}
-            done["ready", i] = [ready[0], back[1], back[2], back[3]]
+            own = spread(info, pieces[i], given[i], behind)
+            last = own[0]
+            got = {r: swap(own[r], size, r) for r in (1, 3, 2)}
+            ready[i] = [own[0], got[1], got[2], got[3]]
         else:
-            outs = finish(info, arrays, done["ready", i], outs, first, FINISH_STEP[i], factor, behind)
+            outs = finish(info, arrays, ready[i], outs, first, FINISH_STEP[i], factor, behind)
     return tuple(outs)
 
 

time: 82.1 us -> 78.6 us (0.957)
  waiting for transfers between devices: 38.3 us -> 28.9 us
  starting transfers between devices: 21.6 us -> 26.6 us
  Pallas kernels: 19.6 us -> 20.7 us
    ppermute x14, waiting for transfers between devices: 37 us -> 26.2 us  [swap(): return lax.ppermute(array, 'local', [(i, i ^ mask) for i in range(size)])]
    ppermute x14, starting transfers between devices: 21.4 us -> 26.4 us  [swap(): return lax.ppermute(array, 'local', [(i, i ^ mask) for i in range(size)])]
    ppermute x2, waiting for transfers between devices: 1.34 us -> 2.67 us  [local(): across = lax.ppermute(halves, 'node', [(0, 1), (1, 0)])]
    pallas_call x6, Pallas kernels: 2.97 us -> 4.1 us  [the longest x2 1.73 us: spread(): pl.pallas_call(functools.partial(spread_kernel, len(given) > 1), out_shap...]
  transfers between devices with their start and end apart: 16 -> 16, of which waited for: 9 -> 8; matrix products, arithmetic and copies ran while one was open for 0% -> 0% of each run, Pallas kernels for 12% -> 16%
where the time goes in v3:
time: 78.6 us; the launch traced here: 78.4 us
  waiting for transfers between devices  28.9 us (37%)
  starting transfers between devices  26.6 us (34%)
  Pallas kernels  20.7 us (26%)
  local copies, waits for them, and re-layouts  0.98 us (1%)
    ppermute x14, starting transfers between devices, swap(): return lax.ppermute(array, 'local', [(i, i ^ mask) for i in range(size)])  26.4 us
    ppermute x14, waiting for transfers between devices, swap(): return lax.ppermute(array, 'local', [(i, i ^ mask) for i in range(size)])  26.2 us
    pallas_call x2, Pallas kernels, finish(): pl.pallas_call(functools.partial(finish_kernel, step, factor), out_shape=...  8.73 us
    pallas_call x2, Pallas kernels, states(): pl.pallas_call(functools.partial(state_kernel, first, heads), out_shape=[...  7.85 us
    ppermute x2, waiting for transfers between devices, local(): across = lax.ppermute(halves, 'node', [(0, 1), (1, 0)])  2.67 us
    pallas_call x2, Pallas kernels, spread(): pl.pallas_call(functools.partial(spread_kernel, len(given) > 1), out_shap...  1.73 us
  transfers between devices with their start and end apart: 16, of which 8 were waited for; matrix products, arithmetic and copies ran while one was open for 0% of the time, Pallas kernels for 16%

profile of v3, /device:TPU:0, one launch (start us, length us, event | category | flops | bytes accessed | tf_op | source)
XLA Modules:
  0.0 78.4 jit_solution(16429543780469713719)
XLA Ops:
  0.7 0.6 pad_add_fusion.info.refs_0_
  1.2 3.8 %shard_map.75 = (f32[2,8,32,128]{3,2,1,0:T(8,128)}, f32[2,8,32,128]{3,2,1,0:T(8,128)}, f32[2,8,32,128]{3,2,1,0:T(8,128)}, f32[2,8,32,128]{3,2,1,0:T(8,128)}) custom-call(s32[3]{0:T(128)} %pad_add_fusion.info.refs_0_, bf16[192,2048]{1,0:T(8,128)(2,1)} %q.7, bf16[192,2048]{1,0:T(8,128)(2,1)} %k.7, bf16[192,2048]{1,0:T(8,128)(2,1)} %v.7, bf16[192,2048]{1,0:T(8,128)(2,1)} %g.7, ...), custom_call_target="tpu_custom_call" | custom-call | tf_op jit(solution)/shard_map/pallas_call | solution.py:78
  5.1 3.0 %collective-permute-start.3 = (f32[2,8,32,128]{3,2,1,0:T(8,128)}, f32[2,8,32,128]{3,2,1,0:T(8,128)S(1)}, u32[]{:S(2)}, u32[]{:S(2)}) collective-permute-start(f32[2,8,32,128]{3,2,1,0:T(8,128)} %get-tuple-element.33), channel_id=1, source_target_pairs={{0,1},{1,0},{2,3},{3,2},{4,5},{5,4},{6,7},{7,6},{8,9},{9,8},{10,11... | collective-permute-start | bytes 786440 | tf_op jit(solution)/shard_map/ppermute | solution.py:220
  8.1 1.6 %collective-permute-start.4 = (f32[2,8,32,128]{3,2,1,0:T(8,128)}, f32[2,8,32,128]{3,2,1,0:T(8,128)S(1)}, u32[]{:S(2)}, u32[]{:S(2)}) collective-permute-start(f32[2,8,32,128]{3,2,1,0:T(8,128)} %get-tuple-element.34), channel_id=1, source_target_pairs={{0,2},{1,3},{2,0},{3,1},{4,6},{5,7},{6,4},{7,5},{8,10},{9,11},{10,... | collective-permute-start | bytes 786440 | tf_op jit(solution)/shard_map/ppermute | solution.py:220
  9.7 0.0 collective-permute-start.5
  9.7 0.0 copy-start.6
  9.7 4.0 %shard_map.76 = (f32[2,8,32,128]{3,2,1,0:T(8,128)}, f32[2,8,32,128]{3,2,1,0:T(8,128)}, f32[2,8,32,128]{3,2,1,0:T(8,128)}, f32[2,8,32,128]{3,2,1,0:T(8,128)}) custom-call(s32[3]{0:T(128)} %pad_add_fusion.info.refs_0_, bf16[192,2048]{1,0:T(8,128)(2,1)} %q.7, bf16[192,2048]{1,0:T(8,128)(2,1)} %k.7, bf16[192,2048]{1,0:T(8,128)(2,1)} %v.7, bf16[192,2048]{1,0:T(8,128)(2,1)} %g.7, ...), custom_call_target="tpu_custom_call" | custom-call | tf_op jit(solution)/shard_map/pallas_call | solution.py:78
  13.7 2.0 %collective-permute-start = (f32[2,8,32,128]{3,2,1,0:T(8,128)}, f32[2,8,32,128]{3,2,1,0:T(8,128)S(1)}, u32[]{:S(2)}, u32[]{:S(2)}) collective-permute-start(f32[2,8,32,128]{3,2,1,0:T(8,128)} %get-tuple-element.30), channel_id=1, source_target_pairs={{0,1},{1,0},{2,3},{3,2},{4,5},{5,4},{6,7},{7,6},{8,9},{9,8},{10,11... | collective-permute-start | bytes 786440 | tf_op jit(solution)/shard_map/ppermute | solution.py:220
  15.7 1.6 %collective-permute-start.1 = (f32[2,8,32,128]{3,2,1,0:T(8,128)}, f32[2,8,32,128]{3,2,1,0:T(8,128)S(1)}, u32[]{:S(2)}, u32[]{:S(2)}) collective-permute-start(f32[2,8,32,128]{3,2,1,0:T(8,128)} %get-tuple-element.31), channel_id=1, source_target_pairs={{0,2},{1,3},{2,0},{3,1},{4,6},{5,7},{6,4},{7,5},{8,10},{9,11},{10,... | collective-permute-start | bytes 786440 | tf_op jit(solution)/shard_map/ppermute | solution.py:220
  17.3 0.0 collective-permute-done.3.b.refs_1_
  17.3 0.0 copy-start.7
  17.3 0.4 collective-permute-start.2
  17.7 0.0 collective-permute-done.4.c.refs_2_
  17.7 5.0 %collective-permute-done.5.d.refs_3_ = f32[2,8,32,128]{3,2,1,0:T(8,128)S(1)} collective-permute-done((f32[2,8,32,128]{3,2,1,0:T(8,128)}, f32[2,8,32,128]{3,2,1,0:T(8,128)S(1)}, u32[]{:S(2)}, u32[]{:S(2)}) %collective-permute-start.5) | collective-permute-done | bytes 262176 | tf_op jit(solution)/shard_map/ppermute | solution.py:220
  22.7 0.0 copy-done.6
  22.7 0.0 copy-done.7
  22.7 0.0 copy-start.4
  22.7 0.9 %copy-done.4 = f32[2,8,32,128]{3,2,1,0:T(8,128)S(1)} copy-done((f32[2,8,32,128]{3,2,1,0:T(8,128)S(1)}, f32[2,8,32,128]{3,2,1,0:T(8,128)}, u32[]{:S(2)}) %copy-start.4) | copy-done | bytes 262168
  23.7 0.6 shard_map.77
  24.3 0.1 collective-permute-start.6
  24.4 1.3 %collective-permute-done.6.across.refs_4_ = f32[8,32,128]{2,1,0:T(8,128)S(1)} collective-permute-done((f32[8,32,128]{2,1,0:T(8,128)S(1)}, f32[8,32,128]{2,1,0:T(8,128)S(1)}, u32[]{:S(2)}, u32[]{:S(2)}) %collective-permute-start.6) | collective-permute-done | bytes 131104 | tf_op jit(solution)/shard_map/ppermute | solution.py:248
  25.7 0.0 copy-start.5
  25.7 0.6 shard_map.78.refs_0_
  26.3 3.1 %collective-permute-start.9 = (f32[2,8,32,128]{3,2,1,0:T(8,128)S(1)}, f32[2,8,32,128]{3,2,1,0:T(8,128)S(1)}, u32[]{:S(2)}, u32[]{:S(2)}) collective-permute-start(f32[2,8,32,128]{3,2,1,0:T(8,128)S(1)} %shard_map.78.refs_0_), channel_id=1, source_target_pairs={{0,4},{1,5},{2,6},{3,7},{4,0},{5,1},{6,2},{7,3},{8,12},{9,13},{10,... | collective-permute-start | bytes 786440 | tf_op jit(solution)/shard_map/ppermute | solution.py:220
  29.4 0.0 collective-permute-done.b.refs_1_
  29.4 0.0 collective-permute-done.1.c.refs_2_
  29.4 6.8 %collective-permute-done.2.d.refs_3_ = f32[2,8,32,128]{3,2,1,0:T(8,128)S(1)} collective-permute-done((f32[2,8,32,128]{3,2,1,0:T(8,128)}, f32[2,8,32,128]{3,2,1,0:T(8,128)S(1)}, u32[]{:S(2)}, u32[]{:S(2)}) %collective-permute-start.2) | collective-permute-done | bytes 262176 | tf_op jit(solution)/shard_map/ppermute | solution.py:220
  36.2 0.0 copy-done.5
  36.2 0.6 shard_map.79
  36.8 0.1 collective-permute-start.7
  36.9 1.3 %collective-permute-done.7.across.refs_4_ = f32[8,32,128]{2,1,0:T(8,128)S(1)} collective-permute-done((f32[8,32,128]{2,1,0:T(8,128)S(1)}, f32[8,32,128]{2,1,0:T(8,128)S(1)}, u32[]{:S(2)}, u32[]{:S(2)}) %collective-permute-start.7) | collective-permute-done | bytes 131104 | tf_op jit(solution)/shard_map/ppermute | solution.py:248
  38.2 0.6 shard_map.80.refs_6_
  38.8 1.1 %collective-permute-start.8 = (f32[2,8,32,128]{3,2,1,0:T(8,128)S(1)}, f32[2,8,32,128]{3,2,1,0:T(8,128)S(1)}, u32[]{:S(2)}, u32[]{:S(2)}) collective-permute-start(f32[2,8,32,128]{3,2,1,0:T(8,128)S(1)} %shard_map.80.refs_6_), channel_id=1, source_target_pairs={{0,4},{1,5},{2,6},{3,7},{4,0},{5,1},{6,2},{7,3},{8,12},{9,13},{10,... | collective-permute-start | bytes 786440 | tf_op jit(solution)/shard_map/ppermute | solution.py:220
  39.9 1.8 %collective-permute-done.9.refs_5_ = f32[2,8,32,128]{3,2,1,0:T(8,128)S(1)} collective-permute-done((f32[2,8,32,128]{3,2,1,0:T(8,128)S(1)}, f32[2,8,32,128]{3,2,1,0:T(8,128)S(1)}, u32[]{:S(2)}, u32[]{:S(2)}) %collective-permute-start.9) | collective-permute-done | bytes 262176 | tf_op jit(solution)/shard_map/ppermute | solution.py:220
  41.7 0.0 copy-start.2
  41.7 0.0 copy-start.3
  41.7 0.9 %shard_map.81 = (f32[2,8,32,128]{3,2,1,0:T(8,128)S(1)}, f32[2,8,32,128]{3,2,1,0:T(8,128)S(1)}, f32[2,8,32,128]{3,2,1,0:T(8,128)S(1)}, f32[2,8,32,128]{3,2,1,0:T(8,128)S(1)}) custom-call(s32[3]{0:T(128)S(1)} %copy-done.7, f32[2,8,32,128]{3,2,1,0:T(8,128)S(1)} %copy-done.6, f32[2,8,32,128]{3,2,1,0:T(8,128)S(1)} %collective-permute-done.3.b.refs_1_, ...), custom_call_target="tpu_custom_call" | custom-call | tf_op jit(solution)/shard_map/pallas_call | solution.py:151
  42.5 1.6 %collective-permute-start.13 = (f32[2,8,32,128]{3,2,1,0:T(8,128)S(1)}, f32[2,8,32,128]{3,2,1,0:T(8,128)S(1)}, u32[]{:S(2)}, u32[]{:S(2)}) collective-permute-start(f32[2,8,32,128]{3,2,1,0:T(8,128)S(1)} %get-tuple-element.45), channel_id=1, source_target_pairs={{0,1},{1,0},{2,3},{3,2},{4,5},{5,4},{6,7},{7,6},{8,9},{9,8},{10,11... | collective-permute-start | bytes 786440 | tf_op jit(solution)/shard_map/ppermute | solution.py:220
  44.2 5.7 %collective-permute-start.14 = (f32[2,8,32,128]{3,2,1,0:T(8,128)S(1)}, f32[2,8,32,128]{3,2,1,0:T(8,128)S(1)}, u32[]{:S(2)}, u32[]{:S(2)}) collective-permute-start(f32[2,8,32,128]{3,2,1,0:T(8,128)S(1)} %get-tuple-element.46), channel_id=1, source_target_pairs={{0,2},{1,3},{2,0},{3,1},{4,6},{5,7},{6,4},{7,5},{8,10},{9,11},{10,... | collective-permute-start | bytes 786440 | tf_op jit(solution)/shard_map/ppermute | solution.py:220
  49.9 1.4 %collective-permute-start.15 = (f32[2,8,32,128]{3,2,1,0:T(8,128)S(1)}, f32[2,8,32,128]{3,2,1,0:T(8,128)S(1)}, u32[]{:S(2)}, u32[]{:S(2)}) collective-permute-start(f32[2,8,32,128]{3,2,1,0:T(8,128)S(1)} %get-tuple-element.47), channel_id=1, source_target_pairs={{0,3},{1,2},{2,1},{3,0},{4,7},{5,6},{6,5},{7,4},{8,11},{9,10},{10,... | collective-permute-start | bytes 786440 | tf_op jit(solution)/shard_map/ppermute | solution.py:220
  51.3 2.5 %collective-permute-done.8.refs_5_ = f32[2,8,32,128]{3,2,1,0:T(8,128)S(1)} collective-permute-done((f32[2,8,32,128]{3,2,1,0:T(8,128)S(1)}, f32[2,8,32,128]{3,2,1,0:T(8,128)S(1)}, u32[]{:S(2)}, u32[]{:S(2)}) %collective-permute-start.8) | collective-permute-done | bytes 262176 | tf_op jit(solution)/shard_map/ppermute | solution.py:220
  53.8 0.0 copy-start
  53.8 0.0 copy-start.1
  53.8 0.9 %shard_map.82 = (f32[2,8,32,128]{3,2,1,0:T(8,128)S(1)}, f32[2,8,32,128]{3,2,1,0:T(8,128)S(1)}, f32[2,8,32,128]{3,2,1,0:T(8,128)S(1)}, f32[2,8,32,128]{3,2,1,0:T(8,128)S(1)}) custom-call(s32[3]{0:T(128)S(1)} %copy-done.7, f32[2,8,32,128]{3,2,1,0:T(8,128)S(1)} %copy-done.5, f32[2,8,32,128]{3,2,1,0:T(8,128)S(1)} %collective-permute-done.b.refs_1_, ...), custom_call_target="tpu_custom_call" | custom-call | tf_op jit(solution)/shard_map/pallas_call | solution.py:151
  54.7 1.7 %collective-permute-start.10 = (f32[2,8,32,128]{3,2,1,0:T(8,128)S(1)}, f32[2,8,32,128]{3,2,1,0:T(8,128)S(1)}, u32[]{:S(2)}, u32[]{:S(2)}) collective-permute-start(f32[2,8,32,128]{3,2,1,0:T(8,128)S(1)} %get-tuple-element.42), channel_id=1, source_target_pairs={{0,1},{1,0},{2,3},{3,2},{4,5},{5,4},{6,7},{7,6},{8,9},{9,8},{10,11... | collective-permute-start | bytes 786440 | tf_op jit(solution)/shard_map/ppermute | solution.py:220
  56.4 0.0 collective-permute-start.11
  56.5 0.0 collective-permute-done.13.refs_1_
  56.5 3.1 %collective-permute-start.12 = (f32[2,8,32,128]{3,2,1,0:T(8,128)S(1)}, f32[2,8,32,128]{3,2,1,0:T(8,128)S(1)}, u32[]{:S(2)}, u32[]{:S(2)}) collective-permute-start(f32[2,8,32,128]{3,2,1,0:T(8,128)S(1)} %get-tuple-element.44), channel_id=1, source_target_pairs={{0,3},{1,2},{2,1},{3,0},{4,7},{5,6},{6,5},{7,4},{8,11},{9,10},{10,... | collective-permute-start | bytes 786440 | tf_op jit(solution)/shard_map/ppermute | solution.py:220
  59.6 0.0 collective-permute-done.14.refs_2_
  59.6 6.7 %collective-permute-done.15.refs_3_ = f32[2,8,32,128]{3,2,1,0:T(8,128)S(1)} collective-permute-done((f32[2,8,32,128]{3,2,1,0:T(8,128)S(1)}, f32[2,8,32,128]{3,2,1,0:T(8,128)S(1)}, u32[]{:S(2)}, u32[]{:S(2)}) %collective-permute-start.15) | collective-permute-done | bytes 262176 | tf_op jit(solution)/shard_map/ppermute | solution.py:220
  66.3 0.0 copy-done.2
  66.3 0.0 copy-done.3
  66.3 0.0 copy-done
  66.3 0.0 copy-done.1
  66.4 4.4 %shard_map.83 = (bf16[192,2048]{1,0:T(8,128)(2,1)}, bf16[192,2048]{1,0:T(8,128)(2,1)}, bf16[192,2048]{1,0:T(8,128)(2,1)}, bf16[192,2048]{1,0:T(8,128)(2,1)}) custom-call(s32[3]{0:T(128)S(1)} %copy-done.7, bf16[192,2048]{1,0:T(8,128)(2,1)S(1)} %copy-done, bf16[192,2048]{1,0:T(8,128)(2,1)S(1)} %copy-done.1, bf16[192,2048]{1,0:T(8,128)(2,1)S(1)} %copy-done.2, ...), custom_call_target="tpu_custom_call" | custom-call | tf_op jit(solution)/shard_map/pallas_call | solution.py:202
  70.7 0.0 collective-permute-done.10.refs_1_
  70.7 0.0 collective-permute-done.11.refs_2_
  70.7 3.3 %collective-permute-done.12.refs_3_ = f32[2,8,32,128]{3,2,1,0:T(8,128)S(1)} collective-permute-done((f32[2,8,32,128]{3,2,1,0:T(8,128)S(1)}, f32[2,8,32,128]{3,2,1,0:T(8,128)S(1)}, u32[]{:S(2)}, u32[]{:S(2)}) %collective-permute-start.12) | collective-permute-done | bytes 262176 | tf_op jit(solution)/shard_map/ppermute | solution.py:220
  74.1 4.4 %shard_map.84 = (bf16[192,2048]{1,0:T(8,128)(2,1)}, bf16[192,2048]{1,0:T(8,128)(2,1)}, bf16[192,2048]{1,0:T(8,128)(2,1)}, bf16[192,2048]{1,0:T(8,128)(2,1)}) custom-call(s32[3]{0:T(128)S(1)} %copy-done.7, bf16[192,2048]{1,0:T(8,128)(2,1)S(1)} %copy-done, ...), custom_call_target="tpu_custom_call", output_to_operand_aliasing={{0}: (9, {}), {1}: (10, {}), {2}: (11, {}), {3}: (12, {})} | custom-call | tf_op jit(solution)/shard_map/pallas_call | solution.py:202
Async XLA Ops:
  5.1 12.2 %collective-permute-start.3 = (f32[2,8,32,128]{3,2,1,0:T(8,128)}, f32[2,8,32,128]{3,2,1,0:T(8,128)S(1)}, u32[]{:S(2)}, u32[]{:S(2)}) collective-permute-start(f32[2,8,32,128]{3,2,1,0:T(8,128)} %get-tuple-element.33), channel_id=1, source_target_pairs={{0,1},{1,0},{2,3},{3,2},{4,5},{5,4},{6,7},{7,6},{8,9},{9,8},{10,11... | collective-permute-start | bytes 786440 | tf_op jit(solution)/shard_map/ppermute | solution.py:220
  8.1 9.6 %collective-permute-start.4 = (f32[2,8,32,128]{3,2,1,0:T(8,128)}, f32[2,8,32,128]{3,2,1,0:T(8,128)S(1)}, u32[]{:S(2)}, u32[]{:S(2)}) collective-permute-start(f32[2,8,32,128]{3,2,1,0:T(8,128)} %get-tuple-element.34), channel_id=1, source_target_pairs={{0,2},{1,3},{2,0},{3,1},{4,6},{5,7},{6,4},{7,5},{8,10},{9,11},{10,... | collective-permute-start | bytes 786440 | tf_op jit(solution)/shard_map/ppermute | solution.py:220
  9.7 13.0 %collective-permute-start.5 = (f32[2,8,32,128]{3,2,1,0:T(8,128)}, f32[2,8,32,128]{3,2,1,0:T(8,128)S(1)}, u32[]{:S(2)}, u32[]{:S(2)}) collective-permute-start(f32[2,8,32,128]{3,2,1,0:T(8,128)} %get-tuple-element.35), channel_id=1, source_target_pairs={{0,3},{1,2},{2,1},{3,0},{4,7},{5,6},{6,5},{7,4},{8,11},{9,10},{10,... | collective-permute-start | bytes 786440 | tf_op jit(solution)/shard_map/ppermute | solution.py:220
  9.7 13.0 %copy-start.6 = (f32[2,8,32,128]{3,2,1,0:T(8,128)S(1)}, f32[2,8,32,128]{3,2,1,0:T(8,128)}, u32[]{:S(2)}) copy-start(f32[2,8,32,128]{3,2,1,0:T(8,128)} %get-tuple-element.28.refs_0_.a) | copy-start | bytes 786436
  13.7 15.7 %collective-permute-start = (f32[2,8,32,128]{3,2,1,0:T(8,128)}, f32[2,8,32,128]{3,2,1,0:T(8,128)S(1)}, u32[]{:S(2)}, u32[]{:S(2)}) collective-permute-start(f32[2,8,32,128]{3,2,1,0:T(8,128)} %get-tuple-element.30), channel_id=1, source_target_pairs={{0,1},{1,0},{2,3},{3,2},{4,5},{5,4},{6,7},{7,6},{8,9},{9,8},{10,11... | collective-permute-start | bytes 786440 | tf_op jit(solution)/shard_map/ppermute | solution.py:220
  15.7 13.7 %collective-permute-start.1 = (f32[2,8,32,128]{3,2,1,0:T(8,128)}, f32[2,8,32,128]{3,2,1,0:T(8,128)S(1)}, u32[]{:S(2)}, u32[]{:S(2)}) collective-permute-start(f32[2,8,32,128]{3,2,1,0:T(8,128)} %get-tuple-element.31), channel_id=1, source_target_pairs={{0,2},{1,3},{2,0},{3,1},{4,6},{5,7},{6,4},{7,5},{8,10},{9,11},{10,... | collective-permute-start | bytes 786440 | tf_op jit(solution)/shard_map/ppermute | solution.py:220
  17.3 5.4 %copy-start.7 = (s32[3]{0:T(128)S(1)}, s32[3]{0:T(128)}, u32[]{:S(2)}) copy-start(s32[3]{0:T(128)} %pad_add_fusion.info.refs_0_) | copy-start | bytes 40
  17.3 18.9 %collective-permute-start.2 = (f32[2,8,32,128]{3,2,1,0:T(8,128)}, f32[2,8,32,128]{3,2,1,0:T(8,128)S(1)}, u32[]{:S(2)}, u32[]{:S(2)}) collective-permute-start(f32[2,8,32,128]{3,2,1,0:T(8,128)} %get-tuple-element.32), channel_id=1, source_target_pairs={{0,3},{1,2},{2,1},{3,0},{4,7},{5,6},{6,5},{7,4},{8,11},{9,10},{10,... | collective-permute-start | bytes 786440 | tf_op jit(solution)/shard_map/ppermute | solution.py:220
  22.7 1.0 %copy-start.4 = (f32[2,8,32,128]{3,2,1,0:T(8,128)S(1)}, f32[2,8,32,128]{3,2,1,0:T(8,128)}, u32[]{:S(2)}) copy-start(f32[2,8,32,128]{3,2,1,0:T(8,128)} %get-tuple-element.29.refs_0_.a) | copy-start | bytes 786436
  24.3 1.4 %collective-permute-start.6 = (f32[8,32,128]{2,1,0:T(8,128)S(1)}, f32[8,32,128]{2,1,0:T(8,128)S(1)}, u32[]{:S(2)}, u32[]{:S(2)}) collective-permute-start(f32[8,32,128]{2,1,0:T(8,128)S(1)} %get-tuple-element.37), channel_id=1, source_target_pairs={{0,8},{8,0},{1,9},{9,1},{2,10},{10,2},{3,11},{11,3},{4,12},{12,4},... | collective-permute-start | bytes 393224 | tf_op jit(solution)/shard_map/ppermute | solution.py:248
  25.7 10.5 %copy-start.5 = (f32[2,8,32,128]{3,2,1,0:T(8,128)S(1)}, f32[2,8,32,128]{3,2,1,0:T(8,128)}, u32[]{:S(2)}) copy-start(f32[2,8,32,128]{3,2,1,0:T(8,128)} %get-tuple-element.29.refs_0_.a) | copy-start | bytes 786436
  26.3 15.4 %collective-permute-start.9 = (f32[2,8,32,128]{3,2,1,0:T(8,128)S(1)}, f32[2,8,32,128]{3,2,1,0:T(8,128)S(1)}, u32[]{:S(2)}, u32[]{:S(2)}) collective-permute-start(f32[2,8,32,128]{3,2,1,0:T(8,128)S(1)} %shard_map.78.refs_0_), channel_id=1, source_target_pairs={{0,4},{1,5},{2,6},{3,7},{4,0},{5,1},{6,2},{7,3},{8,12},{9,13},{10,... | collective-permute-start | bytes 786440 | tf_op jit(solution)/shard_map/ppermute | solution.py:220
  36.8 1.4 %collective-permute-start.7 = (f32[8,32,128]{2,1,0:T(8,128)S(1)}, f32[8,32,128]{2,1,0:T(8,128)S(1)}, u32[]{:S(2)}, u32[]{:S(2)}) collective-permute-start(f32[8,32,128]{2,1,0:T(8,128)S(1)} %get-tuple-element.38), channel_id=1, source_target_pairs={{0,8},{8,0},{1,9},{9,1},{2,10},{10,2},{3,11},{11,3},{4,12},{12,4},... | collective-permute-start | bytes 393224 | tf_op jit(solution)/shard_map/ppermute | solution.py:248
  38.8 15.0 %collective-permute-start.8 = (f32[2,8,32,128]{3,2,1,0:T(8,128)S(1)}, f32[2,8,32,128]{3,2,1,0:T(8,128)S(1)}, u32[]{:S(2)}, u32[]{:S(2)}) collective-permute-start(f32[2,8,32,128]{3,2,1,0:T(8,128)S(1)} %shard_map.80.refs_6_), channel_id=1, source_target_pairs={{0,4},{1,5},{2,6},{3,7},{4,0},{5,1},{6,2},{7,3},{8,12},{9,13},{10,... | collective-permute-start | bytes 786440 | tf_op jit(solution)/shard_map/ppermute | solution.py:220
  41.7 24.7 %copy-start.2 = (bf16[192,2048]{1,0:T(8,128)(2,1)S(1)}, bf16[192,2048]{1,0:T(8,128)(2,1)}, u32[]{:S(2)}) copy-start(bf16[192,2048]{1,0:T(8,128)(2,1)} %v.7) | copy-start | bytes 2359300
  41.7 24.7 %copy-start.3 = (bf16[192,2048]{1,0:T(8,128)(2,1)S(1)}, bf16[192,2048]{1,0:T(8,128)(2,1)}, u32[]{:S(2)}) copy-start(bf16[192,2048]{1,0:T(8,128)(2,1)} %g.7) | copy-start | bytes 2359300
  42.5 13.9 %collective-permute-start.13 = (f32[2,8,32,128]{3,2,1,0:T(8,128)S(1)}, f32[2,8,32,128]{3,2,1,0:T(8,128)S(1)}, u32[]{:S(2)}, u32[]{:S(2)}) collective-permute-start(f32[2,8,32,128]{3,2,1,0:T(8,128)S(1)} %get-tuple-element.45), channel_id=1, source_target_pairs={{0,1},{1,0},{2,3},{3,2},{4,5},{5,4},{6,7},{7,6},{8,9},{9,8},{10,11... | collective-permute-start | bytes 786440 | tf_op jit(solution)/shard_map/ppermute | solution.py:220
  44.2 15.4 %collective-permute-start.14 = (f32[2,8,32,128]{3,2,1,0:T(8,128)S(1)}, f32[2,8,32,128]{3,2,1,0:T(8,128)S(1)}, u32[]{:S(2)}, u32[]{:S(2)}) collective-permute-start(f32[2,8,32,128]{3,2,1,0:T(8,128)S(1)} %get-tuple-element.46), channel_id=1, source_target_pairs={{0,2},{1,3},{2,0},{3,1},{4,6},{5,7},{6,4},{7,5},{8,10},{9,11},{10,... | collective-permute-start | bytes 786440 | tf_op jit(solution)/shard_map/ppermute | solution.py:220
  49.9 16.4 %collective-permute-start.15 = (f32[2,8,32,128]{3,2,1,0:T(8,128)S(1)}, f32[2,8,32,128]{3,2,1,0:T(8,128)S(1)}, u32[]{:S(2)}, u32[]{:S(2)}) collective-permute-start(f32[2,8,32,128]{3,2,1,0:T(8,128)S(1)} %get-tuple-element.47), channel_id=1, source_target_pairs={{0,3},{1,2},{2,1},{3,0},{4,7},{5,6},{6,5},{7,4},{8,11},{9,10},{10,... | collective-permute-start | bytes 786440 | tf_op jit(solution)/shard_map/ppermute | solution.py:220
  53.8 12.5 %copy-start = (bf16[192,2048]{1,0:T(8,128)(2,1)S(1)}, bf16[192,2048]{1,0:T(8,128)(2,1)}, u32[]{:S(2)}) copy-start(bf16[192,2048]{1,0:T(8,128)(2,1)} %q.7) | copy-start | bytes 2359300
  53.8 12.5 %copy-start.1 = (bf16[192,2048]{1,0:T(8,128)(2,1)S(1)}, bf16[192,2048]{1,0:T(8,128)(2,1)}, u32[]{:S(2)}) copy-start(bf16[192,2048]{1,0:T(8,128)(2,1)} %k.7) | copy-start | bytes 2359300
  54.7 16.0 %collective-permute-start.10 = (f32[2,8,32,128]{3,2,1,0:T(8,128)S(1)}, f32[2,8,32,128]{3,2,1,0:T(8,128)S(1)}, u32[]{:S(2)}, u32[]{:S(2)}) collective-permute-start(f32[2,8,32,128]{3,2,1,0:T(8,128)S(1)} %get-tuple-element.42), channel_id=1, source_target_pairs={{0,1},{1,0},{2,3},{3,2},{4,5},{5,4},{6,7},{7,6},{8,9},{9,8},{10,11... | collective-permute-start | bytes 786440 | tf_op jit(solution)/shard_map/ppermute | solution.py:220
  56.4 14.3 %collective-permute-start.11 = (f32[2,8,32,128]{3,2,1,0:T(8,128)S(1)}, f32[2,8,32,128]{3,2,1,0:T(8,128)S(1)}, u32[]{:S(2)}, u32[]{:S(2)}) collective-permute-start(f32[2,8,32,128]{3,2,1,0:T(8,128)S(1)} %get-tuple-element.43), channel_id=1, source_target_pairs={{0,2},{1,3},{2,0},{3,1},{4,6},{5,7},{6,4},{7,5},{8,10},{9,11},{10,... | collective-permute-start | bytes 786440 | tf_op jit(solution)/shard_map/ppermute | solution.py:220
  56.5 17.6 %collective-permute-start.12 = (f32[2,8,32,128]{3,2,1,0:T(8,128)S(1)}, f32[2,8,32,128]{3,2,1,0:T(8,128)S(1)}, u32[]{:S(2)}, u32[]{:S(2)}) collective-permute-start(f32[2,8,32,128]{3,2,1,0:T(8,128)S(1)} %get-tuple-element.44), channel_id=1, source_target_pairs={{0,3},{1,2},{2,1},{3,0},{4,7},{5,6},{6,5},{7,4},{8,11},{9,10},{10,... | collective-permute-start | bytes 786440 | tf_op jit(solution)/shard_map/ppermute | solution.py:220

commit v4 on v3

--- a/solution.py
+++ b/solution.py
@@ -12,13 +12,15 @@
 PARTS = 4
 QUARTER = HEAD_DIM // PARTS
 CHUNKS = (8, 8)
-STEP = 4
+STEP = 8
 FINISH_STEP = (4, 4)
 ORDER = (
     ("state", 0),
     ("state", 1),
+    ("inner", 0),
     ("sum", 0),
     ("offer", 0),
+    ("inner", 1),
     ("sum", 1),
     ("offer", 1),
     ("spread", 0),
@@ -30,6 +32,7 @@
 F32 = jnp.float32
 BF16 = jnp.bfloat16
 VMEM_LIMIT = 40 * 1024 * 1024
+SMALL_LIMIT = 16 * 1024 * 1024
 STATE_LIMIT = 60 * 1024 * 1024
 
 SCALARS = pl.BlockSpec(memory_space=pltpu.SMEM)
@@ -170,50 +173,73 @@
     return jnp.stack([prefix, suffix])
 
 
-def finish_kernel(step, factor, info, q, k, v, g, *refs):
-    pieces, (att, qg, kg, vg), hold = refs[:PARTS], refs[-5:-1], refs[-1]
+def inner_kernel(first, step, q, k, v, g, *refs):
+    att, qg, kg, vg = refs[-4:]
     rows = q.shape[0]
-    causal = lax.broadcasted_iota(jnp.int32, (rows, rows), 0) >= lax.broadcasted_iota(
-        jnp.int32, (rows, rows), 1
-    )
+    after = lax.broadcasted_iota(jnp.int32, (rows, rows), 0)
+    before = lax.broadcasted_iota(jnp.int32, (rows, rows), 1)
+    start = pl.program_id(0) * step
     for h in range(step):
-        cols = slice(h * HEAD_DIM, (h + 1) * HEAD_DIM)
+        cols = pl.ds(pl.multiple_of((first + start + h) * HEAD_DIM, HEAD_DIM), HEAD_DIM)
+        here = pl.ds(pl.multiple_of((start + h) * HEAD_DIM, HEAD_DIM), HEAD_DIM)
+        qh, kh, vh, gh = q[:, cols], k[:, cols], v[:, cols], g[:, cols]
+        weights = jnp.where(after >= before, dot(qh, kh, 1, 1), 0.0).astype(BF16)
+        grad_weights = jnp.where(after >= before, dot(gh, vh, 1, 1), 0.0).astype(BF16)
+        att[:, here] = dot(weights, vh, 1, 0)
+        qg[:, here] = dot(grad_weights, kh, 1, 0)
+        kg[:, here] = dot(grad_weights, qh, 0, 0)
+        vg[:, here] = dot(weights, gh, 0, 0)
+
+
+def inner(arrays, first, heads, step, behind):
+    rows = arrays[0].shape[0]
+    return pl.pallas_call(
+        functools.partial(inner_kernel, first, step),
+        out_shape=[jax.ShapeDtypeStruct((rows, heads * HEAD_DIM), F32)] * 4,
+        grid=(heads // step,),
+        in_specs=[WHOLE] * 4 + [LEFT] * len(behind),
+        out_specs=[WHOLE] * 4,
+        compiler_params=pltpu.CompilerParams(vmem_limit_bytes=SMALL_LIMIT),
+    )(*arrays, *behind)
+
+
+def finish_kernel(first, step, factor, info, q, k, v, g, *refs):
+    terms, pieces = refs[:4], refs[4 : 4 + PARTS]
+    outs, hold = refs[-5:-1], refs[-1]
+    start = pl.program_id(0) * step
+    for h in range(step):
+        cols = pl.ds(pl.multiple_of((first + start + h) * HEAD_DIM, HEAD_DIM), HEAD_DIM)
+        here = pl.ds(pl.multiple_of((start + h) * HEAD_DIM, HEAD_DIM), HEAD_DIM)
         for r in range(PARTS):
             at = pl.ds(place(info, r), QUARTER)
-            hold[0, at, :] = pieces[r][0, h].astype(BF16)
-            hold[1, at, :] = pieces[r][1, h].astype(BF16)
-        qh, kh, vh, gh = q[:, cols], k[:, cols], v[:, cols], g[:, cols]
-        prefix, suffix = hold[0], hold[1]
-        weights = jnp.where(causal, dot(qh, kh, 1, 1), 0.0).astype(BF16)
-        grad_weights = jnp.where(causal, dot(gh, vh, 1, 1), 0.0).astype(BF16)
-        att[:, cols] = (factor * (dot(weights, vh, 1, 0) + dot(qh, prefix, 1, 0))).astype(BF16)
-        qg[:, cols] = (factor * (dot(grad_weights, kh, 1, 0) + dot(gh, prefix, 1, 1))).astype(BF16)
-        kg[:, cols] = (factor * (dot(grad_weights, qh, 0, 0) + dot(vh, suffix, 1, 1))).astype(BF16)
-        vg[:, cols] = (factor * (dot(weights, gh, 0, 0) + dot(kh, suffix, 1, 0))).astype(BF16)
-
-
-def finish(info, arrays, pieces, outs, first, step, factor, behind):
+            hold[h, 0, at, :] = pieces[r][0, start + h].astype(BF16)
+            hold[h, 1, at, :] = pieces[r][1, start + h].astype(BF16)
+        prefix, suffix = hold[h, 0], hold[h, 1]
+        outer = (
+            dot(q[:, cols], prefix, 1, 0),
+            dot(g[:, cols], prefix, 1, 1),
+            dot(v[:, cols], suffix, 1, 1),
+            dot(k[:, cols], suffix, 1, 0),
+        )
+        for out, term, more in zip(outs, terms, outer):
+            out[:, h * HEAD_DIM : (h + 1) * HEAD_DIM] = (factor * (term[:, here] + more)).astype(BF16)
+
+
+def finish(info, arrays, terms, pieces, outs, first, step, factor, behind):
     rows, width = arrays[0].shape
     heads = pieces[0].shape[1]
-    columns = pl.BlockSpec((rows, step * HEAD_DIM), lambda i, info: (0, first // step + i))
-    quarter = pl.BlockSpec((2, step, QUARTER, HEAD_DIM), lambda i, info: (0, i, 0, 0))
-    given = [info, *arrays, *pieces, *outs, *behind]
-    fixed = 5 + PARTS
-    return pl.pallas_call(
-        functools.partial(finish_kernel, step, factor),
+    columns = pl.BlockSpec((rows, step * HEAD_DIM), lambda i: (0, first // step + i))
+    fixed = 1 + 4 + 4 + PARTS
+    return pl.pallas_call(
+        functools.partial(finish_kernel, first, step, factor),
         out_shape=[jax.ShapeDtypeStruct((rows, width), BF16)] * 4,
-        grid_spec=pltpu.PrefetchScalarGridSpec(
-            num_scalar_prefetch=1,
-            grid=(heads // step,),
-            in_specs=[columns] * 4
-            + [quarter] * PARTS
-            + [LEFT] * (len(outs) + len(behind)),
-            out_specs=[columns] * 4,
-            scratch_shapes=[pltpu.VMEM((2, HEAD_DIM, HEAD_DIM), BF16)],
-        ),
+        grid=(heads // step,),
+        in_specs=[SCALARS] + [WHOLE] * (8 + PARTS) + [LEFT] * (len(outs) + len(behind)),
+        out_specs=[columns] * 4,
+        scratch_shapes=[pltpu.VMEM((step, 2, HEAD_DIM, HEAD_DIM), BF16)],
         input_output_aliases={fixed + i: i for i in range(len(outs))},
-        compiler_params=pltpu.CompilerParams(vmem_limit_bytes=VMEM_LIMIT),
-    )(*given)
+        compiler_params=pltpu.CompilerParams(vmem_limit_bytes=SMALL_LIMIT),
+    )(info, *arrays, *terms, *pieces, *outs, *behind)
 
 
 def swap(array, size, mask):
@@ -232,7 +258,7 @@
     info = jnp.stack([place_in % PARTS, node, place_in // PARTS]).astype(jnp.int32)
 
     firsts = [sum(CHUNKS[:i]) for i in range(len(CHUNKS))]
-    pieces, given, ready, state = {}, {}, {}, {}
+    pieces, given, ready, state, terms = {}, {}, {}, {}, {}
     outs = ()
     last = info
     for stage, i in ORDER:
@@ -259,8 +285,13 @@
             last = own[0]
             got = {r: swap(own[r], size, r) for r in (1, 3, 2)}
             ready[i] = [own[0], got[1], got[2], got[3]]
+        elif stage == "inner":
+            terms[i] = inner(arrays, first, count, FINISH_STEP[i], behind)
+            last = terms[i][0]
         else:
-            outs = finish(info, arrays, ready[i], outs, first, FINISH_STEP[i], factor, behind)
+            outs = finish(
+                info, arrays, terms[i], ready[i], outs, first, FINISH_STEP[i], factor, behind
+            )
     return tuple(outs)
 
 

time: 78.6 us -> 76.4 us (0.972)
  starting transfers between devices: 26.6 us -> 20.4 us
  waiting for transfers between devices: 28.9 us -> 31.5 us
  Pallas kernels: 20.7 us -> 21.9 us
    ppermute x14, starting transfers between devices: 26.4 us -> 20.2 us  [swap(): return lax.ppermute(array, 'local', [(i, i ^ mask) for i in range(size)])]
    ppermute x14, waiting for transfers between devices: 26.2 us -> 28.8 us  [swap(): return lax.ppermute(array, 'local', [(i, i ^ mask) for i in range(size)])]
    pallas_call x2 -> x4, Pallas kernels: 8.73 us -> 10.6 us  [the longest x2 5.78 us: inner(): pl.pallas_call(functools.partial(inner_kernel, first, step), out_shape=[j...]
  transfers between devices with their start and end apart: 16 -> 16, of which waited for: 8 -> 9; matrix products, arithmetic and copies ran while one was open for 0% -> 0% of each run, Pallas kernels for 16% -> 21%
where the time goes in v4:
time: 76.4 us; the launch traced here: 76.2 us
  waiting for transfers between devices  31.5 us (41%)
  Pallas kernels  21.9 us (29%)
  starting transfers between devices  20.4 us (27%)
  local copies, waits for them, and re-layouts  0.97 us (1%)
  between operations  0.81 us (1%)
    ppermute x14, waiting for transfers between devices, swap(): return lax.ppermute(array, 'local', [(i, i ^ mask) for i in range(size)])  28.8 us
    ppermute x14, starting transfers between devices, swap(): return lax.ppermute(array, 'local', [(i, i ^ mask) for i in range(size)])  20.2 us
    pallas_call x2, Pallas kernels, states(): pl.pallas_call(functools.partial(state_kernel, first, heads), out_shape=[...  7.25 us
    pallas_call x2, Pallas kernels, inner(): pl.pallas_call(functools.partial(inner_kernel, first, step), out_shape=[j...  5.78 us
    pallas_call x2, Pallas kernels, finish(): pl.pallas_call(functools.partial(finish_kernel, first, step, factor), out...  4.78 us
    ppermute x2, waiting for transfers between devices, local(): across = lax.ppermute(halves, 'node', [(0, 1), (1, 0)])  2.67 us
    pallas_call x2, Pallas kernels, spread(): pl.pallas_call(functools.partial(spread_kernel, len(given) > 1), out_shap...  1.73 us
  transfers between devices with their start and end apart: 16, of which 9 were waited for; matrix products, arithmetic and copies ran while one was open for 0% of the time, Pallas kernels for 21%

profile of v4, /device:TPU:0, one launch (start us, length us, event | category | flops | bytes accessed | tf_op | source)
XLA Modules:
  0.0 76.2 jit_solution(14609156289687470622)
XLA Ops:
  0.7 0.7 pad_add_fusion.info.refs_0_
  1.3 3.5 %shard_map.75 = (f32[2,8,32,128]{3,2,1,0:T(8,128)}, f32[2,8,32,128]{3,2,1,0:T(8,128)}, f32[2,8,32,128]{3,2,1,0:T(8,128)}, f32[2,8,32,128]{3,2,1,0:T(8,128)}) custom-call(s32[3]{0:T(128)} %pad_add_fusion.info.refs_0_, bf16[192,2048]{1,0:T(8,128)(2,1)} %q.11, bf16[192,2048]{1,0:T(8,128)(2,1)} %k.11, bf16[192,2048]{1,0:T(8,128)(2,1)} %v.11, ...), custom_call_target="tpu_custom_call" | custom-call | tf_op jit(solution)/shard_map/pallas_call | solution.py:81
  4.8 3.0 %collective-permute-start = (f32[2,8,32,128]{3,2,1,0:T(8,128)}, f32[2,8,32,128]{3,2,1,0:T(8,128)S(1)}, u32[]{:S(2)}, u32[]{:S(2)}) collective-permute-start(f32[2,8,32,128]{3,2,1,0:T(8,128)} %get-tuple-element.37), channel_id=1, source_target_pairs={{0,1},{1,0},{2,3},{3,2},{4,5},{5,4},{6,7},{7,6},{8,9},{9,8},{10,11... | collective-permute-start | bytes 786440 | tf_op jit(solution)/shard_map/ppermute | solution.py:246
  7.8 1.6 %collective-permute-start.1 = (f32[2,8,32,128]{3,2,1,0:T(8,128)}, f32[2,8,32,128]{3,2,1,0:T(8,128)S(1)}, u32[]{:S(2)}, u32[]{:S(2)}) collective-permute-start(f32[2,8,32,128]{3,2,1,0:T(8,128)} %get-tuple-element.38), channel_id=1, source_target_pairs={{0,2},{1,3},{2,0},{3,1},{4,6},{5,7},{6,4},{7,5},{8,10},{9,11},{10,... | collective-permute-start | bytes 786440 | tf_op jit(solution)/shard_map/ppermute | solution.py:246
  9.4 0.0 collective-permute-start.2
  9.4 0.0 copy-start
  9.4 0.0 copy-start.1
  9.4 0.0 copy-start.2
  9.4 0.0 copy-start.3
  9.5 3.8 %shard_map.76 = (f32[2,8,32,128]{3,2,1,0:T(8,128)}, f32[2,8,32,128]{3,2,1,0:T(8,128)}, f32[2,8,32,128]{3,2,1,0:T(8,128)}, f32[2,8,32,128]{3,2,1,0:T(8,128)}) custom-call(s32[3]{0:T(128)} %pad_add_fusion.info.refs_0_, bf16[192,2048]{1,0:T(8,128)(2,1)} %q.11, bf16[192,2048]{1,0:T(8,128)(2,1)} %k.11, bf16[192,2048]{1,0:T(8,128)(2,1)} %v.11, ...), custom_call_target="tpu_custom_call" | custom-call | tf_op jit(solution)/shard_map/pallas_call | solution.py:81
  13.2 2.0 %collective-permute-start.4 = (f32[2,8,32,128]{3,2,1,0:T(8,128)}, f32[2,8,32,128]{3,2,1,0:T(8,128)S(1)}, u32[]{:S(2)}, u32[]{:S(2)}) collective-permute-start(f32[2,8,32,128]{3,2,1,0:T(8,128)} %get-tuple-element.48), channel_id=1, source_target_pairs={{0,1},{1,0},{2,3},{3,2},{4,5},{5,4},{6,7},{7,6},{8,9},{9,8},{10,11... | collective-permute-start | bytes 786440 | tf_op jit(solution)/shard_map/ppermute | solution.py:246
  15.2 1.6 %collective-permute-start.5 = (f32[2,8,32,128]{3,2,1,0:T(8,128)}, f32[2,8,32,128]{3,2,1,0:T(8,128)S(1)}, u32[]{:S(2)}, u32[]{:S(2)}) collective-permute-start(f32[2,8,32,128]{3,2,1,0:T(8,128)} %get-tuple-element.49), channel_id=1, source_target_pairs={{0,2},{1,3},{2,0},{3,1},{4,6},{5,7},{6,4},{7,5},{8,10},{9,11},{10,... | collective-permute-start | bytes 786440 | tf_op jit(solution)/shard_map/ppermute | solution.py:246
  16.8 0.0 collective-permute-done.b.refs_1_
  16.8 0.6 collective-permute-start.6
  17.4 0.0 copy-done
  17.4 0.0 copy-done.1
  17.4 0.0 copy-done.2
  17.4 0.0 copy-done.3
  17.4 0.0 copy-start.5
  17.4 0.9 %copy-done.5 = f32[2,8,32,128]{3,2,1,0:T(8,128)S(1)} copy-done((f32[2,8,32,128]{3,2,1,0:T(8,128)S(1)}, f32[2,8,32,128]{3,2,1,0:T(8,128)}, u32[]{:S(2)}) %copy-start.5) | copy-done | bytes 262168
  18.4 0.0 copy-start.4
  18.4 2.9 %shard_map.77 = (f32[192,1024]{1,0:T(8,128)S(1)}, f32[192,1024]{1,0:T(8,128)S(1)}, f32[192,1024]{1,0:T(8,128)S(1)}, f32[192,1024]{1,0:T(8,128)S(1)}) custom-call(bf16[192,2048]{1,0:T(8,128)(2,1)S(1)} %copy-done, bf16[192,2048]{1,0:T(8,128)(2,1)S(1)} %copy-done.1, bf16[192,2048]{1,0:T(8,128)(2,1)S(1)} %copy-done.2, bf16[192,2048]{1,0:T(8,128)(2,1)S(1)} %copy-done.3, ...), custom_call_target="tpu_custom_call" | custom-call | tf_op jit(solution)/shard_map/pallas_call | solution.py:196
  21.3 0.0 copy-start.7
  21.3 0.0 collective-permute-done.1.c.refs_2_
  21.3 1.1 %collective-permute-done.2.d.refs_3_ = f32[2,8,32,128]{3,2,1,0:T(8,128)S(1)} collective-permute-done((f32[2,8,32,128]{3,2,1,0:T(8,128)}, f32[2,8,32,128]{3,2,1,0:T(8,128)S(1)}, u32[]{:S(2)}, u32[]{:S(2)}) %collective-permute-start.2) | collective-permute-done | bytes 262176 | tf_op jit(solution)/shard_map/ppermute | solution.py:246
  22.4 0.0 copy-done.4
  22.4 0.0 copy-done.7
  22.4 0.6 shard_map.78
  23.0 0.1 collective-permute-start.3
  23.1 1.3 %collective-permute-done.3.across.refs_4_ = f32[8,32,128]{2,1,0:T(8,128)S(1)} collective-permute-done((f32[8,32,128]{2,1,0:T(8,128)S(1)}, f32[8,32,128]{2,1,0:T(8,128)S(1)}, u32[]{:S(2)}, u32[]{:S(2)}) %collective-permute-start.3) | collective-permute-done | bytes 131104 | tf_op jit(solution)/shard_map/ppermute | solution.py:274
  24.5 0.6 shard_map.79.refs_0_
  25.0 0.0 copy-start.6
  25.0 3.1 %collective-permute-start.9 = (f32[2,8,32,128]{3,2,1,0:T(8,128)S(1)}, f32[2,8,32,128]{3,2,1,0:T(8,128)S(1)}, u32[]{:S(2)}, u32[]{:S(2)}) collective-permute-start(f32[2,8,32,128]{3,2,1,0:T(8,128)S(1)} %shard_map.79.refs_0_), channel_id=1, source_target_pairs={{0,4},{1,5},{2,6},{3,7},{4,0},{5,1},{6,2},{7,3},{8,12},{9,13},{10,... | collective-permute-start | bytes 786440 | tf_op jit(solution)/shard_map/ppermute | solution.py:246
  28.2 2.9 %shard_map.80 = (f32[192,1024]{1,0:T(8,128)S(1)}, f32[192,1024]{1,0:T(8,128)S(1)}, f32[192,1024]{1,0:T(8,128)S(1)}, f32[192,1024]{1,0:T(8,128)S(1)}) custom-call(bf16[192,2048]{1,0:T(8,128)(2,1)S(1)} %copy-done, bf16[192,2048]{1,0:T(8,128)(2,1)S(1)} %copy-done.1, bf16[192,2048]{1,0:T(8,128)(2,1)S(1)} %copy-done.2, bf16[192,2048]{1,0:T(8,128)(2,1)S(1)} %copy-done.3, ...), custom_call_target="tpu_custom_call" | custom-call | tf_op jit(solution)/shard_map/pallas_call | solution.py:196
  31.1 0.0 collective-permute-done.4.b.refs_1_
  31.1 0.0 collective-permute-done.5.c.refs_2_
  31.1 6.0 %collective-permute-done.6.d.refs_3_ = f32[2,8,32,128]{3,2,1,0:T(8,128)S(1)} collective-permute-done((f32[2,8,32,128]{3,2,1,0:T(8,128)}, f32[2,8,32,128]{3,2,1,0:T(8,128)S(1)}, u32[]{:S(2)}, u32[]{:S(2)}) %collective-permute-start.6) | collective-permute-done | bytes 262176 | tf_op jit(solution)/shard_map/ppermute | solution.py:246
  37.1 0.0 copy-done.6
  37.1 0.6 shard_map.81
  37.7 0.1 collective-permute-start.7
  37.8 1.3 %collective-permute-done.7.across.refs_4_ = f32[8,32,128]{2,1,0:T(8,128)S(1)} collective-permute-done((f32[8,32,128]{2,1,0:T(8,128)S(1)}, f32[8,32,128]{2,1,0:T(8,128)S(1)}, u32[]{:S(2)}, u32[]{:S(2)}) %collective-permute-start.7) | collective-permute-done | bytes 131104 | tf_op jit(solution)/shard_map/ppermute | solution.py:274
  39.1 0.6 shard_map.82.refs_6_
  39.7 0.8 %collective-permute-start.8 = (f32[2,8,32,128]{3,2,1,0:T(8,128)S(1)}, f32[2,8,32,128]{3,2,1,0:T(8,128)S(1)}, u32[]{:S(2)}, u32[]{:S(2)}) collective-permute-start(f32[2,8,32,128]{3,2,1,0:T(8,128)S(1)} %shard_map.82.refs_6_), channel_id=1, source_target_pairs={{0,4},{1,5},{2,6},{3,7},{4,0},{5,1},{6,2},{7,3},{8,12},{9,13},{10,... | collective-permute-start | bytes 786440 | tf_op jit(solution)/shard_map/ppermute | solution.py:246
  40.5 0.0 collective-permute-done.9.refs_5_
  40.5 0.9 %shard_map.83 = (f32[2,8,32,128]{3,2,1,0:T(8,128)S(1)}, f32[2,8,32,128]{3,2,1,0:T(8,128)S(1)}, f32[2,8,32,128]{3,2,1,0:T(8,128)S(1)}, f32[2,8,32,128]{3,2,1,0:T(8,128)S(1)}) custom-call(s32[3]{0:T(128)S(1)} %copy-done.7, f32[2,8,32,128]{3,2,1,0:T(8,128)S(1)} %copy-done.4, f32[2,8,32,128]{3,2,1,0:T(8,128)S(1)} %collective-permute-done.b.refs_1_, ...), custom_call_target="tpu_custom_call" | custom-call | tf_op jit(solution)/shard_map/pallas_call | solution.py:154
  41.4 2.0 %collective-permute-start.13 = (f32[2,8,32,128]{3,2,1,0:T(8,128)S(1)}, f32[2,8,32,128]{3,2,1,0:T(8,128)S(1)}, u32[]{:S(2)}, u32[]{:S(2)}) collective-permute-start(f32[2,8,32,128]{3,2,1,0:T(8,128)S(1)} %get-tuple-element.61), channel_id=1, source_target_pairs={{0,1},{1,0},{2,3},{3,2},{4,5},{5,4},{6,7},{7,6},{8,9},{9,8},{10,11... | collective-permute-start | bytes 786440 | tf_op jit(solution)/shard_map/ppermute | solution.py:246
  43.4 1.9 %collective-permute-start.14 = (f32[2,8,32,128]{3,2,1,0:T(8,128)S(1)}, f32[2,8,32,128]{3,2,1,0:T(8,128)S(1)}, u32[]{:S(2)}, u32[]{:S(2)}) collective-permute-start(f32[2,8,32,128]{3,2,1,0:T(8,128)S(1)} %get-tuple-element.62), channel_id=1, source_target_pairs={{0,2},{1,3},{2,0},{3,1},{4,6},{5,7},{6,4},{7,5},{8,10},{9,11},{10,... | collective-permute-start | bytes 786440 | tf_op jit(solution)/shard_map/ppermute | solution.py:246
  45.3 0.0 collective-permute-start.15
  45.3 9.4 %collective-permute-done.8.refs_5_ = f32[2,8,32,128]{3,2,1,0:T(8,128)S(1)} collective-permute-done((f32[2,8,32,128]{3,2,1,0:T(8,128)S(1)}, f32[2,8,32,128]{3,2,1,0:T(8,128)S(1)}, u32[]{:S(2)}, u32[]{:S(2)}) %collective-permute-start.8) | collective-permute-done | bytes 262176 | tf_op jit(solution)/shard_map/ppermute | solution.py:246
  54.7 0.9 %shard_map.84 = (f32[2,8,32,128]{3,2,1,0:T(8,128)S(1)}, f32[2,8,32,128]{3,2,1,0:T(8,128)S(1)}, f32[2,8,32,128]{3,2,1,0:T(8,128)S(1)}, f32[2,8,32,128]{3,2,1,0:T(8,128)S(1)}) custom-call(s32[3]{0:T(128)S(1)} %copy-done.7, f32[2,8,32,128]{3,2,1,0:T(8,128)S(1)} %copy-done.6, f32[2,8,32,128]{3,2,1,0:T(8,128)S(1)} %collective-permute-done.4.b.refs_1_, ...), custom_call_target="tpu_custom_call" | custom-call | tf_op jit(solution)/shard_map/pallas_call | solution.py:154
  55.6 1.5 %collective-permute-start.10 = (f32[2,8,32,128]{3,2,1,0:T(8,128)S(1)}, f32[2,8,32,128]{3,2,1,0:T(8,128)S(1)}, u32[]{:S(2)}, u32[]{:S(2)}) collective-permute-start(f32[2,8,32,128]{3,2,1,0:T(8,128)S(1)} %get-tuple-element.55), channel_id=1, source_target_pairs={{0,1},{1,0},{2,3},{3,2},{4,5},{5,4},{6,7},{7,6},{8,9},{9,8},{10,11... | collective-permute-start | bytes 786440 | tf_op jit(solution)/shard_map/ppermute | solution.py:246
  57.1 0.0 collective-permute-start.11
  57.1 0.0 collective-permute-done.13.refs_5_
  57.1 2.1 %collective-permute-start.12 = (f32[2,8,32,128]{3,2,1,0:T(8,128)S(1)}, f32[2,8,32,128]{3,2,1,0:T(8,128)S(1)}, u32[]{:S(2)}, u32[]{:S(2)}) collective-permute-start(f32[2,8,32,128]{3,2,1,0:T(8,128)S(1)} %get-tuple-element.57), channel_id=1, source_target_pairs={{0,3},{1,2},{2,1},{3,0},{4,7},{5,6},{6,5},{7,4},{8,11},{9,10},{10,... | collective-permute-start | bytes 786440 | tf_op jit(solution)/shard_map/ppermute | solution.py:246
  59.2 0.0 collective-permute-done.14.refs_6_
  59.2 4.1 %collective-permute-done.15.refs_7_ = f32[2,8,32,128]{3,2,1,0:T(8,128)S(1)} collective-permute-done((f32[2,8,32,128]{3,2,1,0:T(8,128)S(1)}, f32[2,8,32,128]{3,2,1,0:T(8,128)S(1)}, u32[]{:S(2)}, u32[]{:S(2)}) %collective-permute-start.15) | collective-permute-done | bytes 262176 | tf_op jit(solution)/shard_map/ppermute | solution.py:246
  63.3 2.4 %shard_map.85 = (bf16[192,2048]{1,0:T(8,128)(2,1)}, bf16[192,2048]{1,0:T(8,128)(2,1)}, bf16[192,2048]{1,0:T(8,128)(2,1)}, bf16[192,2048]{1,0:T(8,128)(2,1)}) custom-call(s32[3]{0:T(128)S(1)} %copy-done.7, bf16[192,2048]{1,0:T(8,128)(2,1)S(1)} %copy-done, bf16[192,2048]{1,0:T(8,128)(2,1)S(1)} %copy-done.1, bf16[192,2048]{1,0:T(8,128)(2,1)S(1)} %copy-done.2, ...), custom_call_target="tpu_custom_call" | custom-call | tf_op jit(solution)/shard_map/pallas_call | solution.py:233
  65.7 3.1 %collective-permute-done.10.refs_5_ = f32[2,8,32,128]{3,2,1,0:T(8,128)S(1)} collective-permute-done((f32[2,8,32,128]{3,2,1,0:T(8,128)S(1)}, f32[2,8,32,128]{3,2,1,0:T(8,128)S(1)}, u32[]{:S(2)}, u32[]{:S(2)}) %collective-permute-start.10) | collective-permute-done | bytes 262176 | tf_op jit(solution)/shard_map/ppermute | solution.py:246
  68.8 0.2 collective-permute-done.11.refs_6_
  69.1 4.7 %collective-permute-done.12.refs_7_ = f32[2,8,32,128]{3,2,1,0:T(8,128)S(1)} collective-permute-done((f32[2,8,32,128]{3,2,1,0:T(8,128)S(1)}, f32[2,8,32,128]{3,2,1,0:T(8,128)S(1)}, u32[]{:S(2)}, u32[]{:S(2)}) %collective-permute-start.12) | collective-permute-done | bytes 262176 | tf_op jit(solution)/shard_map/ppermute | solution.py:246
  73.8 2.4 %shard_map.86 = (bf16[192,2048]{1,0:T(8,128)(2,1)}, bf16[192,2048]{1,0:T(8,128)(2,1)}, bf16[192,2048]{1,0:T(8,128)(2,1)}, bf16[192,2048]{1,0:T(8,128)(2,1)}) custom-call(s32[3]{0:T(128)S(1)} %copy-done.7, bf16[192,2048]{1,0:T(8,128)(2,1)S(1)} %copy-done, ...), custom_call_target="tpu_custom_call", output_to_operand_aliasing={{0}: (13, {}), {1}: (14, {}), {2}: (15, {}), {3}: (16, {})} | custom-call | tf_op jit(solution)/shard_map/pallas_call | solution.py:233
Async XLA Ops:
  4.8 12.0 %collective-permute-start = (f32[2,8,32,128]{3,2,1,0:T(8,128)}, f32[2,8,32,128]{3,2,1,0:T(8,128)S(1)}, u32[]{:S(2)}, u32[]{:S(2)}) collective-permute-start(f32[2,8,32,128]{3,2,1,0:T(8,128)} %get-tuple-element.37), channel_id=1, source_target_pairs={{0,1},{1,0},{2,3},{3,2},{4,5},{5,4},{6,7},{7,6},{8,9},{9,8},{10,11... | collective-permute-start | bytes 786440 | tf_op jit(solution)/shard_map/ppermute | solution.py:246
  7.8 13.5 %collective-permute-start.1 = (f32[2,8,32,128]{3,2,1,0:T(8,128)}, f32[2,8,32,128]{3,2,1,0:T(8,128)S(1)}, u32[]{:S(2)}, u32[]{:S(2)}) collective-permute-start(f32[2,8,32,128]{3,2,1,0:T(8,128)} %get-tuple-element.38), channel_id=1, source_target_pairs={{0,2},{1,3},{2,0},{3,1},{4,6},{5,7},{6,4},{7,5},{8,10},{9,11},{10,... | collective-permute-start | bytes 786440 | tf_op jit(solution)/shard_map/ppermute | solution.py:246
  9.4 13.0 %collective-permute-start.2 = (f32[2,8,32,128]{3,2,1,0:T(8,128)}, f32[2,8,32,128]{3,2,1,0:T(8,128)S(1)}, u32[]{:S(2)}, u32[]{:S(2)}) collective-permute-start(f32[2,8,32,128]{3,2,1,0:T(8,128)} %get-tuple-element.39), channel_id=1, source_target_pairs={{0,3},{1,2},{2,1},{3,0},{4,7},{5,6},{6,5},{7,4},{8,11},{9,10},{10,... | collective-permute-start | bytes 786440 | tf_op jit(solution)/shard_map/ppermute | solution.py:246
  9.4 8.0 %copy-start = (bf16[192,2048]{1,0:T(8,128)(2,1)S(1)}, bf16[192,2048]{1,0:T(8,128)(2,1)}, u32[]{:S(2)}) copy-start(bf16[192,2048]{1,0:T(8,128)(2,1)} %q.11) | copy-start | bytes 2359300
  9.4 8.0 %copy-start.1 = (bf16[192,2048]{1,0:T(8,128)(2,1)S(1)}, bf16[192,2048]{1,0:T(8,128)(2,1)}, u32[]{:S(2)}) copy-start(bf16[192,2048]{1,0:T(8,128)(2,1)} %k.11) | copy-start | bytes 2359300
  9.4 8.0 %copy-start.2 = (bf16[192,2048]{1,0:T(8,128)(2,1)S(1)}, bf16[192,2048]{1,0:T(8,128)(2,1)}, u32[]{:S(2)}) copy-start(bf16[192,2048]{1,0:T(8,128)(2,1)} %v.11) | copy-start | bytes 2359300
  9.4 8.0 %copy-start.3 = (bf16[192,2048]{1,0:T(8,128)(2,1)S(1)}, bf16[192,2048]{1,0:T(8,128)(2,1)}, u32[]{:S(2)}) copy-start(bf16[192,2048]{1,0:T(8,128)(2,1)} %g.11) | copy-start | bytes 2359300
  13.2 17.8 %collective-permute-start.4 = (f32[2,8,32,128]{3,2,1,0:T(8,128)}, f32[2,8,32,128]{3,2,1,0:T(8,128)S(1)}, u32[]{:S(2)}, u32[]{:S(2)}) collective-permute-start(f32[2,8,32,128]{3,2,1,0:T(8,128)} %get-tuple-element.48), channel_id=1, source_target_pairs={{0,1},{1,0},{2,3},{3,2},{4,5},{5,4},{6,7},{7,6},{8,9},{9,8},{10,11... | collective-permute-start | bytes 786440 | tf_op jit(solution)/shard_map/ppermute | solution.py:246
  15.2 15.9 %collective-permute-start.5 = (f32[2,8,32,128]{3,2,1,0:T(8,128)}, f32[2,8,32,128]{3,2,1,0:T(8,128)S(1)}, u32[]{:S(2)}, u32[]{:S(2)}) collective-permute-start(f32[2,8,32,128]{3,2,1,0:T(8,128)} %get-tuple-element.49), channel_id=1, source_target_pairs={{0,2},{1,3},{2,0},{3,1},{4,6},{5,7},{6,4},{7,5},{8,10},{9,11},{10,... | collective-permute-start | bytes 786440 | tf_op jit(solution)/shard_map/ppermute | solution.py:246
  16.8 20.3 %collective-permute-start.6 = (f32[2,8,32,128]{3,2,1,0:T(8,128)}, f32[2,8,32,128]{3,2,1,0:T(8,128)S(1)}, u32[]{:S(2)}, u32[]{:S(2)}) collective-permute-start(f32[2,8,32,128]{3,2,1,0:T(8,128)} %get-tuple-element.50), channel_id=1, source_target_pairs={{0,3},{1,2},{2,1},{3,0},{4,7},{5,6},{6,5},{7,4},{8,11},{9,10},{10,... | collective-permute-start | bytes 786440 | tf_op jit(solution)/shard_map/ppermute | solution.py:246
  17.4 1.0 %copy-start.5 = (f32[2,8,32,128]{3,2,1,0:T(8,128)S(1)}, f32[2,8,32,128]{3,2,1,0:T(8,128)}, u32[]{:S(2)}) copy-start(f32[2,8,32,128]{3,2,1,0:T(8,128)} %get-tuple-element.40.refs_0_.a) | copy-start | bytes 786436
  18.4 4.1 %copy-start.4 = (f32[2,8,32,128]{3,2,1,0:T(8,128)S(1)}, f32[2,8,32,128]{3,2,1,0:T(8,128)}, u32[]{:S(2)}) copy-start(f32[2,8,32,128]{3,2,1,0:T(8,128)} %get-tuple-element.36.refs_0_.a) | copy-start | bytes 786436
  21.3 1.1 %copy-start.7 = (s32[3]{0:T(128)S(1)}, s32[3]{0:T(128)}, u32[]{:S(2)}) copy-start(s32[3]{0:T(128)} %pad_add_fusion.info.refs_0_) | copy-start | bytes 40
  23.0 1.4 %collective-permute-start.3 = (f32[8,32,128]{2,1,0:T(8,128)S(1)}, f32[8,32,128]{2,1,0:T(8,128)S(1)}, u32[]{:S(2)}, u32[]{:S(2)}) collective-permute-start(f32[8,32,128]{2,1,0:T(8,128)S(1)} %get-tuple-element.43), channel_id=1, source_target_pairs={{0,8},{8,0},{1,9},{9,1},{2,10},{10,2},{3,11},{11,3},{4,12},{12,4},... | collective-permute-start | bytes 393224 | tf_op jit(solution)/shard_map/ppermute | solution.py:274
  25.0 12.0 %copy-start.6 = (f32[2,8,32,128]{3,2,1,0:T(8,128)S(1)}, f32[2,8,32,128]{3,2,1,0:T(8,128)}, u32[]{:S(2)}) copy-start(f32[2,8,32,128]{3,2,1,0:T(8,128)} %get-tuple-element.40.refs_0_.a) | copy-start | bytes 786436
  25.0 15.5 %collective-permute-start.9 = (f32[2,8,32,128]{3,2,1,0:T(8,128)S(1)}, f32[2,8,32,128]{3,2,1,0:T(8,128)S(1)}, u32[]{:S(2)}, u32[]{:S(2)}) collective-permute-start(f32[2,8,32,128]{3,2,1,0:T(8,128)S(1)} %shard_map.79.refs_0_), channel_id=1, source_target_pairs={{0,4},{1,5},{2,6},{3,7},{4,0},{5,1},{6,2},{7,3},{8,12},{9,13},{10,... | collective-permute-start | bytes 786440 | tf_op jit(solution)/shard_map/ppermute | solution.py:246
  37.7 1.4 %collective-permute-start.7 = (f32[8,32,128]{2,1,0:T(8,128)S(1)}, f32[8,32,128]{2,1,0:T(8,128)S(1)}, u32[]{:S(2)}, u32[]{:S(2)}) collective-permute-start(f32[8,32,128]{2,1,0:T(8,128)S(1)} %get-tuple-element.51), channel_id=1, source_target_pairs={{0,8},{8,0},{1,9},{9,1},{2,10},{10,2},{3,11},{11,3},{4,12},{12,4},... | collective-permute-start | bytes 393224 | tf_op jit(solution)/shard_map/ppermute | solution.py:274
  39.7 15.0 %collective-permute-start.8 = (f32[2,8,32,128]{3,2,1,0:T(8,128)S(1)}, f32[2,8,32,128]{3,2,1,0:T(8,128)S(1)}, u32[]{:S(2)}, u32[]{:S(2)}) collective-permute-start(f32[2,8,32,128]{3,2,1,0:T(8,128)S(1)} %shard_map.82.refs_6_), channel_id=1, source_target_pairs={{0,4},{1,5},{2,6},{3,7},{4,0},{5,1},{6,2},{7,3},{8,12},{9,13},{10,... | collective-permute-start | bytes 786440 | tf_op jit(solution)/shard_map/ppermute | solution.py:246
  41.4 15.7 %collective-permute-start.13 = (f32[2,8,32,128]{3,2,1,0:T(8,128)S(1)}, f32[2,8,32,128]{3,2,1,0:T(8,128)S(1)}, u32[]{:S(2)}, u32[]{:S(2)}) collective-permute-start(f32[2,8,32,128]{3,2,1,0:T(8,128)S(1)} %get-tuple-element.61), channel_id=1, source_target_pairs={{0,1},{1,0},{2,3},{3,2},{4,5},{5,4},{6,7},{7,6},{8,9},{9,8},{10,11... | collective-permute-start | bytes 786440 | tf_op jit(solution)/shard_map/ppermute | solution.py:246
  43.4 15.7 %collective-permute-start.14 = (f32[2,8,32,128]{3,2,1,0:T(8,128)S(1)}, f32[2,8,32,128]{3,2,1,0:T(8,128)S(1)}, u32[]{:S(2)}, u32[]{:S(2)}) collective-permute-start(f32[2,8,32,128]{3,2,1,0:T(8,128)S(1)} %get-tuple-element.62), channel_id=1, source_target_pairs={{0,2},{1,3},{2,0},{3,1},{4,6},{5,7},{6,4},{7,5},{8,10},{9,11},{10,... | collective-permute-start | bytes 786440 | tf_op jit(solution)/shard_map/ppermute | solution.py:246
  45.3 18.0 %collective-permute-start.15 = (f32[2,8,32,128]{3,2,1,0:T(8,128)S(1)}, f32[2,8,32,128]{3,2,1,0:T(8,128)S(1)}, u32[]{:S(2)}, u32[]{:S(2)}) collective-permute-start(f32[2,8,32,128]{3,2,1,0:T(8,128)S(1)} %get-tuple-element.63), channel_id=1, source_target_pairs={{0,3},{1,2},{2,1},{3,0},{4,7},{5,6},{6,5},{7,4},{8,11},{9,10},{10,... | collective-permute-start | bytes 786440 | tf_op jit(solution)/shard_map/ppermute | solution.py:246
  55.6 13.2 %collective-permute-start.10 = (f32[2,8,32,128]{3,2,1,0:T(8,128)S(1)}, f32[2,8,32,128]{3,2,1,0:T(8,128)S(1)}, u32[]{:S(2)}, u32[]{:S(2)}) collective-permute-start(f32[2,8,32,128]{3,2,1,0:T(8,128)S(1)} %get-tuple-element.55), channel_id=1, source_target_pairs={{0,1},{1,0},{2,3},{3,2},{4,5},{5,4},{6,7},{7,6},{8,9},{9,8},{10,11... | collective-permute-start | bytes 786440 | tf_op jit(solution)/shard_map/ppermute | solution.py:246
  57.1 12.0 %collective-permute-start.11 = (f32[2,8,32,128]{3,2,1,0:T(8,128)S(1)}, f32[2,8,32,128]{3,2,1,0:T(8,128)S(1)}, u32[]{:S(2)}, u32[]{:S(2)}) collective-permute-start(f32[2,8,32,128]{3,2,1,0:T(8,128)S(1)} %get-tuple-element.56), channel_id=1, source_target_pairs={{0,2},{1,3},{2,0},{3,1},{4,6},{5,7},{6,4},{7,5},{8,10},{9,11},{10,... | collective-permute-start | bytes 786440 | tf_op jit(solution)/shard_map/ppermute | solution.py:246
  57.1 16.7 %collective-permute-start.12 = (f32[2,8,32,128]{3,2,1,0:T(8,128)S(1)}, f32[2,8,32,128]{3,2,1,0:T(8,128)S(1)}, u32[]{:S(2)}, u32[]{:S(2)}) collective-permute-start(f32[2,8,32,128]{3,2,1,0:T(8,128)S(1)} %get-tuple-element.57), channel_id=1, source_target_pairs={{0,3},{1,2},{2,1},{3,0},{4,7},{5,6},{6,5},{7,4},{8,11},{9,10},{10,... | collective-permute-start | bytes 786440 | tf_op jit(solution)/shard_map/ppermute | solution.py:246

commit v5 on v4

--- a/solution.py
+++ b/solution.py
@@ -13,6 +13,7 @@
 QUARTER = HEAD_DIM // PARTS
 CHUNKS = (8, 8)
 STEP = 8
+TURN = (0, 3, 2, 1)
 FINISH_STEP = (4, 4)
 ORDER = (
     ("state", 0),
@@ -210,10 +211,10 @@
     for h in range(step):
         cols = pl.ds(pl.multiple_of((first + start + h) * HEAD_DIM, HEAD_DIM), HEAD_DIM)
         here = pl.ds(pl.multiple_of((start + h) * HEAD_DIM, HEAD_DIM), HEAD_DIM)
-        for r in range(PARTS):
+        for r, piece in zip(TURN, pieces):
             at = pl.ds(place(info, r), QUARTER)
-            hold[h, 0, at, :] = pieces[r][0, start + h].astype(BF16)
-            hold[h, 1, at, :] = pieces[r][1, start + h].astype(BF16)
+            hold[h, 0, at, :] = piece[0, start + h].astype(BF16)
+            hold[h, 1, at, :] = piece[1, start + h].astype(BF16)
         prefix, suffix = hold[h, 0], hold[h, 1]
         outer = (
             dot(q[:, cols], prefix, 1, 0),
@@ -267,10 +268,10 @@
         if stage == "state":
             own = states(info, arrays, first, count, behind)
             last = own[0]
-            got = {r: swap(own[r], size, r) for r in (1, 3, 2)}
+            got = {r: swap(own[r], size, r) for r in TURN[1:]}
             pieces[i] = [own[0], got[1], got[2], got[3]]
         elif stage == "sum":
-            last, halves = block_sum(info, pieces[i], behind)
+            last, halves = block_sum(info, [pieces[i][r] for r in TURN], behind)
             across = lax.ppermute(halves, "node", [(0, 1), (1, 0)])
             state[i] = last, across
         elif stage == "offer":
@@ -283,14 +284,14 @@
         elif stage == "spread":
             own = spread(info, pieces[i], given[i], behind)
             last = own[0]
-            got = {r: swap(own[r], size, r) for r in (1, 3, 2)}
+            got = {r: swap(own[r], size, r) for r in TURN[1:]}
             ready[i] = [own[0], got[1], got[2], got[3]]
         elif stage == "inner":
             terms[i] = inner(arrays, first, count, FINISH_STEP[i], behind)
             last = terms[i][0]
         else:
             outs = finish(
-                info, arrays, terms[i], ready[i], outs, first, FINISH_STEP[i], factor, behind
+                info, arrays, terms[i], [ready[i][r] for r in TURN], outs, first, FINISH_STEP[i], factor, behind
             )
     return tuple(outs)
 

time: 76.4 us -> 74.8 us (0.979)
  waiting for transfers between devices: 31.5 us -> 28.2 us
  starting transfers between devices: 20.4 us -> 21.4 us
    ppermute x14, waiting for transfers between devices: 28.8 us -> 25.5 us  [swap(): return lax.ppermute(array, 'local', [(i, i ^ mask) for i in range(size)])]
    ppermute x14, starting transfers between devices: 20.2 us -> 21.3 us  [swap(): return lax.ppermute(array, 'local', [(i, i ^ mask) for i in range(size)])]
  transfers between devices with their start and end apart: 16 -> 16, of which waited for: 9 -> 8; matrix products, arithmetic and copies ran while one was open for 0% -> 0% of each run, Pallas kernels for 21% -> 22%
where the time goes in v5:
time: 74.8 us; the launch traced here: 74.6 us
  waiting for transfers between devices  28.2 us (38%)
  Pallas kernels  21.9 us (29%)
  starting transfers between devices  21.4 us (29%)
  local copies, waits for them, and re-layouts  1.6 us (2%)
  between operations  0.82 us (1%)
    ppermute x14, waiting for transfers between devices, swap(): return lax.ppermute(array, 'local', [(i, i ^ mask) for i in range(size)])  25.5 us
    ppermute x14, starting transfers between devices, swap(): return lax.ppermute(array, 'local', [(i, i ^ mask) for i in range(size)])  21.3 us
    pallas_call x2, Pallas kernels, states(): pl.pallas_call(functools.partial(state_kernel, first, heads), out_shape=[...  7.27 us
    pallas_call x2, Pallas kernels, inner(): pl.pallas_call(functools.partial(inner_kernel, first, step), out_shape=[j...  5.78 us
    pallas_call x2, Pallas kernels, finish(): pl.pallas_call(functools.partial(finish_kernel, first, step, factor), out...  4.79 us
    ppermute x2, waiting for transfers between devices, local(): across = lax.ppermute(halves, 'node', [(0, 1), (1, 0)])  2.67 us
    pallas_call x2, Pallas kernels, spread(): pl.pallas_call(functools.partial(spread_kernel, len(given) > 1), out_shap...  1.73 us
    unnamed x16, local copies, waits for them, and re-layouts  1.6 us
  transfers between devices with their start and end apart: 16, of which 8 were waited for; matrix products, arithmetic and copies ran while one was open for 0% of the time, Pallas kernels for 22%

profile of v5, /device:TPU:0, one launch (start us, length us, event | category | flops | bytes accessed | tf_op | source)
XLA Modules:
  0.0 74.6 jit_solution(11624251969004597290)
XLA Ops:
  0.7 0.7 pad_add_fusion.info.refs_0_
  1.3 3.5 %shard_map.75 = (f32[2,8,32,128]{3,2,1,0:T(8,128)}, f32[2,8,32,128]{3,2,1,0:T(8,128)}, f32[2,8,32,128]{3,2,1,0:T(8,128)}, f32[2,8,32,128]{3,2,1,0:T(8,128)}) custom-call(s32[3]{0:T(128)} %pad_add_fusion.info.refs_0_, bf16[192,2048]{1,0:T(8,128)(2,1)} %q.11, bf16[192,2048]{1,0:T(8,128)(2,1)} %k.11, bf16[192,2048]{1,0:T(8,128)(2,1)} %v.11, ...), custom_call_target="tpu_custom_call" | custom-call | tf_op jit(solution)/shard_map/pallas_call | solution.py:82
  4.8 4.1 %collective-permute-start = (f32[2,8,32,128]{3,2,1,0:T(8,128)}, f32[2,8,32,128]{3,2,1,0:T(8,128)S(1)}, u32[]{:S(2)}, u32[]{:S(2)}) collective-permute-start(f32[2,8,32,128]{3,2,1,0:T(8,128)} %get-tuple-element.37), channel_id=1, source_target_pairs={{0,3},{1,2},{2,1},{3,0},{4,7},{5,6},{6,5},{7,4},{8,11},{9,10},{10,... | collective-permute-start | bytes 786440 | tf_op jit(solution)/shard_map/ppermute | solution.py:247
  8.9 0.4 collective-permute-start.1
  9.3 0.2 collective-permute-start.2
  9.5 0.0 copy-start
  9.5 0.0 copy-start.1
  9.5 0.0 copy-start.2
  9.5 0.0 copy-start.3
  9.5 3.8 %shard_map.76 = (f32[2,8,32,128]{3,2,1,0:T(8,128)}, f32[2,8,32,128]{3,2,1,0:T(8,128)}, f32[2,8,32,128]{3,2,1,0:T(8,128)}, f32[2,8,32,128]{3,2,1,0:T(8,128)}) custom-call(s32[3]{0:T(128)} %pad_add_fusion.info.refs_0_, bf16[192,2048]{1,0:T(8,128)(2,1)} %q.11, bf16[192,2048]{1,0:T(8,128)(2,1)} %k.11, bf16[192,2048]{1,0:T(8,128)(2,1)} %v.11, ...), custom_call_target="tpu_custom_call" | custom-call | tf_op jit(solution)/shard_map/pallas_call | solution.py:82
  13.3 1.9 %collective-permute-start.4 = (f32[2,8,32,128]{3,2,1,0:T(8,128)}, f32[2,8,32,128]{3,2,1,0:T(8,128)S(1)}, u32[]{:S(2)}, u32[]{:S(2)}) collective-permute-start(f32[2,8,32,128]{3,2,1,0:T(8,128)} %get-tuple-element.48), channel_id=1, source_target_pairs={{0,1},{1,0},{2,3},{3,2},{4,5},{5,4},{6,7},{7,6},{8,9},{9,8},{10,11... | collective-permute-start | bytes 786440 | tf_op jit(solution)/shard_map/ppermute | solution.py:247
  15.2 1.6 %collective-permute-start.5 = (f32[2,8,32,128]{3,2,1,0:T(8,128)}, f32[2,8,32,128]{3,2,1,0:T(8,128)S(1)}, u32[]{:S(2)}, u32[]{:S(2)}) collective-permute-start(f32[2,8,32,128]{3,2,1,0:T(8,128)} %get-tuple-element.49), channel_id=1, source_target_pairs={{0,2},{1,3},{2,0},{3,1},{4,6},{5,7},{6,4},{7,5},{8,10},{9,11},{10,... | collective-permute-start | bytes 786440 | tf_op jit(solution)/shard_map/ppermute | solution.py:247
  16.8 0.0 collective-permute-done.b.refs_3_
  16.8 2.4 %collective-permute-start.6 = (f32[2,8,32,128]{3,2,1,0:T(8,128)}, f32[2,8,32,128]{3,2,1,0:T(8,128)S(1)}, u32[]{:S(2)}, u32[]{:S(2)}) collective-permute-start(f32[2,8,32,128]{3,2,1,0:T(8,128)} %get-tuple-element.50), channel_id=1, source_target_pairs={{0,3},{1,2},{2,1},{3,0},{4,7},{5,6},{6,5},{7,4},{8,11},{9,10},{10,... | collective-permute-start | bytes 786440 | tf_op jit(solution)/shard_map/ppermute | solution.py:247
  19.2 0.0 copy-done
  19.2 0.0 copy-done.1
  19.2 0.0 copy-done.2
  19.2 0.0 copy-done.3
  19.2 0.0 copy-start.5
  19.2 0.9 %copy-done.5 = f32[2,8,32,128]{3,2,1,0:T(8,128)S(1)} copy-done((f32[2,8,32,128]{3,2,1,0:T(8,128)S(1)}, f32[2,8,32,128]{3,2,1,0:T(8,128)}, u32[]{:S(2)}) %copy-start.5) | copy-done | bytes 262168
  20.2 0.0 copy-start.4
  20.2 2.9 %shard_map.77 = (f32[192,1024]{1,0:T(8,128)S(1)}, f32[192,1024]{1,0:T(8,128)S(1)}, f32[192,1024]{1,0:T(8,128)S(1)}, f32[192,1024]{1,0:T(8,128)S(1)}) custom-call(bf16[192,2048]{1,0:T(8,128)(2,1)S(1)} %copy-done, bf16[192,2048]{1,0:T(8,128)(2,1)S(1)} %copy-done.1, bf16[192,2048]{1,0:T(8,128)(2,1)S(1)} %copy-done.2, bf16[192,2048]{1,0:T(8,128)(2,1)S(1)} %copy-done.3, ...), custom_call_target="tpu_custom_call" | custom-call | tf_op jit(solution)/shard_map/pallas_call | solution.py:197
  23.1 0.0 copy-start.7
  23.1 0.0 collective-permute-done.1.c.refs_2_
  23.1 0.0 collective-permute-done.2.d.refs_1_
  23.1 0.0 copy-done.4
  23.1 0.6 copy-done.7
  23.8 0.6 shard_map.78
  24.4 0.1 collective-permute-start.3
  24.5 1.3 %collective-permute-done.3.across.refs_4_ = f32[8,32,128]{2,1,0:T(8,128)S(1)} collective-permute-done((f32[8,32,128]{2,1,0:T(8,128)S(1)}, f32[8,32,128]{2,1,0:T(8,128)S(1)}, u32[]{:S(2)}, u32[]{:S(2)}) %collective-permute-start.3) | collective-permute-done | bytes 131104 | tf_op jit(solution)/shard_map/ppermute | solution.py:275
  25.8 0.6 shard_map.79.refs_0_
  26.4 0.0 copy-start.6
  26.4 2.7 %collective-permute-start.9 = (f32[2,8,32,128]{3,2,1,0:T(8,128)S(1)}, f32[2,8,32,128]{3,2,1,0:T(8,128)S(1)}, u32[]{:S(2)}, u32[]{:S(2)}) collective-permute-start(f32[2,8,32,128]{3,2,1,0:T(8,128)S(1)} %shard_map.79.refs_0_), channel_id=1, source_target_pairs={{0,4},{1,5},{2,6},{3,7},{4,0},{5,1},{6,2},{7,3},{8,12},{9,13},{10,... | collective-permute-start | bytes 786440 | tf_op jit(solution)/shard_map/ppermute | solution.py:247
  29.0 2.9 %shard_map.80 = (f32[192,1024]{1,0:T(8,128)S(1)}, f32[192,1024]{1,0:T(8,128)S(1)}, f32[192,1024]{1,0:T(8,128)S(1)}, f32[192,1024]{1,0:T(8,128)S(1)}) custom-call(bf16[192,2048]{1,0:T(8,128)(2,1)S(1)} %copy-done, bf16[192,2048]{1,0:T(8,128)(2,1)S(1)} %copy-done.1, bf16[192,2048]{1,0:T(8,128)(2,1)S(1)} %copy-done.2, bf16[192,2048]{1,0:T(8,128)(2,1)S(1)} %copy-done.3, ...), custom_call_target="tpu_custom_call" | custom-call | tf_op jit(solution)/shard_map/pallas_call | solution.py:197
  31.9 0.0 collective-permute-done.4.d.refs_1_
  31.9 0.0 collective-permute-done.5.c.refs_2_
  31.9 4.7 %collective-permute-done.6.b.refs_3_ = f32[2,8,32,128]{3,2,1,0:T(8,128)S(1)} collective-permute-done((f32[2,8,32,128]{3,2,1,0:T(8,128)}, f32[2,8,32,128]{3,2,1,0:T(8,128)S(1)}, u32[]{:S(2)}, u32[]{:S(2)}) %collective-permute-start.6) | collective-permute-done | bytes 262176 | tf_op jit(solution)/shard_map/ppermute | solution.py:247
  36.7 0.0 copy-done.6
  36.7 0.6 shard_map.81
  37.3 0.1 collective-permute-start.7
  37.4 1.3 %collective-permute-done.7.across.refs_4_ = f32[8,32,128]{2,1,0:T(8,128)S(1)} collective-permute-done((f32[8,32,128]{2,1,0:T(8,128)S(1)}, f32[8,32,128]{2,1,0:T(8,128)S(1)}, u32[]{:S(2)}, u32[]{:S(2)}) %collective-permute-start.7) | collective-permute-done | bytes 131104 | tf_op jit(solution)/shard_map/ppermute | solution.py:275
  38.7 0.6 shard_map.82.refs_6_
  39.3 0.9 %collective-permute-start.8 = (f32[2,8,32,128]{3,2,1,0:T(8,128)S(1)}, f32[2,8,32,128]{3,2,1,0:T(8,128)S(1)}, u32[]{:S(2)}, u32[]{:S(2)}) collective-permute-start(f32[2,8,32,128]{3,2,1,0:T(8,128)S(1)} %shard_map.82.refs_6_), channel_id=1, source_target_pairs={{0,4},{1,5},{2,6},{3,7},{4,0},{5,1},{6,2},{7,3},{8,12},{9,13},{10,... | collective-permute-start | bytes 786440 | tf_op jit(solution)/shard_map/ppermute | solution.py:247
  40.2 1.2 %collective-permute-done.9.refs_5_ = f32[2,8,32,128]{3,2,1,0:T(8,128)S(1)} collective-permute-done((f32[2,8,32,128]{3,2,1,0:T(8,128)S(1)}, f32[2,8,32,128]{3,2,1,0:T(8,128)S(1)}, u32[]{:S(2)}, u32[]{:S(2)}) %collective-permute-start.9) | collective-permute-done | bytes 262176 | tf_op jit(solution)/shard_map/ppermute | solution.py:247
  41.4 0.9 %shard_map.83 = (f32[2,8,32,128]{3,2,1,0:T(8,128)S(1)}, f32[2,8,32,128]{3,2,1,0:T(8,128)S(1)}, f32[2,8,32,128]{3,2,1,0:T(8,128)S(1)}, f32[2,8,32,128]{3,2,1,0:T(8,128)S(1)}) custom-call(s32[3]{0:T(128)S(1)} %copy-done.7, f32[2,8,32,128]{3,2,1,0:T(8,128)S(1)} %copy-done.4, f32[2,8,32,128]{3,2,1,0:T(8,128)S(1)} %collective-permute-done.2.d.refs_1_, ...), custom_call_target="tpu_custom_call" | custom-call | tf_op jit(solution)/shard_map/pallas_call | solution.py:155
  42.2 2.2 %collective-permute-start.13 = (f32[2,8,32,128]{3,2,1,0:T(8,128)S(1)}, f32[2,8,32,128]{3,2,1,0:T(8,128)S(1)}, u32[]{:S(2)}, u32[]{:S(2)}) collective-permute-start(f32[2,8,32,128]{3,2,1,0:T(8,128)S(1)} %get-tuple-element.61), channel_id=1, source_target_pairs={{0,3},{1,2},{2,1},{3,0},{4,7},{5,6},{6,5},{7,4},{8,11},{9,10},{10,... | collective-permute-start | bytes 786440 | tf_op jit(solution)/shard_map/ppermute | solution.py:247
  44.4 0.0 collective-permute-start.14
  44.4 1.4 %collective-permute-start.15 = (f32[2,8,32,128]{3,2,1,0:T(8,128)S(1)}, f32[2,8,32,128]{3,2,1,0:T(8,128)S(1)}, u32[]{:S(2)}, u32[]{:S(2)}) collective-permute-start(f32[2,8,32,128]{3,2,1,0:T(8,128)S(1)} %get-tuple-element.63), channel_id=1, source_target_pairs={{0,1},{1,0},{2,3},{3,2},{4,5},{5,4},{6,7},{7,6},{8,9},{9,8},{10,11... | collective-permute-start | bytes 786440 | tf_op jit(solution)/shard_map/ppermute | solution.py:247
  45.8 8.4 %collective-permute-done.8.refs_5_ = f32[2,8,32,128]{3,2,1,0:T(8,128)S(1)} collective-permute-done((f32[2,8,32,128]{3,2,1,0:T(8,128)S(1)}, f32[2,8,32,128]{3,2,1,0:T(8,128)S(1)}, u32[]{:S(2)}, u32[]{:S(2)}) %collective-permute-start.8) | collective-permute-done | bytes 262176 | tf_op jit(solution)/shard_map/ppermute | solution.py:247
  54.2 0.9 %shard_map.84 = (f32[2,8,32,128]{3,2,1,0:T(8,128)S(1)}, f32[2,8,32,128]{3,2,1,0:T(8,128)S(1)}, f32[2,8,32,128]{3,2,1,0:T(8,128)S(1)}, f32[2,8,32,128]{3,2,1,0:T(8,128)S(1)}) custom-call(s32[3]{0:T(128)S(1)} %copy-done.7, f32[2,8,32,128]{3,2,1,0:T(8,128)S(1)} %copy-done.6, f32[2,8,32,128]{3,2,1,0:T(8,128)S(1)} %collective-permute-done.4.d.refs_1_, ...), custom_call_target="tpu_custom_call" | custom-call | tf_op jit(solution)/shard_map/pallas_call | solution.py:155
  55.0 0.1 collective-permute-start.10
  55.1 3.1 %collective-permute-start.11 = (f32[2,8,32,128]{3,2,1,0:T(8,128)S(1)}, f32[2,8,32,128]{3,2,1,0:T(8,128)S(1)}, u32[]{:S(2)}, u32[]{:S(2)}) collective-permute-start(f32[2,8,32,128]{3,2,1,0:T(8,128)S(1)} %get-tuple-element.56), channel_id=1, source_target_pairs={{0,2},{1,3},{2,0},{3,1},{4,6},{5,7},{6,4},{7,5},{8,10},{9,11},{10,... | collective-permute-start | bytes 786440 | tf_op jit(solution)/shard_map/ppermute | solution.py:247
  58.2 0.0 collective-permute-done.13.refs_5_
  58.2 0.4 collective-permute-start.12
  58.6 4.1 %collective-permute-done.14.refs_6_ = f32[2,8,32,128]{3,2,1,0:T(8,128)S(1)} collective-permute-done((f32[2,8,32,128]{3,2,1,0:T(8,128)S(1)}, f32[2,8,32,128]{3,2,1,0:T(8,128)S(1)}, u32[]{:S(2)}, u32[]{:S(2)}) %collective-permute-start.14) | collective-permute-done | bytes 262176 | tf_op jit(solution)/shard_map/ppermute | solution.py:247
  62.7 0.0 collective-permute-done.15.refs_7_
  62.7 2.4 %shard_map.85 = (bf16[192,2048]{1,0:T(8,128)(2,1)}, bf16[192,2048]{1,0:T(8,128)(2,1)}, bf16[192,2048]{1,0:T(8,128)(2,1)}, bf16[192,2048]{1,0:T(8,128)(2,1)}) custom-call(s32[3]{0:T(128)S(1)} %copy-done.7, bf16[192,2048]{1,0:T(8,128)(2,1)S(1)} %copy-done, bf16[192,2048]{1,0:T(8,128)(2,1)S(1)} %copy-done.1, bf16[192,2048]{1,0:T(8,128)(2,1)S(1)} %copy-done.2, ...), custom_call_target="tpu_custom_call" | custom-call | tf_op jit(solution)/shard_map/pallas_call | solution.py:234
  65.1 4.2 %collective-permute-done.10.refs_5_ = f32[2,8,32,128]{3,2,1,0:T(8,128)S(1)} collective-permute-done((f32[2,8,32,128]{3,2,1,0:T(8,128)S(1)}, f32[2,8,32,128]{3,2,1,0:T(8,128)S(1)}, u32[]{:S(2)}, u32[]{:S(2)}) %collective-permute-start.10) | collective-permute-done | bytes 262176 | tf_op jit(solution)/shard_map/ppermute | solution.py:247
  69.3 2.9 %collective-permute-done.11.refs_6_ = f32[2,8,32,128]{3,2,1,0:T(8,128)S(1)} collective-permute-done((f32[2,8,32,128]{3,2,1,0:T(8,128)S(1)}, f32[2,8,32,128]{3,2,1,0:T(8,128)S(1)}, u32[]{:S(2)}, u32[]{:S(2)}) %collective-permute-start.11) | collective-permute-done | bytes 262176 | tf_op jit(solution)/shard_map/ppermute | solution.py:247
  72.2 0.0 collective-permute-done.12.refs_7_
  72.2 2.4 %shard_map.86 = (bf16[192,2048]{1,0:T(8,128)(2,1)}, bf16[192,2048]{1,0:T(8,128)(2,1)}, bf16[192,2048]{1,0:T(8,128)(2,1)}, bf16[192,2048]{1,0:T(8,128)(2,1)}) custom-call(s32[3]{0:T(128)S(1)} %copy-done.7, bf16[192,2048]{1,0:T(8,128)(2,1)S(1)} %copy-done, ...), custom_call_target="tpu_custom_call", output_to_operand_aliasing={{0}: (13, {}), {1}: (14, {}), {2}: (15, {}), {3}: (16, {})} | custom-call | tf_op jit(solution)/shard_map/pallas_call | solution.py:234
Async XLA Ops:
  4.8 12.0 %collective-permute-start = (f32[2,8,32,128]{3,2,1,0:T(8,128)}, f32[2,8,32,128]{3,2,1,0:T(8,128)S(1)}, u32[]{:S(2)}, u32[]{:S(2)}) collective-permute-start(f32[2,8,32,128]{3,2,1,0:T(8,128)} %get-tuple-element.37), channel_id=1, source_target_pairs={{0,3},{1,2},{2,1},{3,0},{4,7},{5,6},{6,5},{7,4},{8,11},{9,10},{10,... | collective-permute-start | bytes 786440 | tf_op jit(solution)/shard_map/ppermute | solution.py:247
  8.9 14.2 %collective-permute-start.1 = (f32[2,8,32,128]{3,2,1,0:T(8,128)}, f32[2,8,32,128]{3,2,1,0:T(8,128)S(1)}, u32[]{:S(2)}, u32[]{:S(2)}) collective-permute-start(f32[2,8,32,128]{3,2,1,0:T(8,128)} %get-tuple-element.38), channel_id=1, source_target_pairs={{0,2},{1,3},{2,0},{3,1},{4,6},{5,7},{6,4},{7,5},{8,10},{9,11},{10,... | collective-permute-start | bytes 786440 | tf_op jit(solution)/shard_map/ppermute | solution.py:247
  9.3 13.8 %collective-permute-start.2 = (f32[2,8,32,128]{3,2,1,0:T(8,128)}, f32[2,8,32,128]{3,2,1,0:T(8,128)S(1)}, u32[]{:S(2)}, u32[]{:S(2)}) collective-permute-start(f32[2,8,32,128]{3,2,1,0:T(8,128)} %get-tuple-element.39), channel_id=1, source_target_pairs={{0,1},{1,0},{2,3},{3,2},{4,5},{5,4},{6,7},{7,6},{8,9},{9,8},{10,11... | collective-permute-start | bytes 786440 | tf_op jit(solution)/shard_map/ppermute | solution.py:247
  9.5 9.7 %copy-start = (bf16[192,2048]{1,0:T(8,128)(2,1)S(1)}, bf16[192,2048]{1,0:T(8,128)(2,1)}, u32[]{:S(2)}) copy-start(bf16[192,2048]{1,0:T(8,128)(2,1)} %q.11) | copy-start | bytes 2359300
  9.5 9.7 %copy-start.1 = (bf16[192,2048]{1,0:T(8,128)(2,1)S(1)}, bf16[192,2048]{1,0:T(8,128)(2,1)}, u32[]{:S(2)}) copy-start(bf16[192,2048]{1,0:T(8,128)(2,1)} %k.11) | copy-start | bytes 2359300
  9.5 9.7 %copy-start.2 = (bf16[192,2048]{1,0:T(8,128)(2,1)S(1)}, bf16[192,2048]{1,0:T(8,128)(2,1)}, u32[]{:S(2)}) copy-start(bf16[192,2048]{1,0:T(8,128)(2,1)} %v.11) | copy-start | bytes 2359300
  9.5 9.7 %copy-start.3 = (bf16[192,2048]{1,0:T(8,128)(2,1)S(1)}, bf16[192,2048]{1,0:T(8,128)(2,1)}, u32[]{:S(2)}) copy-start(bf16[192,2048]{1,0:T(8,128)(2,1)} %g.11) | copy-start | bytes 2359300
  13.3 18.6 %collective-permute-start.4 = (f32[2,8,32,128]{3,2,1,0:T(8,128)}, f32[2,8,32,128]{3,2,1,0:T(8,128)S(1)}, u32[]{:S(2)}, u32[]{:S(2)}) collective-permute-start(f32[2,8,32,128]{3,2,1,0:T(8,128)} %get-tuple-element.48), channel_id=1, source_target_pairs={{0,1},{1,0},{2,3},{3,2},{4,5},{5,4},{6,7},{7,6},{8,9},{9,8},{10,11... | collective-permute-start | bytes 786440 | tf_op jit(solution)/shard_map/ppermute | solution.py:247
  15.2 16.7 %collective-permute-start.5 = (f32[2,8,32,128]{3,2,1,0:T(8,128)}, f32[2,8,32,128]{3,2,1,0:T(8,128)S(1)}, u32[]{:S(2)}, u32[]{:S(2)}) collective-permute-start(f32[2,8,32,128]{3,2,1,0:T(8,128)} %get-tuple-element.49), channel_id=1, source_target_pairs={{0,2},{1,3},{2,0},{3,1},{4,6},{5,7},{6,4},{7,5},{8,10},{9,11},{10,... | collective-permute-start | bytes 786440 | tf_op jit(solution)/shard_map/ppermute | solution.py:247
  16.8 19.9 %collective-permute-start.6 = (f32[2,8,32,128]{3,2,1,0:T(8,128)}, f32[2,8,32,128]{3,2,1,0:T(8,128)S(1)}, u32[]{:S(2)}, u32[]{:S(2)}) collective-permute-start(f32[2,8,32,128]{3,2,1,0:T(8,128)} %get-tuple-element.50), channel_id=1, source_target_pairs={{0,3},{1,2},{2,1},{3,0},{4,7},{5,6},{6,5},{7,4},{8,11},{9,10},{10,... | collective-permute-start | bytes 786440 | tf_op jit(solution)/shard_map/ppermute | solution.py:247
  19.2 1.0 %copy-start.5 = (f32[2,8,32,128]{3,2,1,0:T(8,128)S(1)}, f32[2,8,32,128]{3,2,1,0:T(8,128)}, u32[]{:S(2)}) copy-start(f32[2,8,32,128]{3,2,1,0:T(8,128)} %get-tuple-element.40.refs_0_.a) | copy-start | bytes 786436
  20.2 2.9 %copy-start.4 = (f32[2,8,32,128]{3,2,1,0:T(8,128)S(1)}, f32[2,8,32,128]{3,2,1,0:T(8,128)}, u32[]{:S(2)}) copy-start(f32[2,8,32,128]{3,2,1,0:T(8,128)} %get-tuple-element.36.refs_0_.a) | copy-start | bytes 786436
  23.1 0.7 copy-start.7
  24.4 1.4 %collective-permute-start.3 = (f32[8,32,128]{2,1,0:T(8,128)S(1)}, f32[8,32,128]{2,1,0:T(8,128)S(1)}, u32[]{:S(2)}, u32[]{:S(2)}) collective-permute-start(f32[8,32,128]{2,1,0:T(8,128)S(1)} %get-tuple-element.43), channel_id=1, source_target_pairs={{0,8},{8,0},{1,9},{9,1},{2,10},{10,2},{3,11},{11,3},{4,12},{12,4},... | collective-permute-start | bytes 393224 | tf_op jit(solution)/shard_map/ppermute | solution.py:275
  26.4 10.3 %copy-start.6 = (f32[2,8,32,128]{3,2,1,0:T(8,128)S(1)}, f32[2,8,32,128]{3,2,1,0:T(8,128)}, u32[]{:S(2)}) copy-start(f32[2,8,32,128]{3,2,1,0:T(8,128)} %get-tuple-element.40.refs_0_.a) | copy-start | bytes 786436
  26.4 15.0 %collective-permute-start.9 = (f32[2,8,32,128]{3,2,1,0:T(8,128)S(1)}, f32[2,8,32,128]{3,2,1,0:T(8,128)S(1)}, u32[]{:S(2)}, u32[]{:S(2)}) collective-permute-start(f32[2,8,32,128]{3,2,1,0:T(8,128)S(1)} %shard_map.79.refs_0_), channel_id=1, source_target_pairs={{0,4},{1,5},{2,6},{3,7},{4,0},{5,1},{6,2},{7,3},{8,12},{9,13},{10,... | collective-permute-start | bytes 786440 | tf_op jit(solution)/shard_map/ppermute | solution.py:247
  37.3 1.4 %collective-permute-start.7 = (f32[8,32,128]{2,1,0:T(8,128)S(1)}, f32[8,32,128]{2,1,0:T(8,128)S(1)}, u32[]{:S(2)}, u32[]{:S(2)}) collective-permute-start(f32[8,32,128]{2,1,0:T(8,128)S(1)} %get-tuple-element.51), channel_id=1, source_target_pairs={{0,8},{8,0},{1,9},{9,1},{2,10},{10,2},{3,11},{11,3},{4,12},{12,4},... | collective-permute-start | bytes 393224 | tf_op jit(solution)/shard_map/ppermute | solution.py:275
  39.3 14.9 %collective-permute-start.8 = (f32[2,8,32,128]{3,2,1,0:T(8,128)S(1)}, f32[2,8,32,128]{3,2,1,0:T(8,128)S(1)}, u32[]{:S(2)}, u32[]{:S(2)}) collective-permute-start(f32[2,8,32,128]{3,2,1,0:T(8,128)S(1)} %shard_map.82.refs_6_), channel_id=1, source_target_pairs={{0,4},{1,5},{2,6},{3,7},{4,0},{5,1},{6,2},{7,3},{8,12},{9,13},{10,... | collective-permute-start | bytes 786440 | tf_op jit(solution)/shard_map/ppermute | solution.py:247
  42.2 16.0 %collective-permute-start.13 = (f32[2,8,32,128]{3,2,1,0:T(8,128)S(1)}, f32[2,8,32,128]{3,2,1,0:T(8,128)S(1)}, u32[]{:S(2)}, u32[]{:S(2)}) collective-permute-start(f32[2,8,32,128]{3,2,1,0:T(8,128)S(1)} %get-tuple-element.61), channel_id=1, source_target_pairs={{0,3},{1,2},{2,1},{3,0},{4,7},{5,6},{6,5},{7,4},{8,11},{9,10},{10,... | collective-permute-start | bytes 786440 | tf_op jit(solution)/shard_map/ppermute | solution.py:247
  44.4 18.2 %collective-permute-start.14 = (f32[2,8,32,128]{3,2,1,0:T(8,128)S(1)}, f32[2,8,32,128]{3,2,1,0:T(8,128)S(1)}, u32[]{:S(2)}, u32[]{:S(2)}) collective-permute-start(f32[2,8,32,128]{3,2,1,0:T(8,128)S(1)} %get-tuple-element.62), channel_id=1, source_target_pairs={{0,2},{1,3},{2,0},{3,1},{4,6},{5,7},{6,4},{7,5},{8,10},{9,11},{10,... | collective-permute-start | bytes 786440 | tf_op jit(solution)/shard_map/ppermute | solution.py:247
  44.4 18.2 %collective-permute-start.15 = (f32[2,8,32,128]{3,2,1,0:T(8,128)S(1)}, f32[2,8,32,128]{3,2,1,0:T(8,128)S(1)}, u32[]{:S(2)}, u32[]{:S(2)}) collective-permute-start(f32[2,8,32,128]{3,2,1,0:T(8,128)S(1)} %get-tuple-element.63), channel_id=1, source_target_pairs={{0,1},{1,0},{2,3},{3,2},{4,5},{5,4},{6,7},{7,6},{8,9},{9,8},{10,11... | collective-permute-start | bytes 786440 | tf_op jit(solution)/shard_map/ppermute | solution.py:247
  55.0 14.3 %collective-permute-start.10 = (f32[2,8,32,128]{3,2,1,0:T(8,128)S(1)}, f32[2,8,32,128]{3,2,1,0:T(8,128)S(1)}, u32[]{:S(2)}, u32[]{:S(2)}) collective-permute-start(f32[2,8,32,128]{3,2,1,0:T(8,128)S(1)} %get-tuple-element.55), channel_id=1, source_target_pairs={{0,3},{1,2},{2,1},{3,0},{4,7},{5,6},{6,5},{7,4},{8,11},{9,10},{10,... | collective-permute-start | bytes 786440 | tf_op jit(solution)/shard_map/ppermute | solution.py:247
  55.1 17.1 %collective-permute-start.11 = (f32[2,8,32,128]{3,2,1,0:T(8,128)S(1)}, f32[2,8,32,128]{3,2,1,0:T(8,128)S(1)}, u32[]{:S(2)}, u32[]{:S(2)}) collective-permute-start(f32[2,8,32,128]{3,2,1,0:T(8,128)S(1)} %get-tuple-element.56), channel_id=1, source_target_pairs={{0,2},{1,3},{2,0},{3,1},{4,6},{5,7},{6,4},{7,5},{8,10},{9,11},{10,... | collective-permute-start | bytes 786440 | tf_op jit(solution)/shard_map/ppermute | solution.py:247
  58.2 14.0 %collective-permute-start.12 = (f32[2,8,32,128]{3,2,1,0:T(8,128)S(1)}, f32[2,8,32,128]{3,2,1,0:T(8,128)S(1)}, u32[]{:S(2)}, u32[]{:S(2)}) collective-permute-start(f32[2,8,32,128]{3,2,1,0:T(8,128)S(1)} %get-tuple-element.57), channel_id=1, source_target_pairs={{0,1},{1,0},{2,3},{3,2},{4,5},{5,4},{6,7},{7,6},{8,9},{9,8},{10,11... | collective-permute-start | bytes 786440 | tf_op jit(solution)/shard_map/ppermute | solution.py:247

commit v6 on v5

--- a/solution.py
+++ b/solution.py
@@ -112,18 +112,20 @@
 
 def offer_kernel(info, total, across, *refs):
     out = refs[-1]
-    upper = info[2] > 0
-    whole = 1 - info[1]
-    other = info[1]
-    send = jnp.logical_xor(upper, whole == 0)
-    out[other] = total[other]
-    out[whole] = across[...] + jnp.where(send, total[whole], 0.0)
+    node, upper = info[1], jnp.where(info[2] > 0, 1, 0)
+    half = out.shape[1]
+    for j in range(2):
+        heads = slice(j * half, (j + 1) * half)
+        out[j] = total[upper, heads] + jnp.where(node != upper, across[heads], 0.0)
+    heads = pl.ds(node * half, half)
+    out[2] = jnp.where(node == upper, across[heads], total[1 - upper, heads])
 
 
 def offer(info, total, across, behind):
+    heads = total.shape[1]
     return pl.pallas_call(
         offer_kernel,
-        out_shape=jax.ShapeDtypeStruct(total.shape, F32),
+        out_shape=jax.ShapeDtypeStruct((3, heads // 2, *total.shape[2:]), F32),
         in_specs=[SCALARS, WHOLE, WHOLE] + [LEFT] * len(behind),
         out_specs=WHOLE,
         compiler_params=pltpu.CompilerParams(vmem_limit_bytes=VMEM_LIMIT),
@@ -131,24 +133,32 @@
 
 
 def spread_kernel(pair, info, *refs):
-    pieces, given, outs = refs[:PARTS], refs[PARTS : PARTS + 1 + pair], refs[-PARTS:]
-    mine, node, upper = info[0], info[1], info[2] > 0
-    if pair:
-        across, other = given
-        late = node > 0
-        prefix = jnp.where(late, across[...], 0.0) + jnp.where(late | upper, other[0], 0.0)
-        suffix = jnp.where(late, 0.0, across[...]) + jnp.where(late & upper, 0.0, other[1])
-    else:
-        prefix, suffix = given[0][0], given[0][1]
-    for r in range(PARTS):
-        before, after = prefix, suffix
-        for other in range(PARTS):
-            if other != r:
-                earlier = (mine ^ other) < (mine ^ r)
-                before = before + jnp.where(earlier, pieces[other][0], 0.0)
-                after = after + jnp.where(earlier, 0.0, pieces[other][1])
-        outs[r][0] = before
-        outs[r][1] = after
+    count = 3 if pair else 1
+    pieces, given, outs = refs[:PARTS], refs[PARTS : PARTS + count], refs[-PARTS:]
+    mine, node, upper = info[0], info[1], jnp.where(info[2] > 0, 1, 0)
+    half = pieces[0].shape[1] // 2
+    for j in range(2):
+        heads = slice(j * half, (j + 1) * half)
+        if pair:
+            across, here, there = given
+            alone = node != upper
+            main = here[j]
+            extra = jnp.where(node == j, here[2], there[2])
+            whole = across[heads] + jnp.where(alone, extra, main)
+            part = jnp.where(alone, main, 0.0)
+            prefix = jnp.where(node > 0, whole, part)
+            suffix = jnp.where(node > 0, part, whole)
+        else:
+            prefix, suffix = given[0][0, heads], given[0][1, heads]
+        for r in range(PARTS):
+            before, after = prefix, suffix
+            for other in range(PARTS):
+                if other != r:
+                    earlier = (mine ^ other) < (mine ^ r)
+                    before = before + jnp.where(earlier, pieces[other][0, heads], 0.0)
+                    after = after + jnp.where(earlier, 0.0, pieces[other][1, heads])
+            outs[r][0, heads] = before
+            outs[r][1, heads] = after
 
 
 def spread(info, pieces, given, behind):
@@ -278,7 +288,8 @@
             total, across = state[i]
             if blocks == 2:
                 last = offer(info, total, across, behind)
-                given[i] = [across, swap(last, size, PARTS)]
+                other = swap(last, size, PARTS)
+                given[i] = [across, other, lax.ppermute(other, "node", [(0, 1), (1, 0)])]
             else:
                 given[i] = [sums_outside(total, node, place_in // PARTS, blocks)]
         elif stage == "spread":

time: 74.8 us -> 74.2 us (level)
  waiting for transfers between devices: 28.2 us -> 25.6 us
  starting transfers between devices: 21.4 us -> 23.5 us
    ppermute x14, waiting for transfers between devices: 25.5 us -> 23.4 us  [swap(): return lax.ppermute(array, 'local', [(i, i ^ mask) for i in range(size)])]
    ppermute x14, starting transfers between devices: 21.3 us -> 22.9 us  [swap(): return lax.ppermute(array, 'local', [(i, i ^ mask) for i in range(size)])]
  transfers between devices with their start and end apart: 16 -> 18, of which waited for: 8 -> 8; matrix products, arithmetic and copies ran while one was open for 0% -> 0% of each run, Pallas kernels for 22% -> 22%
where the time goes in v6:
time: 74.2 us; the launch traced here: 74 us
  waiting for transfers between devices  25.6 us (35%)
  starting transfers between devices  23.5 us (32%)
  Pallas kernels  21.8 us (29%)
  local copies, waits for them, and re-layouts  1.59 us (2%)
  between operations  0.83 us (1%)
    ppermute x14, waiting for transfers between devices, swap(): return lax.ppermute(array, 'local', [(i, i ^ mask) for i in range(size)])  23.4 us
    ppermute x14, starting transfers between devices, swap(): return lax.ppermute(array, 'local', [(i, i ^ mask) for i in range(size)])  22.9 us
    pallas_call x2, Pallas kernels, states(): pl.pallas_call(functools.partial(state_kernel, first, heads), out_shape=[...  7.27 us
    pallas_call x2, Pallas kernels, inner(): pl.pallas_call(functools.partial(inner_kernel, first, step), out_shape=[j...  5.78 us
    pallas_call x2, Pallas kernels, finish(): pl.pallas_call(functools.partial(finish_kernel, first, step, factor), out...  4.77 us
    ppermute x2, waiting for transfers between devices, local(): across = lax.ppermute(halves, 'node', [(0, 1), (1, 0)])  2.17 us
    pallas_call x2, Pallas kernels, spread(): pl.pallas_call(functools.partial(spread_kernel, len(given) > 1), out_shap...  1.61 us
    unnamed x16, local copies, waits for them, and re-layouts  1.59 us
  transfers between devices with their start and end apart: 18, of which 8 were waited for; matrix products, arithmetic and copies ran while one was open for 0% of the time, Pallas kernels for 22%

profile of v6, /device:TPU:0, one launch (start us, length us, event | category | flops | bytes accessed | tf_op | source)
XLA Modules:
  0.0 74.0 jit_solution(12004117682672818865)
XLA Ops:
  0.7 0.7 pad_add_fusion.info.refs_0_
  1.3 3.5 %shard_map.75 = (f32[2,8,32,128]{3,2,1,0:T(8,128)}, f32[2,8,32,128]{3,2,1,0:T(8,128)}, f32[2,8,32,128]{3,2,1,0:T(8,128)}, f32[2,8,32,128]{3,2,1,0:T(8,128)}) custom-call(s32[3]{0:T(128)} %pad_add_fusion.info.refs_0_, bf16[192,2048]{1,0:T(8,128)(2,1)} %q.11, bf16[192,2048]{1,0:T(8,128)(2,1)} %k.11, bf16[192,2048]{1,0:T(8,128)(2,1)} %v.11, ...), custom_call_target="tpu_custom_call" | custom-call | tf_op jit(solution)/shard_map/pallas_call | solution.py:82
  4.8 4.1 %collective-permute-start = (f32[2,8,32,128]{3,2,1,0:T(8,128)}, f32[2,8,32,128]{3,2,1,0:T(8,128)S(1)}, u32[]{:S(2)}, u32[]{:S(2)}) collective-permute-start(f32[2,8,32,128]{3,2,1,0:T(8,128)} %get-tuple-element.37), channel_id=1, source_target_pairs={{0,3},{1,2},{2,1},{3,0},{4,7},{5,6},{6,5},{7,4},{8,11},{9,10},{10,... | collective-permute-start | bytes 786440 | tf_op jit(solution)/shard_map/ppermute | solution.py:257
  8.9 0.4 collective-permute-start.1
  9.3 0.2 collective-permute-start.2
  9.5 0.0 copy-start
  9.5 0.0 copy-start.1
  9.5 0.0 copy-start.2
  9.5 0.0 copy-start.3
  9.5 3.8 %shard_map.76 = (f32[2,8,32,128]{3,2,1,0:T(8,128)}, f32[2,8,32,128]{3,2,1,0:T(8,128)}, f32[2,8,32,128]{3,2,1,0:T(8,128)}, f32[2,8,32,128]{3,2,1,0:T(8,128)}) custom-call(s32[3]{0:T(128)} %pad_add_fusion.info.refs_0_, bf16[192,2048]{1,0:T(8,128)(2,1)} %q.11, bf16[192,2048]{1,0:T(8,128)(2,1)} %k.11, bf16[192,2048]{1,0:T(8,128)(2,1)} %v.11, ...), custom_call_target="tpu_custom_call" | custom-call | tf_op jit(solution)/shard_map/pallas_call | solution.py:82
  13.3 1.9 %collective-permute-start.4 = (f32[2,8,32,128]{3,2,1,0:T(8,128)}, f32[2,8,32,128]{3,2,1,0:T(8,128)S(1)}, u32[]{:S(2)}, u32[]{:S(2)}) collective-permute-start(f32[2,8,32,128]{3,2,1,0:T(8,128)} %get-tuple-element.48), channel_id=1, source_target_pairs={{0,1},{1,0},{2,3},{3,2},{4,5},{5,4},{6,7},{7,6},{8,9},{9,8},{10,11... | collective-permute-start | bytes 786440 | tf_op jit(solution)/shard_map/ppermute | solution.py:257
  15.2 1.6 %collective-permute-start.5 = (f32[2,8,32,128]{3,2,1,0:T(8,128)}, f32[2,8,32,128]{3,2,1,0:T(8,128)S(1)}, u32[]{:S(2)}, u32[]{:S(2)}) collective-permute-start(f32[2,8,32,128]{3,2,1,0:T(8,128)} %get-tuple-element.49), channel_id=1, source_target_pairs={{0,2},{1,3},{2,0},{3,1},{4,6},{5,7},{6,4},{7,5},{8,10},{9,11},{10,... | collective-permute-start | bytes 786440 | tf_op jit(solution)/shard_map/ppermute | solution.py:257
  16.8 0.0 collective-permute-done.b.refs_3_
  16.8 2.4 %collective-permute-start.6 = (f32[2,8,32,128]{3,2,1,0:T(8,128)}, f32[2,8,32,128]{3,2,1,0:T(8,128)S(1)}, u32[]{:S(2)}, u32[]{:S(2)}) collective-permute-start(f32[2,8,32,128]{3,2,1,0:T(8,128)} %get-tuple-element.50), channel_id=1, source_target_pairs={{0,3},{1,2},{2,1},{3,0},{4,7},{5,6},{6,5},{7,4},{8,11},{9,10},{10,... | collective-permute-start | bytes 786440 | tf_op jit(solution)/shard_map/ppermute | solution.py:257
  19.2 0.0 copy-done
  19.2 0.0 copy-done.1
  19.2 0.0 copy-done.2
  19.2 0.0 copy-done.3
  19.2 0.0 copy-start.5
  19.2 0.9 %copy-done.5 = f32[2,8,32,128]{3,2,1,0:T(8,128)S(1)} copy-done((f32[2,8,32,128]{3,2,1,0:T(8,128)S(1)}, f32[2,8,32,128]{3,2,1,0:T(8,128)}, u32[]{:S(2)}) %copy-start.5) | copy-done | bytes 262168
  20.2 2.9 %shard_map.77 = (f32[192,1024]{1,0:T(8,128)S(1)}, f32[192,1024]{1,0:T(8,128)S(1)}, f32[192,1024]{1,0:T(8,128)S(1)}, f32[192,1024]{1,0:T(8,128)S(1)}) custom-call(bf16[192,2048]{1,0:T(8,128)(2,1)S(1)} %copy-done, bf16[192,2048]{1,0:T(8,128)(2,1)S(1)} %copy-done.1, bf16[192,2048]{1,0:T(8,128)(2,1)S(1)} %copy-done.2, bf16[192,2048]{1,0:T(8,128)(2,1)S(1)} %copy-done.3, ...), custom_call_target="tpu_custom_call" | custom-call | tf_op jit(solution)/shard_map/pallas_call | solution.py:207
  23.1 0.0 copy-start.7
  23.1 0.0 collective-permute-done.1.c.refs_2_
  23.1 0.0 collective-permute-done.2.d.refs_1_
  23.1 0.0 copy-done.4
  23.1 0.6 copy-done.7
  23.8 0.6 shard_map.78
  24.4 0.1 collective-permute-start.3
  24.5 1.3 %collective-permute-done.3.across.refs_4_ = f32[8,32,128]{2,1,0:T(8,128)S(1)} collective-permute-done((f32[8,32,128]{2,1,0:T(8,128)S(1)}, f32[8,32,128]{2,1,0:T(8,128)S(1)}, u32[]{:S(2)}, u32[]{:S(2)}) %collective-permute-start.3) | collective-permute-done | bytes 131104 | tf_op jit(solution)/shard_map/ppermute | solution.py:285
  25.8 0.6 shard_map.79.refs_0_
  26.4 0.0 copy-start.6
  26.4 2.7 %collective-permute-start.10 = (f32[3,4,32,128]{3,2,1,0:T(8,128)S(1)}, f32[3,4,32,128]{3,2,1,0:T(8,128)S(1)}, u32[]{:S(2)}, u32[]{:S(2)}) collective-permute-start(f32[3,4,32,128]{3,2,1,0:T(8,128)S(1)} %shard_map.79.refs_0_), channel_id=1, source_target_pairs={{0,4},{1,5},{2,6},{3,7},{4,0},{5,1},{6,2},{7,3},{8,12},{9,13},{10,... | collective-permute-start | bytes 589832 | tf_op jit(solution)/shard_map/ppermute | solution.py:257
  29.0 2.9 %shard_map.80 = (f32[192,1024]{1,0:T(8,128)S(1)}, f32[192,1024]{1,0:T(8,128)S(1)}, f32[192,1024]{1,0:T(8,128)S(1)}, f32[192,1024]{1,0:T(8,128)S(1)}) custom-call(bf16[192,2048]{1,0:T(8,128)(2,1)S(1)} %copy-done, bf16[192,2048]{1,0:T(8,128)(2,1)S(1)} %copy-done.1, bf16[192,2048]{1,0:T(8,128)(2,1)S(1)} %copy-done.2, bf16[192,2048]{1,0:T(8,128)(2,1)S(1)} %copy-done.3, ...), custom_call_target="tpu_custom_call" | custom-call | tf_op jit(solution)/shard_map/pallas_call | solution.py:207
  31.9 0.0 collective-permute-done.4.d.refs_1_
  31.9 0.0 collective-permute-done.5.c.refs_2_
  31.9 4.5 %collective-permute-done.6.b.refs_3_ = f32[2,8,32,128]{3,2,1,0:T(8,128)S(1)} collective-permute-done((f32[2,8,32,128]{3,2,1,0:T(8,128)}, f32[2,8,32,128]{3,2,1,0:T(8,128)S(1)}, u32[]{:S(2)}, u32[]{:S(2)}) %collective-permute-start.6) | collective-permute-done | bytes 262176 | tf_op jit(solution)/shard_map/ppermute | solution.py:257
  36.5 0.0 copy-done.6
  36.5 0.6 shard_map.81
  37.1 0.1 collective-permute-start.7
  37.2 0.0 collective-permute-done.10.refs_5_
  37.2 0.5 collective-permute-start.11
  37.7 0.8 %collective-permute-done.7.across.refs_4_ = f32[8,32,128]{2,1,0:T(8,128)S(1)} collective-permute-done((f32[8,32,128]{2,1,0:T(8,128)S(1)}, f32[8,32,128]{2,1,0:T(8,128)S(1)}, u32[]{:S(2)}, u32[]{:S(2)}) %collective-permute-start.7) | collective-permute-done | bytes 131104 | tf_op jit(solution)/shard_map/ppermute | solution.py:285
  38.5 0.6 shard_map.82.refs_7_
  39.1 1.1 %collective-permute-start.8 = (f32[3,4,32,128]{3,2,1,0:T(8,128)S(1)}, f32[3,4,32,128]{3,2,1,0:T(8,128)S(1)}, u32[]{:S(2)}, u32[]{:S(2)}) collective-permute-start(f32[3,4,32,128]{3,2,1,0:T(8,128)S(1)} %shard_map.82.refs_7_), channel_id=1, source_target_pairs={{0,4},{1,5},{2,6},{3,7},{4,0},{5,1},{6,2},{7,3},{8,12},{9,13},{10,... | collective-permute-start | bytes 589832 | tf_op jit(solution)/shard_map/ppermute | solution.py:257
  40.2 0.0 collective-permute-done.11.refs_6_
  40.2 0.8 %shard_map.83 = (f32[2,8,32,128]{3,2,1,0:T(8,128)S(1)}, f32[2,8,32,128]{3,2,1,0:T(8,128)S(1)}, f32[2,8,32,128]{3,2,1,0:T(8,128)S(1)}, f32[2,8,32,128]{3,2,1,0:T(8,128)S(1)}) custom-call(s32[3]{0:T(128)S(1)} %copy-done.7, f32[2,8,32,128]{3,2,1,0:T(8,128)S(1)} %copy-done.4, f32[2,8,32,128]{3,2,1,0:T(8,128)S(1)} %collective-permute-done.2.d.refs_1_, ...), custom_call_target="tpu_custom_call" | custom-call | tf_op jit(solution)/shard_map/pallas_call | solution.py:165
  41.0 3.3 %collective-permute-start.15 = (f32[2,8,32,128]{3,2,1,0:T(8,128)S(1)}, f32[2,8,32,128]{3,2,1,0:T(8,128)S(1)}, u32[]{:S(2)}, u32[]{:S(2)}) collective-permute-start(f32[2,8,32,128]{3,2,1,0:T(8,128)S(1)} %get-tuple-element.61), channel_id=1, source_target_pairs={{0,3},{1,2},{2,1},{3,0},{4,7},{5,6},{6,5},{7,4},{8,11},{9,10},{10,... | collective-permute-start | bytes 786440 | tf_op jit(solution)/shard_map/ppermute | solution.py:257
  44.4 7.0 %collective-permute-done.8.refs_5_ = f32[3,4,32,128]{3,2,1,0:T(8,128)S(1)} collective-permute-done((f32[3,4,32,128]{3,2,1,0:T(8,128)S(1)}, f32[3,4,32,128]{3,2,1,0:T(8,128)S(1)}, u32[]{:S(2)}, u32[]{:S(2)}) %collective-permute-start.8) | collective-permute-done | bytes 196640 | tf_op jit(solution)/shard_map/ppermute | solution.py:257
  51.3 0.0 collective-permute-start.9
  51.3 0.0 collective-permute-start.16
  51.3 1.6 %collective-permute-start.17 = (f32[2,8,32,128]{3,2,1,0:T(8,128)S(1)}, f32[2,8,32,128]{3,2,1,0:T(8,128)S(1)}, u32[]{:S(2)}, u32[]{:S(2)}) collective-permute-start(f32[2,8,32,128]{3,2,1,0:T(8,128)S(1)} %get-tuple-element.63), channel_id=1, source_target_pairs={{0,1},{1,0},{2,3},{3,2},{4,5},{5,4},{6,7},{7,6},{8,9},{9,8},{10,11... | collective-permute-start | bytes 786440 | tf_op jit(solution)/shard_map/ppermute | solution.py:257
  53.0 0.0 collective-permute-done.9.refs_6_
  53.0 0.8 %shard_map.84 = (f32[2,8,32,128]{3,2,1,0:T(8,128)S(1)}, f32[2,8,32,128]{3,2,1,0:T(8,128)S(1)}, f32[2,8,32,128]{3,2,1,0:T(8,128)S(1)}, f32[2,8,32,128]{3,2,1,0:T(8,128)S(1)}) custom-call(s32[3]{0:T(128)S(1)} %copy-done.7, f32[2,8,32,128]{3,2,1,0:T(8,128)S(1)} %copy-done.6, f32[2,8,32,128]{3,2,1,0:T(8,128)S(1)} %collective-permute-done.4.d.refs_1_, ...), custom_call_target="tpu_custom_call" | custom-call | tf_op jit(solution)/shard_map/pallas_call | solution.py:165
  53.8 1.9 %collective-permute-start.12 = (f32[2,8,32,128]{3,2,1,0:T(8,128)S(1)}, f32[2,8,32,128]{3,2,1,0:T(8,128)S(1)}, u32[]{:S(2)}, u32[]{:S(2)}) collective-permute-start(f32[2,8,32,128]{3,2,1,0:T(8,128)S(1)} %get-tuple-element.55), channel_id=1, source_target_pairs={{0,3},{1,2},{2,1},{3,0},{4,7},{5,6},{6,5},{7,4},{8,11},{9,10},{10,... | collective-permute-start | bytes 786440 | tf_op jit(solution)/shard_map/ppermute | solution.py:257
  55.7 1.0 %collective-permute-start.13 = (f32[2,8,32,128]{3,2,1,0:T(8,128)S(1)}, f32[2,8,32,128]{3,2,1,0:T(8,128)S(1)}, u32[]{:S(2)}, u32[]{:S(2)}) collective-permute-start(f32[2,8,32,128]{3,2,1,0:T(8,128)S(1)} %get-tuple-element.56), channel_id=1, source_target_pairs={{0,2},{1,3},{2,0},{3,1},{4,6},{5,7},{6,4},{7,5},{8,10},{9,11},{10,... | collective-permute-start | bytes 786440 | tf_op jit(solution)/shard_map/ppermute | solution.py:257
  56.7 0.0 collective-permute-done.15.refs_5_
  56.7 0.6 collective-permute-start.14
  57.3 3.1 %collective-permute-done.16.refs_6_ = f32[2,8,32,128]{3,2,1,0:T(8,128)S(1)} collective-permute-done((f32[2,8,32,128]{3,2,1,0:T(8,128)S(1)}, f32[2,8,32,128]{3,2,1,0:T(8,128)S(1)}, u32[]{:S(2)}, u32[]{:S(2)}) %collective-permute-start.16) | collective-permute-done | bytes 262176 | tf_op jit(solution)/shard_map/ppermute | solution.py:257
  60.4 4.4 %collective-permute-done.17.refs_7_ = f32[2,8,32,128]{3,2,1,0:T(8,128)S(1)} collective-permute-done((f32[2,8,32,128]{3,2,1,0:T(8,128)S(1)}, f32[2,8,32,128]{3,2,1,0:T(8,128)S(1)}, u32[]{:S(2)}, u32[]{:S(2)}) %collective-permute-start.17) | collective-permute-done | bytes 262176 | tf_op jit(solution)/shard_map/ppermute | solution.py:257
  64.8 2.4 %shard_map.85 = (bf16[192,2048]{1,0:T(8,128)(2,1)}, bf16[192,2048]{1,0:T(8,128)(2,1)}, bf16[192,2048]{1,0:T(8,128)(2,1)}, bf16[192,2048]{1,0:T(8,128)(2,1)}) custom-call(s32[3]{0:T(128)S(1)} %copy-done.7, bf16[192,2048]{1,0:T(8,128)(2,1)S(1)} %copy-done, bf16[192,2048]{1,0:T(8,128)(2,1)S(1)} %copy-done.1, bf16[192,2048]{1,0:T(8,128)(2,1)S(1)} %copy-done.2, ...), custom_call_target="tpu_custom_call" | custom-call | tf_op jit(solution)/shard_map/pallas_call | solution.py:244
  67.2 0.0 collective-permute-done.12.refs_5_
  67.2 4.1 %collective-permute-done.13.refs_6_ = f32[2,8,32,128]{3,2,1,0:T(8,128)S(1)} collective-permute-done((f32[2,8,32,128]{3,2,1,0:T(8,128)S(1)}, f32[2,8,32,128]{3,2,1,0:T(8,128)S(1)}, u32[]{:S(2)}, u32[]{:S(2)}) %collective-permute-start.13) | collective-permute-done | bytes 262176 | tf_op jit(solution)/shard_map/ppermute | solution.py:257
  71.3 0.3 collective-permute-done.14.refs_7_
  71.6 2.4 %shard_map.86 = (bf16[192,2048]{1,0:T(8,128)(2,1)}, bf16[192,2048]{1,0:T(8,128)(2,1)}, bf16[192,2048]{1,0:T(8,128)(2,1)}, bf16[192,2048]{1,0:T(8,128)(2,1)}) custom-call(s32[3]{0:T(128)S(1)} %copy-done.7, bf16[192,2048]{1,0:T(8,128)(2,1)S(1)} %copy-done, ...), custom_call_target="tpu_custom_call", output_to_operand_aliasing={{0}: (13, {}), {1}: (14, {}), {2}: (15, {}), {3}: (16, {})} | custom-call | tf_op jit(solution)/shard_map/pallas_call | solution.py:244
  (1 shorter events, 0.0 us)
Async XLA Ops:
  4.8 12.0 %collective-permute-start = (f32[2,8,32,128]{3,2,1,0:T(8,128)}, f32[2,8,32,128]{3,2,1,0:T(8,128)S(1)}, u32[]{:S(2)}, u32[]{:S(2)}) collective-permute-start(f32[2,8,32,128]{3,2,1,0:T(8,128)} %get-tuple-element.37), channel_id=1, source_target_pairs={{0,3},{1,2},{2,1},{3,0},{4,7},{5,6},{6,5},{7,4},{8,11},{9,10},{10,... | collective-permute-start | bytes 786440 | tf_op jit(solution)/shard_map/ppermute | solution.py:257
  8.9 14.2 %collective-permute-start.1 = (f32[2,8,32,128]{3,2,1,0:T(8,128)}, f32[2,8,32,128]{3,2,1,0:T(8,128)S(1)}, u32[]{:S(2)}, u32[]{:S(2)}) collective-permute-start(f32[2,8,32,128]{3,2,1,0:T(8,128)} %get-tuple-element.38), channel_id=1, source_target_pairs={{0,2},{1,3},{2,0},{3,1},{4,6},{5,7},{6,4},{7,5},{8,10},{9,11},{10,... | collective-permute-start | bytes 786440 | tf_op jit(solution)/shard_map/ppermute | solution.py:257
  9.3 13.8 %collective-permute-start.2 = (f32[2,8,32,128]{3,2,1,0:T(8,128)}, f32[2,8,32,128]{3,2,1,0:T(8,128)S(1)}, u32[]{:S(2)}, u32[]{:S(2)}) collective-permute-start(f32[2,8,32,128]{3,2,1,0:T(8,128)} %get-tuple-element.39), channel_id=1, source_target_pairs={{0,1},{1,0},{2,3},{3,2},{4,5},{5,4},{6,7},{7,6},{8,9},{9,8},{10,11... | collective-permute-start | bytes 786440 | tf_op jit(solution)/shard_map/ppermute | solution.py:257
  9.5 9.7 %copy-start = (bf16[192,2048]{1,0:T(8,128)(2,1)S(1)}, bf16[192,2048]{1,0:T(8,128)(2,1)}, u32[]{:S(2)}) copy-start(bf16[192,2048]{1,0:T(8,128)(2,1)} %q.11) | copy-start | bytes 2359300
  9.5 9.7 %copy-start.1 = (bf16[192,2048]{1,0:T(8,128)(2,1)S(1)}, bf16[192,2048]{1,0:T(8,128)(2,1)}, u32[]{:S(2)}) copy-start(bf16[192,2048]{1,0:T(8,128)(2,1)} %k.11) | copy-start | bytes 2359300
  9.5 9.7 %copy-start.2 = (bf16[192,2048]{1,0:T(8,128)(2,1)S(1)}, bf16[192,2048]{1,0:T(8,128)(2,1)}, u32[]{:S(2)}) copy-start(bf16[192,2048]{1,0:T(8,128)(2,1)} %v.11) | copy-start | bytes 2359300
  9.5 9.7 %copy-start.3 = (bf16[192,2048]{1,0:T(8,128)(2,1)S(1)}, bf16[192,2048]{1,0:T(8,128)(2,1)}, u32[]{:S(2)}) copy-start(bf16[192,2048]{1,0:T(8,128)(2,1)} %g.11) | copy-start | bytes 2359300
  13.3 18.6 %collective-permute-start.4 = (f32[2,8,32,128]{3,2,1,0:T(8,128)}, f32[2,8,32,128]{3,2,1,0:T(8,128)S(1)}, u32[]{:S(2)}, u32[]{:S(2)}) collective-permute-start(f32[2,8,32,128]{3,2,1,0:T(8,128)} %get-tuple-element.48), channel_id=1, source_target_pairs={{0,1},{1,0},{2,3},{3,2},{4,5},{5,4},{6,7},{7,6},{8,9},{9,8},{10,11... | collective-permute-start | bytes 786440 | tf_op jit(solution)/shard_map/ppermute | solution.py:257
  15.2 16.7 %collective-permute-start.5 = (f32[2,8,32,128]{3,2,1,0:T(8,128)}, f32[2,8,32,128]{3,2,1,0:T(8,128)S(1)}, u32[]{:S(2)}, u32[]{:S(2)}) collective-permute-start(f32[2,8,32,128]{3,2,1,0:T(8,128)} %get-tuple-element.49), channel_id=1, source_target_pairs={{0,2},{1,3},{2,0},{3,1},{4,6},{5,7},{6,4},{7,5},{8,10},{9,11},{10,... | collective-permute-start | bytes 786440 | tf_op jit(solution)/shard_map/ppermute | solution.py:257
  16.8 19.7 %collective-permute-start.6 = (f32[2,8,32,128]{3,2,1,0:T(8,128)}, f32[2,8,32,128]{3,2,1,0:T(8,128)S(1)}, u32[]{:S(2)}, u32[]{:S(2)}) collective-permute-start(f32[2,8,32,128]{3,2,1,0:T(8,128)} %get-tuple-element.50), channel_id=1, source_target_pairs={{0,3},{1,2},{2,1},{3,0},{4,7},{5,6},{6,5},{7,4},{8,11},{9,10},{10,... | collective-permute-start | bytes 786440 | tf_op jit(solution)/shard_map/ppermute | solution.py:257
  19.2 1.0 %copy-start.5 = (f32[2,8,32,128]{3,2,1,0:T(8,128)S(1)}, f32[2,8,32,128]{3,2,1,0:T(8,128)}, u32[]{:S(2)}) copy-start(f32[2,8,32,128]{3,2,1,0:T(8,128)} %get-tuple-element.40.refs_0_.a) | copy-start | bytes 786436
  20.2 2.9 %copy-start.4 = (f32[2,8,32,128]{3,2,1,0:T(8,128)S(1)}, f32[2,8,32,128]{3,2,1,0:T(8,128)}, u32[]{:S(2)}) copy-start(f32[2,8,32,128]{3,2,1,0:T(8,128)} %get-tuple-element.36.refs_0_.a) | copy-start | bytes 786436
  23.1 0.7 copy-start.7
  24.4 1.4 %collective-permute-start.3 = (f32[8,32,128]{2,1,0:T(8,128)S(1)}, f32[8,32,128]{2,1,0:T(8,128)S(1)}, u32[]{:S(2)}, u32[]{:S(2)}) collective-permute-start(f32[8,32,128]{2,1,0:T(8,128)S(1)} %get-tuple-element.43), channel_id=1, source_target_pairs={{0,8},{8,0},{1,9},{9,1},{2,10},{10,2},{3,11},{11,3},{4,12},{12,4},... | collective-permute-start | bytes 393224 | tf_op jit(solution)/shard_map/ppermute | solution.py:285
  26.4 10.1 %copy-start.6 = (f32[2,8,32,128]{3,2,1,0:T(8,128)S(1)}, f32[2,8,32,128]{3,2,1,0:T(8,128)}, u32[]{:S(2)}) copy-start(f32[2,8,32,128]{3,2,1,0:T(8,128)} %get-tuple-element.40.refs_0_.a) | copy-start | bytes 786436
  26.4 10.8 %collective-permute-start.10 = (f32[3,4,32,128]{3,2,1,0:T(8,128)S(1)}, f32[3,4,32,128]{3,2,1,0:T(8,128)S(1)}, u32[]{:S(2)}, u32[]{:S(2)}) collective-permute-start(f32[3,4,32,128]{3,2,1,0:T(8,128)S(1)} %shard_map.79.refs_0_), channel_id=1, source_target_pairs={{0,4},{1,5},{2,6},{3,7},{4,0},{5,1},{6,2},{7,3},{8,12},{9,13},{10,... | collective-permute-start | bytes 589832 | tf_op jit(solution)/shard_map/ppermute | solution.py:257
  37.1 1.4 %collective-permute-start.7 = (f32[8,32,128]{2,1,0:T(8,128)S(1)}, f32[8,32,128]{2,1,0:T(8,128)S(1)}, u32[]{:S(2)}, u32[]{:S(2)}) collective-permute-start(f32[8,32,128]{2,1,0:T(8,128)S(1)} %get-tuple-element.51), channel_id=1, source_target_pairs={{0,8},{8,0},{1,9},{9,1},{2,10},{10,2},{3,11},{11,3},{4,12},{12,4},... | collective-permute-start | bytes 393224 | tf_op jit(solution)/shard_map/ppermute | solution.py:285
  37.2 3.0 %collective-permute-start.11 = (f32[3,4,32,128]{3,2,1,0:T(8,128)S(1)}, f32[3,4,32,128]{3,2,1,0:T(8,128)S(1)}, u32[]{:S(2)}, u32[]{:S(2)}) collective-permute-start(f32[3,4,32,128]{3,2,1,0:T(8,128)S(1)} %collective-permute-done.10.refs_5_), channel_id=1, source_target_pairs={{0,8},{8,0},{1,9},{9,1},{2,10},{10,2},{3,11},{11,3},{4,12},{12,4},... | collective-permute-start | bytes 589832 | tf_op jit(solution)/shard_map/ppermute | solution.py:292
  39.1 12.2 %collective-permute-start.8 = (f32[3,4,32,128]{3,2,1,0:T(8,128)S(1)}, f32[3,4,32,128]{3,2,1,0:T(8,128)S(1)}, u32[]{:S(2)}, u32[]{:S(2)}) collective-permute-start(f32[3,4,32,128]{3,2,1,0:T(8,128)S(1)} %shard_map.82.refs_7_), channel_id=1, source_target_pairs={{0,4},{1,5},{2,6},{3,7},{4,0},{5,1},{6,2},{7,3},{8,12},{9,13},{10,... | collective-permute-start | bytes 589832 | tf_op jit(solution)/shard_map/ppermute | solution.py:257
  41.0 15.7 %collective-permute-start.15 = (f32[2,8,32,128]{3,2,1,0:T(8,128)S(1)}, f32[2,8,32,128]{3,2,1,0:T(8,128)S(1)}, u32[]{:S(2)}, u32[]{:S(2)}) collective-permute-start(f32[2,8,32,128]{3,2,1,0:T(8,128)S(1)} %get-tuple-element.61), channel_id=1, source_target_pairs={{0,3},{1,2},{2,1},{3,0},{4,7},{5,6},{6,5},{7,4},{8,11},{9,10},{10,... | collective-permute-start | bytes 786440 | tf_op jit(solution)/shard_map/ppermute | solution.py:257
  51.3 1.6 %collective-permute-start.9 = (f32[3,4,32,128]{3,2,1,0:T(8,128)S(1)}, f32[3,4,32,128]{3,2,1,0:T(8,128)S(1)}, u32[]{:S(2)}, u32[]{:S(2)}) collective-permute-start(f32[3,4,32,128]{3,2,1,0:T(8,128)S(1)} %collective-permute-done.8.refs_5_), channel_id=1, source_target_pairs={{0,8},{8,0},{1,9},{9,1},{2,10},{10,2},{3,11},{11,3},{4,12},{12,4},... | collective-permute-start | bytes 589832 | tf_op jit(solution)/shard_map/ppermute | solution.py:292
  51.3 9.1 %collective-permute-start.16 = (f32[2,8,32,128]{3,2,1,0:T(8,128)S(1)}, f32[2,8,32,128]{3,2,1,0:T(8,128)S(1)}, u32[]{:S(2)}, u32[]{:S(2)}) collective-permute-start(f32[2,8,32,128]{3,2,1,0:T(8,128)S(1)} %get-tuple-element.62), channel_id=1, source_target_pairs={{0,2},{1,3},{2,0},{3,1},{4,6},{5,7},{6,4},{7,5},{8,10},{9,11},{10,... | collective-permute-start | bytes 786440 | tf_op jit(solution)/shard_map/ppermute | solution.py:257
  51.3 13.5 %collective-permute-start.17 = (f32[2,8,32,128]{3,2,1,0:T(8,128)S(1)}, f32[2,8,32,128]{3,2,1,0:T(8,128)S(1)}, u32[]{:S(2)}, u32[]{:S(2)}) collective-permute-start(f32[2,8,32,128]{3,2,1,0:T(8,128)S(1)} %get-tuple-element.63), channel_id=1, source_target_pairs={{0,1},{1,0},{2,3},{3,2},{4,5},{5,4},{6,7},{7,6},{8,9},{9,8},{10,11... | collective-permute-start | bytes 786440 | tf_op jit(solution)/shard_map/ppermute | solution.py:257
  53.8 13.4 %collective-permute-start.12 = (f32[2,8,32,128]{3,2,1,0:T(8,128)S(1)}, f32[2,8,32,128]{3,2,1,0:T(8,128)S(1)}, u32[]{:S(2)}, u32[]{:S(2)}) collective-permute-start(f32[2,8,32,128]{3,2,1,0:T(8,128)S(1)} %get-tuple-element.55), channel_id=1, source_target_pairs={{0,3},{1,2},{2,1},{3,0},{4,7},{5,6},{6,5},{7,4},{8,11},{9,10},{10,... | collective-permute-start | bytes 786440 | tf_op jit(solution)/shard_map/ppermute | solution.py:257
  55.7 15.6 %collective-permute-start.13 = (f32[2,8,32,128]{3,2,1,0:T(8,128)S(1)}, f32[2,8,32,128]{3,2,1,0:T(8,128)S(1)}, u32[]{:S(2)}, u32[]{:S(2)}) collective-permute-start(f32[2,8,32,128]{3,2,1,0:T(8,128)S(1)} %get-tuple-element.56), channel_id=1, source_target_pairs={{0,2},{1,3},{2,0},{3,1},{4,6},{5,7},{6,4},{7,5},{8,10},{9,11},{10,... | collective-permute-start | bytes 786440 | tf_op jit(solution)/shard_map/ppermute | solution.py:257
  56.7 14.9 %collective-permute-start.14 = (f32[2,8,32,128]{3,2,1,0:T(8,128)S(1)}, f32[2,8,32,128]{3,2,1,0:T(8,128)S(1)}, u32[]{:S(2)}, u32[]{:S(2)}) collective-permute-start(f32[2,8,32,128]{3,2,1,0:T(8,128)S(1)} %get-tuple-element.57), channel_id=1, source_target_pairs={{0,1},{1,0},{2,3},{3,2},{4,5},{5,4},{6,7},{7,6},{8,9},{9,8},{10,11... | collective-permute-start | bytes 786440 | tf_op jit(solution)/shard_map/ppermute | solution.py:257

commit v7 on v6

--- a/solution.py
+++ b/solution.py
@@ -14,6 +14,7 @@
 CHUNKS = (8, 8)
 STEP = 8
 TURN = (0, 3, 2, 1)
+TURN_BACK = (0, 3, 2, 1)
 FINISH_STEP = (4, 4)
 ORDER = (
     ("state", 0),
@@ -46,11 +47,16 @@
     return lax.dot_general(a, b, (((ca,), (cb,)), ((), ())), preferred_element_type=F32)
 
 
+def unpack(info):
+    return (info[0] >> 1) % PARTS, info[0] & 1, (info[0] >> 1) // PARTS
+
+
 def place(info, r):
     return pl.multiple_of((info[0] ^ r) * QUARTER, QUARTER)
 
 
 def state_kernel(first, heads, info, q, k, v, g, *refs):
+    info = unpack(info)
     outs, (held, hold, sems) = refs[-PARTS - 3 : -3], refs[-3:]
     groups = [(at, min(STEP, heads - at)) for at in range(0, heads, STEP)]
     copies = []
@@ -94,6 +100,7 @@
 
 
 def add_kernel(info, a, b, c, d, *refs):
+    info = unpack(info)
     total, halves = refs[-2:]
     total[...] = (a[...] + b[...]) + (c[...] + d[...])
     halves[...] = total[info[1]]
@@ -111,6 +118,7 @@
 
 
 def offer_kernel(info, total, across, *refs):
+    info = unpack(info)
     out = refs[-1]
     node, upper = info[1], jnp.where(info[2] > 0, 1, 0)
     half = out.shape[1]
@@ -133,6 +141,7 @@
 
 
 def spread_kernel(pair, info, *refs):
+    info = unpack(info)
     count = 3 if pair else 1
     pieces, given, outs = refs[:PARTS], refs[PARTS : PARTS + count], refs[-PARTS:]
     mine, node, upper = info[0], info[1], jnp.where(info[2] > 0, 1, 0)
@@ -215,13 +224,14 @@
 
 
 def finish_kernel(first, step, factor, info, q, k, v, g, *refs):
+    info = unpack(info)
     terms, pieces = refs[:4], refs[4 : 4 + PARTS]
     outs, hold = refs[-5:-1], refs[-1]
     start = pl.program_id(0) * step
     for h in range(step):
         cols = pl.ds(pl.multiple_of((first + start + h) * HEAD_DIM, HEAD_DIM), HEAD_DIM)
         here = pl.ds(pl.multiple_of((start + h) * HEAD_DIM, HEAD_DIM), HEAD_DIM)
-        for r, piece in zip(TURN, pieces):
+        for r, piece in zip(TURN_BACK, pieces):
             at = pl.ds(place(info, r), QUARTER)
             hold[h, 0, at, :] = piece[0, start + h].astype(BF16)
             hold[h, 1, at, :] = piece[1, start + h].astype(BF16)
@@ -266,15 +276,15 @@
     assert nodes == 2 and size % PARTS == 0 and sum(CHUNKS) == heads
     factor = 1.0 / math.sqrt(HEAD_DIM * rows * nodes * size)
     node, place_in = lax.axis_index("node"), lax.axis_index("local")
-    info = jnp.stack([place_in % PARTS, node, place_in // PARTS]).astype(jnp.int32)
+    info = (place_in * 2 + node).astype(jnp.int32).reshape(1)
 
     firsts = [sum(CHUNKS[:i]) for i in range(len(CHUNKS))]
     pieces, given, ready, state, terms = {}, {}, {}, {}, {}
     outs = ()
-    last = info
+    last = None
     for stage, i in ORDER:
         first, count = firsts[i], CHUNKS[i]
-        behind = [last]
+        behind = [] if last is None else [last]
         if stage == "state":
             own = states(info, arrays, first, count, behind)
             last = own[0]
@@ -295,14 +305,14 @@
         elif stage == "spread":
             own = spread(info, pieces[i], given[i], behind)
             last = own[0]
-            got = {r: swap(own[r], size, r) for r in TURN[1:]}
+            got = {r: swap(own[r], size, r) for r in TURN_BACK[1:]}
             ready[i] = [own[0], got[1], got[2], got[3]]
         elif stage == "inner":
             terms[i] = inner(arrays, first, count, FINISH_STEP[i], behind)
             last = terms[i][0]
         else:
             outs = finish(
-                info, arrays, terms[i], [ready[i][r] for r in TURN], outs, first, FINISH_STEP[i], factor, behind
+                info, arrays, terms[i], [ready[i][r] for r in TURN_BACK], outs, first, FINISH_STEP[i], factor, behind
             )
     return tuple(outs)
 

time: 74.2 us -> 70.9 us (0.956)
  Pallas kernels: 21.8 us -> 16.1 us
  waiting for transfers between devices: 25.6 us -> 28 us
  starting transfers between devices: 23.5 us -> 25 us
    ppermute x14, waiting for transfers between devices: 23.4 us -> 25.8 us  [swap(): return lax.ppermute(array, 'local', [(i, i ^ mask) for i in range(size)])]
    ppermute x14, starting transfers between devices: 22.9 us -> 24.3 us  [swap(): return lax.ppermute(array, 'local', [(i, i ^ mask) for i in range(size)])]
    pallas_call x2, Pallas kernels: 7.27 us -> 5.83 us  [states(): pl.pallas_call(functools.partial(state_kernel, first, heads), out_shape=[...]
    pallas_call x2, Pallas kernels: 1.14 us -> 0.05 us  [offer(): pl.pallas_call(offer_kernel, out_shape=jax.ShapeDtypeStruct((3, heads //...]
    pallas_call x2, Pallas kernels: 4.77 us -> 3.69 us  [finish(): pl.pallas_call(functools.partial(finish_kernel, first, step, factor), out...]
    pallas_call x2, Pallas kernels: 1.61 us -> 0.53 us  [spread(): pl.pallas_call(functools.partial(spread_kernel, len(given) > 1), out_shap...]
    pallas_call x2, Pallas kernels: 1.23 us -> 0.16 us  [block_sum(): pl.pallas_call(add_kernel, out_shape=[jax.ShapeDtypeStruct(shape, F32), j...]
    unnamed x16 -> x14, local copies, waits for them, and re-layouts: 1.59 us -> 0.97 us
  transfers between devices with their start and end apart: 18 -> 18, of which waited for: 8 -> 9; matrix products, arithmetic and copies ran while one was open for 0% -> 0% of each run, Pallas kernels for 22% -> 16%
where the time goes in v7:
time: 70.9 us; the launch traced here: 70.8 us
  waiting for transfers between devices  28 us (39%)
  starting transfers between devices  25 us (35%)
  Pallas kernels  16.1 us (23%)
  local copies, waits for them, and re-layouts  0.97 us (1%)
  between operations  0.8 us (1%)
    ppermute x14, waiting for transfers between devices, swap(): return lax.ppermute(array, 'local', [(i, i ^ mask) for i in range(size)])  25.8 us
    ppermute x14, starting transfers between devices, swap(): return lax.ppermute(array, 'local', [(i, i ^ mask) for i in range(size)])  24.3 us
    pallas_call x2, Pallas kernels, states(): pl.pallas_call(functools.partial(state_kernel, first, heads), out_shape=[...  5.83 us
    pallas_call x2, Pallas kernels, inner(): pl.pallas_call(functools.partial(inner_kernel, first, step), out_shape=[j...  5.79 us
    pallas_call x2, Pallas kernels, finish(): pl.pallas_call(functools.partial(finish_kernel, first, step, factor), out...  3.69 us
    ppermute x2, waiting for transfers between devices, local(): across = lax.ppermute(halves, 'node', [(0, 1), (1, 0)])  2.17 us
  transfers between devices with their start and end apart: 18, of which 9 were waited for; matrix products, arithmetic and copies ran while one was open for 0% of the time, Pallas kernels for 16%

profile of v7, /device:TPU:0, one launch (start us, length us, event | category | flops | bytes accessed | tf_op | source)
XLA Modules:
  0.0 70.8 jit_solution(3261320999481429408)
XLA Ops:
  0.6 2.8 %shard_map.75 = (f32[2,8,32,128]{3,2,1,0:T(8,128)}, f32[2,8,32,128]{3,2,1,0:T(8,128)}, f32[2,8,32,128]{3,2,1,0:T(8,128)}, f32[2,8,32,128]{3,2,1,0:T(8,128)}) custom-call(s32[1]{0:T(128)} %bitcast.info, bf16[192,2048]{1,0:T(8,128)(2,1)} %q.11, bf16[192,2048]{1,0:T(8,128)(2,1)} %k.11, bf16[192,2048]{1,0:T(8,128)(2,1)} %v.11, bf16[192,2048]{1,0:T(8,128)(2,1)} %g.11), custom_call_target="tpu_custom_call" | custom-call | tf_op jit(solution)/shard_map/pallas_call | solution.py:88
  3.5 4.1 %collective-permute-start = (f32[2,8,32,128]{3,2,1,0:T(8,128)}, f32[2,8,32,128]{3,2,1,0:T(8,128)S(1)}, u32[]{:S(2)}, u32[]{:S(2)}) collective-permute-start(f32[2,8,32,128]{3,2,1,0:T(8,128)} %get-tuple-element.37), channel_id=1, source_target_pairs={{0,3},{1,2},{2,1},{3,0},{4,7},{5,6},{6,5},{7,4},{8,11},{9,10},{10,... | collective-permute-start | bytes 786440 | tf_op jit(solution)/shard_map/ppermute | solution.py:267
  7.5 0.4 collective-permute-start.1
  8.0 0.2 collective-permute-start.2
  8.2 0.0 copy-start
  8.2 0.0 copy-start.1
  8.2 0.0 copy-start.2
  8.2 0.0 copy-start.3
  8.2 3.0 %shard_map.76 = (f32[2,8,32,128]{3,2,1,0:T(8,128)}, f32[2,8,32,128]{3,2,1,0:T(8,128)}, f32[2,8,32,128]{3,2,1,0:T(8,128)}, f32[2,8,32,128]{3,2,1,0:T(8,128)}) custom-call(s32[1]{0:T(128)} %bitcast.info, bf16[192,2048]{1,0:T(8,128)(2,1)} %q.11, bf16[192,2048]{1,0:T(8,128)(2,1)} %k.11, bf16[192,2048]{1,0:T(8,128)(2,1)} %v.11, bf16[192,2048]{1,0:T(8,128)(2,1)} %g.11, ...), custom_call_target="tpu_custom_call" | custom-call | tf_op jit(solution)/shard_map/pallas_call | solution.py:88
  11.2 1.9 %collective-permute-start.4 = (f32[2,8,32,128]{3,2,1,0:T(8,128)}, f32[2,8,32,128]{3,2,1,0:T(8,128)S(1)}, u32[]{:S(2)}, u32[]{:S(2)}) collective-permute-start(f32[2,8,32,128]{3,2,1,0:T(8,128)} %get-tuple-element.48), channel_id=1, source_target_pairs={{0,1},{1,0},{2,3},{3,2},{4,5},{5,4},{6,7},{7,6},{8,9},{9,8},{10,11... | collective-permute-start | bytes 786440 | tf_op jit(solution)/shard_map/ppermute | solution.py:267
  13.1 1.6 %collective-permute-start.5 = (f32[2,8,32,128]{3,2,1,0:T(8,128)}, f32[2,8,32,128]{3,2,1,0:T(8,128)S(1)}, u32[]{:S(2)}, u32[]{:S(2)}) collective-permute-start(f32[2,8,32,128]{3,2,1,0:T(8,128)} %get-tuple-element.49), channel_id=1, source_target_pairs={{0,2},{1,3},{2,0},{3,1},{4,6},{5,7},{6,4},{7,5},{8,10},{9,11},{10,... | collective-permute-start | bytes 786440 | tf_op jit(solution)/shard_map/ppermute | solution.py:267
  14.7 0.2 collective-permute-done.b.refs_3_
  14.9 3.0 %collective-permute-start.6 = (f32[2,8,32,128]{3,2,1,0:T(8,128)}, f32[2,8,32,128]{3,2,1,0:T(8,128)S(1)}, u32[]{:S(2)}, u32[]{:S(2)}) collective-permute-start(f32[2,8,32,128]{3,2,1,0:T(8,128)} %get-tuple-element.50), channel_id=1, source_target_pairs={{0,3},{1,2},{2,1},{3,0},{4,7},{5,6},{6,5},{7,4},{8,11},{9,10},{10,... | collective-permute-start | bytes 786440 | tf_op jit(solution)/shard_map/ppermute | solution.py:267
  17.9 0.0 copy-done
  17.9 0.0 copy-done.1
  17.9 0.0 copy-done.2
  17.9 0.0 copy-done.3
  17.9 0.0 copy-start.5
  17.9 0.9 %copy-done.5 = f32[2,8,32,128]{3,2,1,0:T(8,128)S(1)} copy-done((f32[2,8,32,128]{3,2,1,0:T(8,128)S(1)}, f32[2,8,32,128]{3,2,1,0:T(8,128)}, u32[]{:S(2)}) %copy-start.5) | copy-done | bytes 262168
  18.8 0.0 copy-start.4
  18.8 2.9 %shard_map.77 = (f32[192,1024]{1,0:T(8,128)S(1)}, f32[192,1024]{1,0:T(8,128)S(1)}, f32[192,1024]{1,0:T(8,128)S(1)}, f32[192,1024]{1,0:T(8,128)S(1)}) custom-call(bf16[192,2048]{1,0:T(8,128)(2,1)S(1)} %copy-done, bf16[192,2048]{1,0:T(8,128)(2,1)S(1)} %copy-done.1, bf16[192,2048]{1,0:T(8,128)(2,1)S(1)} %copy-done.2, bf16[192,2048]{1,0:T(8,128)(2,1)S(1)} %copy-done.3, ...), custom_call_target="tpu_custom_call" | custom-call | tf_op jit(solution)/shard_map/pallas_call | solution.py:216
  21.8 0.0 collective-permute-done.1.c.refs_2_
  21.8 0.0 collective-permute-done.2.d.refs_1_
  21.8 0.0 copy-done.4
  21.8 0.1 shard_map.78
  21.9 0.1 collective-permute-start.3
  22.0 1.3 %collective-permute-done.3.across.refs_4_ = f32[8,32,128]{2,1,0:T(8,128)S(1)} collective-permute-done((f32[8,32,128]{2,1,0:T(8,128)S(1)}, f32[8,32,128]{2,1,0:T(8,128)S(1)}, u32[]{:S(2)}, u32[]{:S(2)}) %collective-permute-start.3) | collective-permute-done | bytes 131104 | tf_op jit(solution)/shard_map/ppermute | solution.py:295
  23.3 0.0 copy-start.6
  23.3 2.7 %collective-permute-start.10 = (f32[3,4,32,128]{3,2,1,0:T(8,128)S(1)}, f32[3,4,32,128]{3,2,1,0:T(8,128)S(1)}, u32[]{:S(2)}, u32[]{:S(2)}) collective-permute-start(f32[3,4,32,128]{3,2,1,0:T(8,128)S(1)} %shard_map.79.refs_0_), channel_id=1, source_target_pairs={{0,4},{1,5},{2,6},{3,7},{4,0},{5,1},{6,2},{7,3},{8,12},{9,13},{10,... | collective-permute-start | bytes 589832 | tf_op jit(solution)/shard_map/ppermute | solution.py:267
  26.0 2.9 %shard_map.80 = (f32[192,1024]{1,0:T(8,128)S(1)}, f32[192,1024]{1,0:T(8,128)S(1)}, f32[192,1024]{1,0:T(8,128)S(1)}, f32[192,1024]{1,0:T(8,128)S(1)}) custom-call(bf16[192,2048]{1,0:T(8,128)(2,1)S(1)} %copy-done, bf16[192,2048]{1,0:T(8,128)(2,1)S(1)} %copy-done.1, bf16[192,2048]{1,0:T(8,128)(2,1)S(1)} %copy-done.2, bf16[192,2048]{1,0:T(8,128)(2,1)S(1)} %copy-done.3, ...), custom_call_target="tpu_custom_call" | custom-call | tf_op jit(solution)/shard_map/pallas_call | solution.py:216
  28.9 0.0 collective-permute-done.4.d.refs_1_
  28.9 0.0 collective-permute-done.5.c.refs_2_
  28.9 6.3 %collective-permute-done.6.b.refs_3_ = f32[2,8,32,128]{3,2,1,0:T(8,128)S(1)} collective-permute-done((f32[2,8,32,128]{3,2,1,0:T(8,128)}, f32[2,8,32,128]{3,2,1,0:T(8,128)S(1)}, u32[]{:S(2)}, u32[]{:S(2)}) %collective-permute-start.6) | collective-permute-done | bytes 262176 | tf_op jit(solution)/shard_map/ppermute | solution.py:267
  35.2 0.0 copy-done.6
  35.2 0.1 shard_map.81
  35.2 0.1 collective-permute-start.7
  35.3 0.0 collective-permute-done.10.refs_5_
  35.3 0.5 collective-permute-start.11
  35.8 0.8 %collective-permute-done.7.across.refs_4_ = f32[8,32,128]{2,1,0:T(8,128)S(1)} collective-permute-done((f32[8,32,128]{2,1,0:T(8,128)S(1)}, f32[8,32,128]{2,1,0:T(8,128)S(1)}, u32[]{:S(2)}, u32[]{:S(2)}) %collective-permute-start.7) | collective-permute-done | bytes 131104 | tf_op jit(solution)/shard_map/ppermute | solution.py:295
  36.7 2.0 %collective-permute-start.8 = (f32[3,4,32,128]{3,2,1,0:T(8,128)S(1)}, f32[3,4,32,128]{3,2,1,0:T(8,128)S(1)}, u32[]{:S(2)}, u32[]{:S(2)}) collective-permute-start(f32[3,4,32,128]{3,2,1,0:T(8,128)S(1)} %shard_map.82.refs_7_), channel_id=1, source_target_pairs={{0,4},{1,5},{2,6},{3,7},{4,0},{5,1},{6,2},{7,3},{8,12},{9,13},{10,... | collective-permute-start | bytes 589832 | tf_op jit(solution)/shard_map/ppermute | solution.py:267
  38.7 0.0 collective-permute-done.11.refs_6_
  38.7 0.3 shard_map.83
  39.0 3.3 %collective-permute-start.15 = (f32[2,8,32,128]{3,2,1,0:T(8,128)S(1)}, f32[2,8,32,128]{3,2,1,0:T(8,128)S(1)}, u32[]{:S(2)}, u32[]{:S(2)}) collective-permute-start(f32[2,8,32,128]{3,2,1,0:T(8,128)S(1)} %get-tuple-element.61), channel_id=1, source_target_pairs={{0,3},{1,2},{2,1},{3,0},{4,7},{5,6},{6,5},{7,4},{8,11},{9,10},{10,... | collective-permute-start | bytes 786440 | tf_op jit(solution)/shard_map/ppermute | solution.py:267
  42.3 6.6 %collective-permute-done.8.refs_5_ = f32[3,4,32,128]{3,2,1,0:T(8,128)S(1)} collective-permute-done((f32[3,4,32,128]{3,2,1,0:T(8,128)S(1)}, f32[3,4,32,128]{3,2,1,0:T(8,128)S(1)}, u32[]{:S(2)}, u32[]{:S(2)}) %collective-permute-start.8) | collective-permute-done | bytes 196640 | tf_op jit(solution)/shard_map/ppermute | solution.py:267
  48.9 0.0 collective-permute-start.9
  48.9 0.0 collective-permute-start.16
  48.9 1.6 %collective-permute-start.17 = (f32[2,8,32,128]{3,2,1,0:T(8,128)S(1)}, f32[2,8,32,128]{3,2,1,0:T(8,128)S(1)}, u32[]{:S(2)}, u32[]{:S(2)}) collective-permute-start(f32[2,8,32,128]{3,2,1,0:T(8,128)S(1)} %get-tuple-element.63), channel_id=1, source_target_pairs={{0,1},{1,0},{2,3},{3,2},{4,5},{5,4},{6,7},{7,6},{8,9},{9,8},{10,11... | collective-permute-start | bytes 786440 | tf_op jit(solution)/shard_map/ppermute | solution.py:267
  50.5 0.0 collective-permute-done.9.refs_6_
  50.5 0.3 shard_map.84
  50.8 1.9 %collective-permute-start.12 = (f32[2,8,32,128]{3,2,1,0:T(8,128)S(1)}, f32[2,8,32,128]{3,2,1,0:T(8,128)S(1)}, u32[]{:S(2)}, u32[]{:S(2)}) collective-permute-start(f32[2,8,32,128]{3,2,1,0:T(8,128)S(1)} %get-tuple-element.55), channel_id=1, source_target_pairs={{0,3},{1,2},{2,1},{3,0},{4,7},{5,6},{6,5},{7,4},{8,11},{9,10},{10,... | collective-permute-start | bytes 786440 | tf_op jit(solution)/shard_map/ppermute | solution.py:267
  52.8 1.0 %collective-permute-start.13 = (f32[2,8,32,128]{3,2,1,0:T(8,128)S(1)}, f32[2,8,32,128]{3,2,1,0:T(8,128)S(1)}, u32[]{:S(2)}, u32[]{:S(2)}) collective-permute-start(f32[2,8,32,128]{3,2,1,0:T(8,128)S(1)} %get-tuple-element.56), channel_id=1, source_target_pairs={{0,2},{1,3},{2,0},{3,1},{4,6},{5,7},{6,4},{7,5},{8,10},{9,11},{10,... | collective-permute-start | bytes 786440 | tf_op jit(solution)/shard_map/ppermute | solution.py:267
  53.8 0.0 collective-permute-done.15.refs_5_
  53.8 0.6 collective-permute-start.14
  54.4 3.6 %collective-permute-done.16.refs_6_ = f32[2,8,32,128]{3,2,1,0:T(8,128)S(1)} collective-permute-done((f32[2,8,32,128]{3,2,1,0:T(8,128)S(1)}, f32[2,8,32,128]{3,2,1,0:T(8,128)S(1)}, u32[]{:S(2)}, u32[]{:S(2)}) %collective-permute-start.16) | collective-permute-done | bytes 262176 | tf_op jit(solution)/shard_map/ppermute | solution.py:267
  58.0 4.4 %collective-permute-done.17.refs_7_ = f32[2,8,32,128]{3,2,1,0:T(8,128)S(1)} collective-permute-done((f32[2,8,32,128]{3,2,1,0:T(8,128)S(1)}, f32[2,8,32,128]{3,2,1,0:T(8,128)S(1)}, u32[]{:S(2)}, u32[]{:S(2)}) %collective-permute-start.17) | collective-permute-done | bytes 262176 | tf_op jit(solution)/shard_map/ppermute | solution.py:267
  62.4 1.8 %shard_map.85 = (bf16[192,2048]{1,0:T(8,128)(2,1)}, bf16[192,2048]{1,0:T(8,128)(2,1)}, bf16[192,2048]{1,0:T(8,128)(2,1)}, bf16[192,2048]{1,0:T(8,128)(2,1)}) custom-call(s32[1]{0:T(128)} %bitcast.info, bf16[192,2048]{1,0:T(8,128)(2,1)S(1)} %copy-done, bf16[192,2048]{1,0:T(8,128)(2,1)S(1)} %copy-done.1, bf16[192,2048]{1,0:T(8,128)(2,1)S(1)} %copy-done.2, ...), custom_call_target="tpu_custom_call" | custom-call | tf_op jit(solution)/shard_map/pallas_call | solution.py:254
  64.2 0.5 collective-permute-done.12.refs_5_
  64.7 4.2 %collective-permute-done.13.refs_6_ = f32[2,8,32,128]{3,2,1,0:T(8,128)S(1)} collective-permute-done((f32[2,8,32,128]{3,2,1,0:T(8,128)S(1)}, f32[2,8,32,128]{3,2,1,0:T(8,128)S(1)}, u32[]{:S(2)}, u32[]{:S(2)}) %collective-permute-start.13) | collective-permute-done | bytes 262176 | tf_op jit(solution)/shard_map/ppermute | solution.py:267
  68.9 0.0 collective-permute-done.14.refs_7_
  68.9 1.8 %shard_map.86 = (bf16[192,2048]{1,0:T(8,128)(2,1)}, bf16[192,2048]{1,0:T(8,128)(2,1)}, bf16[192,2048]{1,0:T(8,128)(2,1)}, bf16[192,2048]{1,0:T(8,128)(2,1)}) custom-call(s32[1]{0:T(128)} %bitcast.info, bf16[192,2048]{1,0:T(8,128)(2,1)S(1)} %copy-done, ...), custom_call_target="tpu_custom_call", output_to_operand_aliasing={{0}: (13, {}), {1}: (14, {}), {2}: (15, {}), {3}: (16, {})} | custom-call | tf_op jit(solution)/shard_map/pallas_call | solution.py:254
  (2 shorter events, 0.1 us)
Async XLA Ops:
  3.5 11.4 %collective-permute-start = (f32[2,8,32,128]{3,2,1,0:T(8,128)}, f32[2,8,32,128]{3,2,1,0:T(8,128)S(1)}, u32[]{:S(2)}, u32[]{:S(2)}) collective-permute-start(f32[2,8,32,128]{3,2,1,0:T(8,128)} %get-tuple-element.37), channel_id=1, source_target_pairs={{0,3},{1,2},{2,1},{3,0},{4,7},{5,6},{6,5},{7,4},{8,11},{9,10},{10,... | collective-permute-start | bytes 786440 | tf_op jit(solution)/shard_map/ppermute | solution.py:267
  7.5 14.2 %collective-permute-start.1 = (f32[2,8,32,128]{3,2,1,0:T(8,128)}, f32[2,8,32,128]{3,2,1,0:T(8,128)S(1)}, u32[]{:S(2)}, u32[]{:S(2)}) collective-permute-start(f32[2,8,32,128]{3,2,1,0:T(8,128)} %get-tuple-element.38), channel_id=1, source_target_pairs={{0,2},{1,3},{2,0},{3,1},{4,6},{5,7},{6,4},{7,5},{8,10},{9,11},{10,... | collective-permute-start | bytes 786440 | tf_op jit(solution)/shard_map/ppermute | solution.py:267
  8.0 13.8 %collective-permute-start.2 = (f32[2,8,32,128]{3,2,1,0:T(8,128)}, f32[2,8,32,128]{3,2,1,0:T(8,128)S(1)}, u32[]{:S(2)}, u32[]{:S(2)}) collective-permute-start(f32[2,8,32,128]{3,2,1,0:T(8,128)} %get-tuple-element.39), channel_id=1, source_target_pairs={{0,1},{1,0},{2,3},{3,2},{4,5},{5,4},{6,7},{7,6},{8,9},{9,8},{10,11... | collective-permute-start | bytes 786440 | tf_op jit(solution)/shard_map/ppermute | solution.py:267
  8.2 9.7 %copy-start = (bf16[192,2048]{1,0:T(8,128)(2,1)S(1)}, bf16[192,2048]{1,0:T(8,128)(2,1)}, u32[]{:S(2)}) copy-start(bf16[192,2048]{1,0:T(8,128)(2,1)} %q.11) | copy-start | bytes 2359300
  8.2 9.7 %copy-start.1 = (bf16[192,2048]{1,0:T(8,128)(2,1)S(1)}, bf16[192,2048]{1,0:T(8,128)(2,1)}, u32[]{:S(2)}) copy-start(bf16[192,2048]{1,0:T(8,128)(2,1)} %k.11) | copy-start | bytes 2359300
  8.2 9.7 %copy-start.2 = (bf16[192,2048]{1,0:T(8,128)(2,1)S(1)}, bf16[192,2048]{1,0:T(8,128)(2,1)}, u32[]{:S(2)}) copy-start(bf16[192,2048]{1,0:T(8,128)(2,1)} %v.11) | copy-start | bytes 2359300
  8.2 9.7 %copy-start.3 = (bf16[192,2048]{1,0:T(8,128)(2,1)S(1)}, bf16[192,2048]{1,0:T(8,128)(2,1)}, u32[]{:S(2)}) copy-start(bf16[192,2048]{1,0:T(8,128)(2,1)} %g.11) | copy-start | bytes 2359300
  11.2 17.7 %collective-permute-start.4 = (f32[2,8,32,128]{3,2,1,0:T(8,128)}, f32[2,8,32,128]{3,2,1,0:T(8,128)S(1)}, u32[]{:S(2)}, u32[]{:S(2)}) collective-permute-start(f32[2,8,32,128]{3,2,1,0:T(8,128)} %get-tuple-element.48), channel_id=1, source_target_pairs={{0,1},{1,0},{2,3},{3,2},{4,5},{5,4},{6,7},{7,6},{8,9},{9,8},{10,11... | collective-permute-start | bytes 786440 | tf_op jit(solution)/shard_map/ppermute | solution.py:267
  13.1 15.8 %collective-permute-start.5 = (f32[2,8,32,128]{3,2,1,0:T(8,128)}, f32[2,8,32,128]{3,2,1,0:T(8,128)S(1)}, u32[]{:S(2)}, u32[]{:S(2)}) collective-permute-start(f32[2,8,32,128]{3,2,1,0:T(8,128)} %get-tuple-element.49), channel_id=1, source_target_pairs={{0,2},{1,3},{2,0},{3,1},{4,6},{5,7},{6,4},{7,5},{8,10},{9,11},{10,... | collective-permute-start | bytes 786440 | tf_op jit(solution)/shard_map/ppermute | solution.py:267
  14.9 20.2 %collective-permute-start.6 = (f32[2,8,32,128]{3,2,1,0:T(8,128)}, f32[2,8,32,128]{3,2,1,0:T(8,128)S(1)}, u32[]{:S(2)}, u32[]{:S(2)}) collective-permute-start(f32[2,8,32,128]{3,2,1,0:T(8,128)} %get-tuple-element.50), channel_id=1, source_target_pairs={{0,3},{1,2},{2,1},{3,0},{4,7},{5,6},{6,5},{7,4},{8,11},{9,10},{10,... | collective-permute-start | bytes 786440 | tf_op jit(solution)/shard_map/ppermute | solution.py:267
  17.9 1.0 %copy-start.5 = (f32[2,8,32,128]{3,2,1,0:T(8,128)S(1)}, f32[2,8,32,128]{3,2,1,0:T(8,128)}, u32[]{:S(2)}) copy-start(f32[2,8,32,128]{3,2,1,0:T(8,128)} %get-tuple-element.40.refs_0_.a) | copy-start | bytes 786436
  18.8 2.9 %copy-start.4 = (f32[2,8,32,128]{3,2,1,0:T(8,128)S(1)}, f32[2,8,32,128]{3,2,1,0:T(8,128)}, u32[]{:S(2)}) copy-start(f32[2,8,32,128]{3,2,1,0:T(8,128)} %get-tuple-element.36.refs_0_.a) | copy-start | bytes 786436
  21.9 1.4 %collective-permute-start.3 = (f32[8,32,128]{2,1,0:T(8,128)S(1)}, f32[8,32,128]{2,1,0:T(8,128)S(1)}, u32[]{:S(2)}, u32[]{:S(2)}) collective-permute-start(f32[8,32,128]{2,1,0:T(8,128)S(1)} %get-tuple-element.43), channel_id=1, source_target_pairs={{0,8},{8,0},{1,9},{9,1},{2,10},{10,2},{3,11},{11,3},{4,12},{12,4},... | collective-permute-start | bytes 393224 | tf_op jit(solution)/shard_map/ppermute | solution.py:295
  23.3 11.8 %copy-start.6 = (f32[2,8,32,128]{3,2,1,0:T(8,128)S(1)}, f32[2,8,32,128]{3,2,1,0:T(8,128)}, u32[]{:S(2)}) copy-start(f32[2,8,32,128]{3,2,1,0:T(8,128)} %get-tuple-element.40.refs_0_.a) | copy-start | bytes 786436
  23.3 12.0 %collective-permute-start.10 = (f32[3,4,32,128]{3,2,1,0:T(8,128)S(1)}, f32[3,4,32,128]{3,2,1,0:T(8,128)S(1)}, u32[]{:S(2)}, u32[]{:S(2)}) collective-permute-start(f32[3,4,32,128]{3,2,1,0:T(8,128)S(1)} %shard_map.79.refs_0_), channel_id=1, source_target_pairs={{0,4},{1,5},{2,6},{3,7},{4,0},{5,1},{6,2},{7,3},{8,12},{9,13},{10,... | collective-permute-start | bytes 589832 | tf_op jit(solution)/shard_map/ppermute | solution.py:267
  35.2 1.4 %collective-permute-start.7 = (f32[8,32,128]{2,1,0:T(8,128)S(1)}, f32[8,32,128]{2,1,0:T(8,128)S(1)}, u32[]{:S(2)}, u32[]{:S(2)}) collective-permute-start(f32[8,32,128]{2,1,0:T(8,128)S(1)} %get-tuple-element.51), channel_id=1, source_target_pairs={{0,8},{8,0},{1,9},{9,1},{2,10},{10,2},{3,11},{11,3},{4,12},{12,4},... | collective-permute-start | bytes 393224 | tf_op jit(solution)/shard_map/ppermute | solution.py:295
  35.3 3.4 %collective-permute-start.11 = (f32[3,4,32,128]{3,2,1,0:T(8,128)S(1)}, f32[3,4,32,128]{3,2,1,0:T(8,128)S(1)}, u32[]{:S(2)}, u32[]{:S(2)}) collective-permute-start(f32[3,4,32,128]{3,2,1,0:T(8,128)S(1)} %collective-permute-done.10.refs_5_), channel_id=1, source_target_pairs={{0,8},{8,0},{1,9},{9,1},{2,10},{10,2},{3,11},{11,3},{4,12},{12,4},... | collective-permute-start | bytes 589832 | tf_op jit(solution)/shard_map/ppermute | solution.py:302
  36.7 12.2 %collective-permute-start.8 = (f32[3,4,32,128]{3,2,1,0:T(8,128)S(1)}, f32[3,4,32,128]{3,2,1,0:T(8,128)S(1)}, u32[]{:S(2)}, u32[]{:S(2)}) collective-permute-start(f32[3,4,32,128]{3,2,1,0:T(8,128)S(1)} %shard_map.82.refs_7_), channel_id=1, source_target_pairs={{0,4},{1,5},{2,6},{3,7},{4,0},{5,1},{6,2},{7,3},{8,12},{9,13},{10,... | collective-permute-start | bytes 589832 | tf_op jit(solution)/shard_map/ppermute | solution.py:267
  39.0 14.8 %collective-permute-start.15 = (f32[2,8,32,128]{3,2,1,0:T(8,128)S(1)}, f32[2,8,32,128]{3,2,1,0:T(8,128)S(1)}, u32[]{:S(2)}, u32[]{:S(2)}) collective-permute-start(f32[2,8,32,128]{3,2,1,0:T(8,128)S(1)} %get-tuple-element.61), channel_id=1, source_target_pairs={{0,3},{1,2},{2,1},{3,0},{4,7},{5,6},{6,5},{7,4},{8,11},{9,10},{10,... | collective-permute-start | bytes 786440 | tf_op jit(solution)/shard_map/ppermute | solution.py:267
  48.9 1.6 %collective-permute-start.9 = (f32[3,4,32,128]{3,2,1,0:T(8,128)S(1)}, f32[3,4,32,128]{3,2,1,0:T(8,128)S(1)}, u32[]{:S(2)}, u32[]{:S(2)}) collective-permute-start(f32[3,4,32,128]{3,2,1,0:T(8,128)S(1)} %collective-permute-done.8.refs_5_), channel_id=1, source_target_pairs={{0,8},{8,0},{1,9},{9,1},{2,10},{10,2},{3,11},{11,3},{4,12},{12,4},... | collective-permute-start | bytes 589832 | tf_op jit(solution)/shard_map/ppermute | solution.py:302
  48.9 9.1 %collective-permute-start.16 = (f32[2,8,32,128]{3,2,1,0:T(8,128)S(1)}, f32[2,8,32,128]{3,2,1,0:T(8,128)S(1)}, u32[]{:S(2)}, u32[]{:S(2)}) collective-permute-start(f32[2,8,32,128]{3,2,1,0:T(8,128)S(1)} %get-tuple-element.62), channel_id=1, source_target_pairs={{0,2},{1,3},{2,0},{3,1},{4,6},{5,7},{6,4},{7,5},{8,10},{9,11},{10,... | collective-permute-start | bytes 786440 | tf_op jit(solution)/shard_map/ppermute | solution.py:267
  48.9 13.5 %collective-permute-start.17 = (f32[2,8,32,128]{3,2,1,0:T(8,128)S(1)}, f32[2,8,32,128]{3,2,1,0:T(8,128)S(1)}, u32[]{:S(2)}, u32[]{:S(2)}) collective-permute-start(f32[2,8,32,128]{3,2,1,0:T(8,128)S(1)} %get-tuple-element.63), channel_id=1, source_target_pairs={{0,1},{1,0},{2,3},{3,2},{4,5},{5,4},{6,7},{7,6},{8,9},{9,8},{10,11... | collective-permute-start | bytes 786440 | tf_op jit(solution)/shard_map/ppermute | solution.py:267
  50.8 13.9 %collective-permute-start.12 = (f32[2,8,32,128]{3,2,1,0:T(8,128)S(1)}, f32[2,8,32,128]{3,2,1,0:T(8,128)S(1)}, u32[]{:S(2)}, u32[]{:S(2)}) collective-permute-start(f32[2,8,32,128]{3,2,1,0:T(8,128)S(1)} %get-tuple-element.55), channel_id=1, source_target_pairs={{0,3},{1,2},{2,1},{3,0},{4,7},{5,6},{6,5},{7,4},{8,11},{9,10},{10,... | collective-permute-start | bytes 786440 | tf_op jit(solution)/shard_map/ppermute | solution.py:267
  52.8 16.2 %collective-permute-start.13 = (f32[2,8,32,128]{3,2,1,0:T(8,128)S(1)}, f32[2,8,32,128]{3,2,1,0:T(8,128)S(1)}, u32[]{:S(2)}, u32[]{:S(2)}) collective-permute-start(f32[2,8,32,128]{3,2,1,0:T(8,128)S(1)} %get-tuple-element.56), channel_id=1, source_target_pairs={{0,2},{1,3},{2,0},{3,1},{4,6},{5,7},{6,4},{7,5},{8,10},{9,11},{10,... | collective-permute-start | bytes 786440 | tf_op jit(solution)/shard_map/ppermute | solution.py:267
  53.8 15.1 %collective-permute-start.14 = (f32[2,8,32,128]{3,2,1,0:T(8,128)S(1)}, f32[2,8,32,128]{3,2,1,0:T(8,128)S(1)}, u32[]{:S(2)}, u32[]{:S(2)}) collective-permute-start(f32[2,8,32,128]{3,2,1,0:T(8,128)S(1)} %get-tuple-element.57), channel_id=1, source_target_pairs={{0,1},{1,0},{2,3},{3,2},{4,5},{5,4},{6,7},{7,6},{8,9},{9,8},{10,11... | collective-permute-start | bytes 786440 | tf_op jit(solution)/shard_map/ppermute | solution.py:267

commit v8 on v7

--- a/solution.py
+++ b/solution.py
@@ -15,7 +15,7 @@
 STEP = 8
 TURN = (0, 3, 2, 1)
 TURN_BACK = (0, 3, 2, 1)
-FINISH_STEP = (4, 4)
+FINISH_STEP = (8, 8)
 ORDER = (
     ("state", 0),
     ("state", 1),
@@ -33,7 +33,7 @@
 
 F32 = jnp.float32
 BF16 = jnp.bfloat16
-VMEM_LIMIT = 40 * 1024 * 1024
+VMEM_LIMIT = 16 * 1024 * 1024
 SMALL_LIMIT = 16 * 1024 * 1024
 STATE_LIMIT = 60 * 1024 * 1024
 
@@ -303,7 +303,7 @@
             else:
                 given[i] = [sums_outside(total, node, place_in // PARTS, blocks)]
         elif stage == "spread":
-            own = spread(info, pieces[i], given[i], behind)
+            own = spread(info, pieces[i], given[i], [])
             last = own[0]
             got = {r: swap(own[r], size, r) for r in TURN_BACK[1:]}
             ready[i] = [own[0], got[1], got[2], got[3]]
@@ -312,7 +312,7 @@
             last = terms[i][0]
         else:
             outs = finish(
-                info, arrays, terms[i], [ready[i][r] for r in TURN_BACK], outs, first, FINISH_STEP[i], factor, behind
+                info, arrays, terms[i], [ready[i][r] for r in TURN_BACK], outs, first, FINISH_STEP[i], factor, []
             )
     return tuple(outs)
 

time: 70.9 us -> 71 us (level)
  no operation moved by 1% of the time
where the time goes in v8:
time: 71 us; the launch traced here: 70.8 us
  waiting for transfers between devices  28.2 us (40%)
  starting transfers between devices  25 us (35%)
  Pallas kernels  15.9 us (22%)
  local copies, waits for them, and re-layouts  0.96 us (1%)
  between operations  0.79 us (1%)
    ppermute x14, waiting for transfers between devices, swap(): return lax.ppermute(array, 'local', [(i, i ^ mask) for i in range(size)])  26.1 us
    ppermute x14, starting transfers between devices, swap(): return lax.ppermute(array, 'local', [(i, i ^ mask) for i in range(size)])  24.3 us
    pallas_call x2, Pallas kernels, states(): pl.pallas_call(functools.partial(state_kernel, first, heads), out_shape=[...  5.84 us
    pallas_call x2, Pallas kernels, inner(): pl.pallas_call(functools.partial(inner_kernel, first, step), out_shape=[j...  5.44 us
    pallas_call x2, Pallas kernels, finish(): pl.pallas_call(functools.partial(finish_kernel, first, step, factor), out...  3.87 us
    ppermute x2, waiting for transfers between devices, local(): across = lax.ppermute(halves, 'node', [(0, 1), (1, 0)])  2.17 us
  transfers between devices with their start and end apart: 18, of which 9 were waited for; matrix products, arithmetic and copies ran while one was open for 0% of the time, Pallas kernels for 16%

profile of v8, /device:TPU:0, one launch (start us, length us, event | category | flops | bytes accessed | tf_op | source)
XLA Modules:
  0.0 70.8 jit_solution(5799797358161233319)
XLA Ops:
  0.6 2.8 %shard_map.75 = (f32[2,8,32,128]{3,2,1,0:T(8,128)}, f32[2,8,32,128]{3,2,1,0:T(8,128)}, f32[2,8,32,128]{3,2,1,0:T(8,128)}, f32[2,8,32,128]{3,2,1,0:T(8,128)}) custom-call(s32[1]{0:T(128)} %bitcast.info, bf16[192,2048]{1,0:T(8,128)(2,1)} %q.11, bf16[192,2048]{1,0:T(8,128)(2,1)} %k.11, bf16[192,2048]{1,0:T(8,128)(2,1)} %v.11, bf16[192,2048]{1,0:T(8,128)(2,1)} %g.11), custom_call_target="tpu_custom_call" | custom-call | tf_op jit(solution)/shard_map/pallas_call | solution.py:88
  3.5 4.1 %collective-permute-start = (f32[2,8,32,128]{3,2,1,0:T(8,128)}, f32[2,8,32,128]{3,2,1,0:T(8,128)S(1)}, u32[]{:S(2)}, u32[]{:S(2)}) collective-permute-start(f32[2,8,32,128]{3,2,1,0:T(8,128)} %get-tuple-element.37), channel_id=1, source_target_pairs={{0,3},{1,2},{2,1},{3,0},{4,7},{5,6},{6,5},{7,4},{8,11},{9,10},{10,... | collective-permute-start | bytes 786440 | tf_op jit(solution)/shard_map/ppermute | solution.py:267
  7.5 0.4 collective-permute-start.1
  8.0 0.2 collective-permute-start.2
  8.2 0.0 copy-start
  8.2 0.0 copy-start.1
  8.2 0.0 copy-start.2
  8.2 0.0 copy-start.3
  8.2 3.0 %shard_map.76 = (f32[2,8,32,128]{3,2,1,0:T(8,128)}, f32[2,8,32,128]{3,2,1,0:T(8,128)}, f32[2,8,32,128]{3,2,1,0:T(8,128)}, f32[2,8,32,128]{3,2,1,0:T(8,128)}) custom-call(s32[1]{0:T(128)} %bitcast.info, bf16[192,2048]{1,0:T(8,128)(2,1)} %q.11, bf16[192,2048]{1,0:T(8,128)(2,1)} %k.11, bf16[192,2048]{1,0:T(8,128)(2,1)} %v.11, bf16[192,2048]{1,0:T(8,128)(2,1)} %g.11, ...), custom_call_target="tpu_custom_call" | custom-call | tf_op jit(solution)/shard_map/pallas_call | solution.py:88
  11.2 1.9 %collective-permute-start.4 = (f32[2,8,32,128]{3,2,1,0:T(8,128)}, f32[2,8,32,128]{3,2,1,0:T(8,128)S(1)}, u32[]{:S(2)}, u32[]{:S(2)}) collective-permute-start(f32[2,8,32,128]{3,2,1,0:T(8,128)} %get-tuple-element.48), channel_id=1, source_target_pairs={{0,1},{1,0},{2,3},{3,2},{4,5},{5,4},{6,7},{7,6},{8,9},{9,8},{10,11... | collective-permute-start | bytes 786440 | tf_op jit(solution)/shard_map/ppermute | solution.py:267
  13.1 1.6 %collective-permute-start.5 = (f32[2,8,32,128]{3,2,1,0:T(8,128)}, f32[2,8,32,128]{3,2,1,0:T(8,128)S(1)}, u32[]{:S(2)}, u32[]{:S(2)}) collective-permute-start(f32[2,8,32,128]{3,2,1,0:T(8,128)} %get-tuple-element.49), channel_id=1, source_target_pairs={{0,2},{1,3},{2,0},{3,1},{4,6},{5,7},{6,4},{7,5},{8,10},{9,11},{10,... | collective-permute-start | bytes 786440 | tf_op jit(solution)/shard_map/ppermute | solution.py:267
  14.7 0.2 collective-permute-done.b.refs_3_
  14.9 3.0 %collective-permute-start.6 = (f32[2,8,32,128]{3,2,1,0:T(8,128)}, f32[2,8,32,128]{3,2,1,0:T(8,128)S(1)}, u32[]{:S(2)}, u32[]{:S(2)}) collective-permute-start(f32[2,8,32,128]{3,2,1,0:T(8,128)} %get-tuple-element.50), channel_id=1, source_target_pairs={{0,3},{1,2},{2,1},{3,0},{4,7},{5,6},{6,5},{7,4},{8,11},{9,10},{10,... | collective-permute-start | bytes 786440 | tf_op jit(solution)/shard_map/ppermute | solution.py:267
  17.9 0.0 copy-done
  17.9 0.0 copy-done.1
  17.9 0.0 copy-done.2
  17.9 0.0 copy-done.3
  17.9 0.0 copy-start.5
  17.9 0.9 %copy-done.5 = f32[2,8,32,128]{3,2,1,0:T(8,128)S(1)} copy-done((f32[2,8,32,128]{3,2,1,0:T(8,128)S(1)}, f32[2,8,32,128]{3,2,1,0:T(8,128)}, u32[]{:S(2)}) %copy-start.5) | copy-done | bytes 262168
  18.8 0.0 copy-start.4
  18.8 2.7 %shard_map.77 = (f32[192,1024]{1,0:T(8,128)S(1)}, f32[192,1024]{1,0:T(8,128)S(1)}, f32[192,1024]{1,0:T(8,128)S(1)}, f32[192,1024]{1,0:T(8,128)S(1)}) custom-call(bf16[192,2048]{1,0:T(8,128)(2,1)S(1)} %copy-done, bf16[192,2048]{1,0:T(8,128)(2,1)S(1)} %copy-done.1, bf16[192,2048]{1,0:T(8,128)(2,1)S(1)} %copy-done.2, bf16[192,2048]{1,0:T(8,128)(2,1)S(1)} %copy-done.3, ...), custom_call_target="tpu_custom_call" | custom-call | tf_op jit(solution)/shard_map/pallas_call | solution.py:216
  21.6 0.0 collective-permute-done.1.c.refs_2_
  21.6 0.0 collective-permute-done.2.d.refs_1_
  21.6 0.0 copy-done.4
  21.6 0.1 shard_map.78
  21.7 0.1 collective-permute-start.3
  21.8 1.3 %collective-permute-done.3.across.refs_4_ = f32[8,32,128]{2,1,0:T(8,128)S(1)} collective-permute-done((f32[8,32,128]{2,1,0:T(8,128)S(1)}, f32[8,32,128]{2,1,0:T(8,128)S(1)}, u32[]{:S(2)}, u32[]{:S(2)}) %collective-permute-start.3) | collective-permute-done | bytes 131104 | tf_op jit(solution)/shard_map/ppermute | solution.py:295
  23.1 2.6 %collective-permute-start.13 = (f32[3,4,32,128]{3,2,1,0:T(8,128)S(1)}, f32[3,4,32,128]{3,2,1,0:T(8,128)S(1)}, u32[]{:S(2)}, u32[]{:S(2)}) collective-permute-start(f32[3,4,32,128]{3,2,1,0:T(8,128)S(1)} %shard_map.79.refs_0_), channel_id=1, source_target_pairs={{0,4},{1,5},{2,6},{3,7},{4,0},{5,1},{6,2},{7,3},{8,12},{9,13},{10,... | collective-permute-start | bytes 589832 | tf_op jit(solution)/shard_map/ppermute | solution.py:267
  25.8 2.7 %shard_map.80 = (f32[192,1024]{1,0:T(8,128)S(1)}, f32[192,1024]{1,0:T(8,128)S(1)}, f32[192,1024]{1,0:T(8,128)S(1)}, f32[192,1024]{1,0:T(8,128)S(1)}) custom-call(bf16[192,2048]{1,0:T(8,128)(2,1)S(1)} %copy-done, bf16[192,2048]{1,0:T(8,128)(2,1)S(1)} %copy-done.1, bf16[192,2048]{1,0:T(8,128)(2,1)S(1)} %copy-done.2, bf16[192,2048]{1,0:T(8,128)(2,1)S(1)} %copy-done.3, ...), custom_call_target="tpu_custom_call" | custom-call | tf_op jit(solution)/shard_map/pallas_call | solution.py:216
  28.5 0.0 collective-permute-done.4.d.refs_1_
  28.5 0.0 collective-permute-done.5.c.refs_2_
  28.5 6.6 %collective-permute-done.6.b.refs_3_ = f32[2,8,32,128]{3,2,1,0:T(8,128)S(1)} collective-permute-done((f32[2,8,32,128]{3,2,1,0:T(8,128)}, f32[2,8,32,128]{3,2,1,0:T(8,128)S(1)}, u32[]{:S(2)}, u32[]{:S(2)}) %collective-permute-start.6) | collective-permute-done | bytes 262176 | tf_op jit(solution)/shard_map/ppermute | solution.py:267
  35.2 0.1 shard_map.81
  35.2 0.1 collective-permute-start.7
  35.3 0.0 collective-permute-done.13.refs_5_
  35.3 0.5 collective-permute-start.14
  35.8 0.8 %collective-permute-done.7.across.refs_4_ = f32[8,32,128]{2,1,0:T(8,128)S(1)} collective-permute-done((f32[8,32,128]{2,1,0:T(8,128)S(1)}, f32[8,32,128]{2,1,0:T(8,128)S(1)}, u32[]{:S(2)}, u32[]{:S(2)}) %collective-permute-start.7) | collective-permute-done | bytes 131104 | tf_op jit(solution)/shard_map/ppermute | solution.py:295
  36.7 2.0 %collective-permute-start.8 = (f32[3,4,32,128]{3,2,1,0:T(8,128)S(1)}, f32[3,4,32,128]{3,2,1,0:T(8,128)S(1)}, u32[]{:S(2)}, u32[]{:S(2)}) collective-permute-start(f32[3,4,32,128]{3,2,1,0:T(8,128)S(1)} %shard_map.82), channel_id=1, source_target_pairs={{0,4},{1,5},{2,6},{3,7},{4,0},{5,1},{6,2},{7,3},{8,12},{9,13},{10,... | collective-permute-start | bytes 589832 | tf_op jit(solution)/shard_map/ppermute | solution.py:267
  38.7 0.0 collective-permute-done.14.refs_6_
  38.7 0.3 shard_map.84
  39.0 3.3 %collective-permute-start.15 = (f32[2,8,32,128]{3,2,1,0:T(8,128)S(1)}, f32[2,8,32,128]{3,2,1,0:T(8,128)S(1)}, u32[]{:S(2)}, u32[]{:S(2)}) collective-permute-start(f32[2,8,32,128]{3,2,1,0:T(8,128)S(1)} %get-tuple-element.61), channel_id=1, source_target_pairs={{0,3},{1,2},{2,1},{3,0},{4,7},{5,6},{6,5},{7,4},{8,11},{9,10},{10,... | collective-permute-start | bytes 786440 | tf_op jit(solution)/shard_map/ppermute | solution.py:267
  42.3 6.6 %collective-permute-done.8.refs_5_ = f32[3,4,32,128]{3,2,1,0:T(8,128)S(1)} collective-permute-done((f32[3,4,32,128]{3,2,1,0:T(8,128)S(1)}, f32[3,4,32,128]{3,2,1,0:T(8,128)S(1)}, u32[]{:S(2)}, u32[]{:S(2)}) %collective-permute-start.8) | collective-permute-done | bytes 196640 | tf_op jit(solution)/shard_map/ppermute | solution.py:267
  48.9 0.0 collective-permute-start.9
  48.9 0.0 collective-permute-start.16
  48.9 1.6 %collective-permute-start.17 = (f32[2,8,32,128]{3,2,1,0:T(8,128)S(1)}, f32[2,8,32,128]{3,2,1,0:T(8,128)S(1)}, u32[]{:S(2)}, u32[]{:S(2)}) collective-permute-start(f32[2,8,32,128]{3,2,1,0:T(8,128)S(1)} %get-tuple-element.63), channel_id=1, source_target_pairs={{0,1},{1,0},{2,3},{3,2},{4,5},{5,4},{6,7},{7,6},{8,9},{9,8},{10,11... | collective-permute-start | bytes 786440 | tf_op jit(solution)/shard_map/ppermute | solution.py:267
  50.5 0.0 collective-permute-done.9.refs_6_
  50.5 0.3 shard_map.83
  50.8 1.9 %collective-permute-start.10 = (f32[2,8,32,128]{3,2,1,0:T(8,128)S(1)}, f32[2,8,32,128]{3,2,1,0:T(8,128)S(1)}, u32[]{:S(2)}, u32[]{:S(2)}) collective-permute-start(f32[2,8,32,128]{3,2,1,0:T(8,128)S(1)} %get-tuple-element.54), channel_id=1, source_target_pairs={{0,3},{1,2},{2,1},{3,0},{4,7},{5,6},{6,5},{7,4},{8,11},{9,10},{10,... | collective-permute-start | bytes 786440 | tf_op jit(solution)/shard_map/ppermute | solution.py:267
  52.7 1.0 %collective-permute-start.11 = (f32[2,8,32,128]{3,2,1,0:T(8,128)S(1)}, f32[2,8,32,128]{3,2,1,0:T(8,128)S(1)}, u32[]{:S(2)}, u32[]{:S(2)}) collective-permute-start(f32[2,8,32,128]{3,2,1,0:T(8,128)S(1)} %get-tuple-element.55), channel_id=1, source_target_pairs={{0,2},{1,3},{2,0},{3,1},{4,6},{5,7},{6,4},{7,5},{8,10},{9,11},{10,... | collective-permute-start | bytes 786440 | tf_op jit(solution)/shard_map/ppermute | solution.py:267
  53.8 0.0 collective-permute-done.15.refs_5_
  53.8 0.6 collective-permute-start.12
  54.4 3.7 %collective-permute-done.16.refs_6_ = f32[2,8,32,128]{3,2,1,0:T(8,128)S(1)} collective-permute-done((f32[2,8,32,128]{3,2,1,0:T(8,128)S(1)}, f32[2,8,32,128]{3,2,1,0:T(8,128)S(1)}, u32[]{:S(2)}, u32[]{:S(2)}) %collective-permute-start.16) | collective-permute-done | bytes 262176 | tf_op jit(solution)/shard_map/ppermute | solution.py:267
  58.0 4.4 %collective-permute-done.17.refs_7_ = f32[2,8,32,128]{3,2,1,0:T(8,128)S(1)} collective-permute-done((f32[2,8,32,128]{3,2,1,0:T(8,128)S(1)}, f32[2,8,32,128]{3,2,1,0:T(8,128)S(1)}, u32[]{:S(2)}, u32[]{:S(2)}) %collective-permute-start.17) | collective-permute-done | bytes 262176 | tf_op jit(solution)/shard_map/ppermute | solution.py:267
  62.4 2.0 %shard_map.85 = (bf16[192,2048]{1,0:T(8,128)(2,1)}, bf16[192,2048]{1,0:T(8,128)(2,1)}, bf16[192,2048]{1,0:T(8,128)(2,1)}, bf16[192,2048]{1,0:T(8,128)(2,1)}) custom-call(s32[1]{0:T(128)} %bitcast.info, bf16[192,2048]{1,0:T(8,128)(2,1)S(1)} %copy-done, bf16[192,2048]{1,0:T(8,128)(2,1)S(1)} %copy-done.1, bf16[192,2048]{1,0:T(8,128)(2,1)S(1)} %copy-done.2, ...), custom_call_target="tpu_custom_call" | custom-call | tf_op jit(solution)/shard_map/pallas_call | solution.py:254
  64.3 0.4 collective-permute-done.10.refs_5_
  64.7 4.2 %collective-permute-done.11.refs_6_ = f32[2,8,32,128]{3,2,1,0:T(8,128)S(1)} collective-permute-done((f32[2,8,32,128]{3,2,1,0:T(8,128)S(1)}, f32[2,8,32,128]{3,2,1,0:T(8,128)S(1)}, u32[]{:S(2)}, u32[]{:S(2)}) %collective-permute-start.11) | collective-permute-done | bytes 262176 | tf_op jit(solution)/shard_map/ppermute | solution.py:267
  68.9 0.0 collective-permute-done.12.refs_7_
  68.9 1.9 %shard_map.86 = (bf16[192,2048]{1,0:T(8,128)(2,1)}, bf16[192,2048]{1,0:T(8,128)(2,1)}, bf16[192,2048]{1,0:T(8,128)(2,1)}, bf16[192,2048]{1,0:T(8,128)(2,1)}) custom-call(s32[1]{0:T(128)} %bitcast.info, bf16[192,2048]{1,0:T(8,128)(2,1)S(1)} %copy-done, ...), custom_call_target="tpu_custom_call", output_to_operand_aliasing={{0}: (13, {}), {1}: (14, {}), {2}: (15, {}), {3}: (16, {})} | custom-call | tf_op jit(solution)/shard_map/pallas_call | solution.py:254
  (2 shorter events, 0.1 us)
Async XLA Ops:
  3.5 11.4 %collective-permute-start = (f32[2,8,32,128]{3,2,1,0:T(8,128)}, f32[2,8,32,128]{3,2,1,0:T(8,128)S(1)}, u32[]{:S(2)}, u32[]{:S(2)}) collective-permute-start(f32[2,8,32,128]{3,2,1,0:T(8,128)} %get-tuple-element.37), channel_id=1, source_target_pairs={{0,3},{1,2},{2,1},{3,0},{4,7},{5,6},{6,5},{7,4},{8,11},{9,10},{10,... | collective-permute-start | bytes 786440 | tf_op jit(solution)/shard_map/ppermute | solution.py:267
  7.5 14.0 %collective-permute-start.1 = (f32[2,8,32,128]{3,2,1,0:T(8,128)}, f32[2,8,32,128]{3,2,1,0:T(8,128)S(1)}, u32[]{:S(2)}, u32[]{:S(2)}) collective-permute-start(f32[2,8,32,128]{3,2,1,0:T(8,128)} %get-tuple-element.38), channel_id=1, source_target_pairs={{0,2},{1,3},{2,0},{3,1},{4,6},{5,7},{6,4},{7,5},{8,10},{9,11},{10,... | collective-permute-start | bytes 786440 | tf_op jit(solution)/shard_map/ppermute | solution.py:267
  8.0 13.6 %collective-permute-start.2 = (f32[2,8,32,128]{3,2,1,0:T(8,128)}, f32[2,8,32,128]{3,2,1,0:T(8,128)S(1)}, u32[]{:S(2)}, u32[]{:S(2)}) collective-permute-start(f32[2,8,32,128]{3,2,1,0:T(8,128)} %get-tuple-element.39), channel_id=1, source_target_pairs={{0,1},{1,0},{2,3},{3,2},{4,5},{5,4},{6,7},{7,6},{8,9},{9,8},{10,11... | collective-permute-start | bytes 786440 | tf_op jit(solution)/shard_map/ppermute | solution.py:267
  8.2 9.7 %copy-start = (bf16[192,2048]{1,0:T(8,128)(2,1)S(1)}, bf16[192,2048]{1,0:T(8,128)(2,1)}, u32[]{:S(2)}) copy-start(bf16[192,2048]{1,0:T(8,128)(2,1)} %q.11) | copy-start | bytes 2359300
  8.2 9.7 %copy-start.1 = (bf16[192,2048]{1,0:T(8,128)(2,1)S(1)}, bf16[192,2048]{1,0:T(8,128)(2,1)}, u32[]{:S(2)}) copy-start(bf16[192,2048]{1,0:T(8,128)(2,1)} %k.11) | copy-start | bytes 2359300
  8.2 9.7 %copy-start.2 = (bf16[192,2048]{1,0:T(8,128)(2,1)S(1)}, bf16[192,2048]{1,0:T(8,128)(2,1)}, u32[]{:S(2)}) copy-start(bf16[192,2048]{1,0:T(8,128)(2,1)} %v.11) | copy-start | bytes 2359300
  8.2 9.7 %copy-start.3 = (bf16[192,2048]{1,0:T(8,128)(2,1)S(1)}, bf16[192,2048]{1,0:T(8,128)(2,1)}, u32[]{:S(2)}) copy-start(bf16[192,2048]{1,0:T(8,128)(2,1)} %g.11) | copy-start | bytes 2359300
  11.2 17.3 %collective-permute-start.4 = (f32[2,8,32,128]{3,2,1,0:T(8,128)}, f32[2,8,32,128]{3,2,1,0:T(8,128)S(1)}, u32[]{:S(2)}, u32[]{:S(2)}) collective-permute-start(f32[2,8,32,128]{3,2,1,0:T(8,128)} %get-tuple-element.48), channel_id=1, source_target_pairs={{0,1},{1,0},{2,3},{3,2},{4,5},{5,4},{6,7},{7,6},{8,9},{9,8},{10,11... | collective-permute-start | bytes 786440 | tf_op jit(solution)/shard_map/ppermute | solution.py:267
  13.1 15.4 %collective-permute-start.5 = (f32[2,8,32,128]{3,2,1,0:T(8,128)}, f32[2,8,32,128]{3,2,1,0:T(8,128)S(1)}, u32[]{:S(2)}, u32[]{:S(2)}) collective-permute-start(f32[2,8,32,128]{3,2,1,0:T(8,128)} %get-tuple-element.49), channel_id=1, source_target_pairs={{0,2},{1,3},{2,0},{3,1},{4,6},{5,7},{6,4},{7,5},{8,10},{9,11},{10,... | collective-permute-start | bytes 786440 | tf_op jit(solution)/shard_map/ppermute | solution.py:267
  14.9 20.2 %collective-permute-start.6 = (f32[2,8,32,128]{3,2,1,0:T(8,128)}, f32[2,8,32,128]{3,2,1,0:T(8,128)S(1)}, u32[]{:S(2)}, u32[]{:S(2)}) collective-permute-start(f32[2,8,32,128]{3,2,1,0:T(8,128)} %get-tuple-element.50), channel_id=1, source_target_pairs={{0,3},{1,2},{2,1},{3,0},{4,7},{5,6},{6,5},{7,4},{8,11},{9,10},{10,... | collective-permute-start | bytes 786440 | tf_op jit(solution)/shard_map/ppermute | solution.py:267
  17.9 1.0 %copy-start.5 = (f32[2,8,32,128]{3,2,1,0:T(8,128)S(1)}, f32[2,8,32,128]{3,2,1,0:T(8,128)}, u32[]{:S(2)}) copy-start(f32[2,8,32,128]{3,2,1,0:T(8,128)} %get-tuple-element.40.refs_0_.a) | copy-start | bytes 786436
  18.8 2.8 %copy-start.4 = (f32[2,8,32,128]{3,2,1,0:T(8,128)S(1)}, f32[2,8,32,128]{3,2,1,0:T(8,128)}, u32[]{:S(2)}) copy-start(f32[2,8,32,128]{3,2,1,0:T(8,128)} %get-tuple-element.36.refs_0_.a) | copy-start | bytes 786436
  21.7 1.4 %collective-permute-start.3 = (f32[8,32,128]{2,1,0:T(8,128)S(1)}, f32[8,32,128]{2,1,0:T(8,128)S(1)}, u32[]{:S(2)}, u32[]{:S(2)}) collective-permute-start(f32[8,32,128]{2,1,0:T(8,128)S(1)} %get-tuple-element.43), channel_id=1, source_target_pairs={{0,8},{8,0},{1,9},{9,1},{2,10},{10,2},{3,11},{11,3},{4,12},{12,4},... | collective-permute-start | bytes 393224 | tf_op jit(solution)/shard_map/ppermute | solution.py:295
  23.1 12.2 %collective-permute-start.13 = (f32[3,4,32,128]{3,2,1,0:T(8,128)S(1)}, f32[3,4,32,128]{3,2,1,0:T(8,128)S(1)}, u32[]{:S(2)}, u32[]{:S(2)}) collective-permute-start(f32[3,4,32,128]{3,2,1,0:T(8,128)S(1)} %shard_map.79.refs_0_), channel_id=1, source_target_pairs={{0,4},{1,5},{2,6},{3,7},{4,0},{5,1},{6,2},{7,3},{8,12},{9,13},{10,... | collective-permute-start | bytes 589832 | tf_op jit(solution)/shard_map/ppermute | solution.py:267
  35.2 1.4 %collective-permute-start.7 = (f32[8,32,128]{2,1,0:T(8,128)S(1)}, f32[8,32,128]{2,1,0:T(8,128)S(1)}, u32[]{:S(2)}, u32[]{:S(2)}) collective-permute-start(f32[8,32,128]{2,1,0:T(8,128)S(1)} %get-tuple-element.51), channel_id=1, source_target_pairs={{0,8},{8,0},{1,9},{9,1},{2,10},{10,2},{3,11},{11,3},{4,12},{12,4},... | collective-permute-start | bytes 393224 | tf_op jit(solution)/shard_map/ppermute | solution.py:295
  35.3 3.4 %collective-permute-start.14 = (f32[3,4,32,128]{3,2,1,0:T(8,128)S(1)}, f32[3,4,32,128]{3,2,1,0:T(8,128)S(1)}, u32[]{:S(2)}, u32[]{:S(2)}) collective-permute-start(f32[3,4,32,128]{3,2,1,0:T(8,128)S(1)} %collective-permute-done.13.refs_5_), channel_id=1, source_target_pairs={{0,8},{8,0},{1,9},{9,1},{2,10},{10,2},{3,11},{11,3},{4,12},{12,4},... | collective-permute-start | bytes 589832 | tf_op jit(solution)/shard_map/ppermute | solution.py:302
  36.7 12.2 %collective-permute-start.8 = (f32[3,4,32,128]{3,2,1,0:T(8,128)S(1)}, f32[3,4,32,128]{3,2,1,0:T(8,128)S(1)}, u32[]{:S(2)}, u32[]{:S(2)}) collective-permute-start(f32[3,4,32,128]{3,2,1,0:T(8,128)S(1)} %shard_map.82), channel_id=1, source_target_pairs={{0,4},{1,5},{2,6},{3,7},{4,0},{5,1},{6,2},{7,3},{8,12},{9,13},{10,... | collective-permute-start | bytes 589832 | tf_op jit(solution)/shard_map/ppermute | solution.py:267
  39.0 14.8 %collective-permute-start.15 = (f32[2,8,32,128]{3,2,1,0:T(8,128)S(1)}, f32[2,8,32,128]{3,2,1,0:T(8,128)S(1)}, u32[]{:S(2)}, u32[]{:S(2)}) collective-permute-start(f32[2,8,32,128]{3,2,1,0:T(8,128)S(1)} %get-tuple-element.61), channel_id=1, source_target_pairs={{0,3},{1,2},{2,1},{3,0},{4,7},{5,6},{6,5},{7,4},{8,11},{9,10},{10,... | collective-permute-start | bytes 786440 | tf_op jit(solution)/shard_map/ppermute | solution.py:267
  48.9 1.6 %collective-permute-start.9 = (f32[3,4,32,128]{3,2,1,0:T(8,128)S(1)}, f32[3,4,32,128]{3,2,1,0:T(8,128)S(1)}, u32[]{:S(2)}, u32[]{:S(2)}) collective-permute-start(f32[3,4,32,128]{3,2,1,0:T(8,128)S(1)} %collective-permute-done.8.refs_5_), channel_id=1, source_target_pairs={{0,8},{8,0},{1,9},{9,1},{2,10},{10,2},{3,11},{11,3},{4,12},{12,4},... | collective-permute-start | bytes 589832 | tf_op jit(solution)/shard_map/ppermute | solution.py:302
  48.9 9.1 %collective-permute-start.16 = (f32[2,8,32,128]{3,2,1,0:T(8,128)S(1)}, f32[2,8,32,128]{3,2,1,0:T(8,128)S(1)}, u32[]{:S(2)}, u32[]{:S(2)}) collective-permute-start(f32[2,8,32,128]{3,2,1,0:T(8,128)S(1)} %get-tuple-element.62), channel_id=1, source_target_pairs={{0,2},{1,3},{2,0},{3,1},{4,6},{5,7},{6,4},{7,5},{8,10},{9,11},{10,... | collective-permute-start | bytes 786440 | tf_op jit(solution)/shard_map/ppermute | solution.py:267
  48.9 13.5 %collective-permute-start.17 = (f32[2,8,32,128]{3,2,1,0:T(8,128)S(1)}, f32[2,8,32,128]{3,2,1,0:T(8,128)S(1)}, u32[]{:S(2)}, u32[]{:S(2)}) collective-permute-start(f32[2,8,32,128]{3,2,1,0:T(8,128)S(1)} %get-tuple-element.63), channel_id=1, source_target_pairs={{0,1},{1,0},{2,3},{3,2},{4,5},{5,4},{6,7},{7,6},{8,9},{9,8},{10,11... | collective-permute-start | bytes 786440 | tf_op jit(solution)/shard_map/ppermute | solution.py:267
  50.8 13.9 %collective-permute-start.10 = (f32[2,8,32,128]{3,2,1,0:T(8,128)S(1)}, f32[2,8,32,128]{3,2,1,0:T(8,128)S(1)}, u32[]{:S(2)}, u32[]{:S(2)}) collective-permute-start(f32[2,8,32,128]{3,2,1,0:T(8,128)S(1)} %get-tuple-element.54), channel_id=1, source_target_pairs={{0,3},{1,2},{2,1},{3,0},{4,7},{5,6},{6,5},{7,4},{8,11},{9,10},{10,... | collective-permute-start | bytes 786440 | tf_op jit(solution)/shard_map/ppermute | solution.py:267
  52.7 16.2 %collective-permute-start.11 = (f32[2,8,32,128]{3,2,1,0:T(8,128)S(1)}, f32[2,8,32,128]{3,2,1,0:T(8,128)S(1)}, u32[]{:S(2)}, u32[]{:S(2)}) collective-permute-start(f32[2,8,32,128]{3,2,1,0:T(8,128)S(1)} %get-tuple-element.55), channel_id=1, source_target_pairs={{0,2},{1,3},{2,0},{3,1},{4,6},{5,7},{6,4},{7,5},{8,10},{9,11},{10,... | collective-permute-start | bytes 786440 | tf_op jit(solution)/shard_map/ppermute | solution.py:267
  53.8 15.2 %collective-permute-start.12 = (f32[2,8,32,128]{3,2,1,0:T(8,128)S(1)}, f32[2,8,32,128]{3,2,1,0:T(8,128)S(1)}, u32[]{:S(2)}, u32[]{:S(2)}) collective-permute-start(f32[2,8,32,128]{3,2,1,0:T(8,128)S(1)} %get-tuple-element.56), channel_id=1, source_target_pairs={{0,1},{1,0},{2,3},{3,2},{4,5},{5,4},{6,7},{7,6},{8,9},{9,8},{10,11... | collective-permute-start | bytes 786440 | tf_op jit(solution)/shard_map/ppermute | solution.py:267
